TPU v7x, 512 devices: a whole 4x8x8 slice. The times are simulated.
512 devices in a mesh: pipe: 4 (over y_hi), tensor: 32 (over x, z), dp: 4 (over y_lo, core).
Axes of the slice: x: 4, y: 8 (y_hi: 4, y_lo: 2; y = y_hi * 2 + y_lo), z: 8, core: 2. Of those that a mesh axis runs over, the one named last changes fastest.
Arguments:
- section_input: bfloat16 [4, 1, 4, 128, 6144], P('pipe', None, 'dp', 'tensor'), may hold values from -6 to 6
- pre_act: bfloat16 [4, 1, 4, 128, 8192], P('pipe', None, 'dp', None, 'tensor'), may hold values from -8 to 8
- cotangent: bfloat16 [1, 4, 128, 6144], P(None, 'dp', 'tensor'), may hold values from -6 to 6
- w_up: bfloat16 [4, 6144, 8192], P('pipe', 'dp', 'tensor'), may hold values from -0.078125 to 0.078125
- w_down: bfloat16 [4, 8192, 6144], P('pipe', 'tensor', 'dp'), may hold values from -0.0625 to 0.0625
Outputs:
- input_grad: bfloat16 [4, 1, 4, 128, 6144], P('pipe', None, 'dp', 'tensor')
- up_grad: bfloat16 [4, 6144, 8192], P('pipe', 'dp', 'tensor')
- down_grad: bfloat16 [4, 8192, 6144], P('pipe', 'tensor', 'dp')
All inputs are finite; a program needn't handle non-finite values.
Results may differ from a plain program's by a relative error of at most 0.034.
Values may be sent and summed in bfloat16 or wider, within the bound.
No kernel may reach another device: no remote copies, remote signals or barrier semaphores. Data moves between devices by JAX's collectives and lax.ppermute only.
A program may use at most 64 MiB of HBM per device.

v0:
```python
import jax
import jax.numpy as jnp
from jax import lax
from jax.sharding import PartitionSpec as P

epsilon = 1e-06


def passed_along(value, axis, steps):
    count = lax.axis_size(axis)
    initial, last = (max(0, -steps), min(count, count - steps))
    return lax.ppermute(value, axis, [(source, source + steps) for source in range(initial, last)])


def regroup(values, groups, parts):
    lead = values.shape[:-2]
    width = values.shape[-1]
    shaped = values.reshape(lead + (groups, parts, -1, width))
    swapped = jnp.swapaxes(shaped, -4, -3)
    return swapped.reshape(lead + (-1, width))


def per_device(section_input, pre_act, cotangent, w_up, w_down):
    pipe_count = lax.axis_size("pipe")
    pipe_index = lax.axis_index("pipe")
    part_count = lax.axis_size("tensor")
    group_count = lax.axis_size("dp")
    micro_count = section_input.shape[1]
    inputs = section_input[0, :, 0].astype(jnp.float32)
    preact_all = pre_act[0, :, 0]
    own_grads = cotangent[:, 0]
    inverse = lax.rsqrt(jnp.mean(inputs * inputs, axis=-1, keepdims=True) + epsilon)
    normed = (inputs * inverse).astype(jnp.bfloat16)
    down_full = lax.all_gather(w_down[0], "dp", axis=1, tiled=True)
    up_full = lax.all_gather(w_up[0], "dp", axis=0, tiled=True)
    carry = jnp.zeros(own_grads.shape[1:], jnp.bfloat16)
    input_store = jnp.zeros(own_grads.shape, jnp.bfloat16)
    grad_store = jnp.zeros((micro_count, preact_all.shape[1], own_grads.shape[2]), jnp.bfloat16)
    pre_store = jnp.zeros(preact_all.shape, jnp.bfloat16)
    for clock_tick in range(micro_count + pipe_count - 1):
        micro_index = clock_tick - (pipe_count - 1 - pipe_index)
        is_valid = jnp.logical_and(micro_index >= 0, micro_index < micro_count)
        safe_index = jnp.clip(micro_index, 0, micro_count - 1)
        own_piece = lax.dynamic_index_in_dim(own_grads, safe_index, 0, keepdims=False)
        grad_in = jnp.where(pipe_index == pipe_count - 1, own_piece, carry)
        grad_rows = lax.all_gather(grad_in, "tensor", axis=0, tiled=True)
        hidden_grad = lax.dot_general(
            grad_rows, down_full, (((1,), (1,)), ((), ())), preferred_element_type=jnp.float32
        )
        preact = lax.dynamic_index_in_dim(preact_all, safe_index, 0, keepdims=False).astype(
            jnp.float32
        )
        sigmoid_u = jax.nn.sigmoid(preact)
        slope = sigmoid_u * (1.0 + preact * (1.0 - sigmoid_u))
        pre_grad = (hidden_grad * slope).astype(jnp.bfloat16)
        normed_grad = lax.psum_scatter(
            lax.dot_general(
                pre_grad, up_full, (((1,), (1,)), ((), ())), preferred_element_type=jnp.float32
            ).astype(jnp.bfloat16),
            "tensor",
            scatter_dimension=0,
            tiled=True,
        ).astype(jnp.float32)
        own_input = lax.dynamic_index_in_dim(inputs, safe_index, 0, keepdims=False)
        own_inverse = lax.dynamic_index_in_dim(inverse, safe_index, 0, keepdims=False)
        mean_term = jnp.mean(normed_grad * own_input, axis=-1, keepdims=True)
        grad_f = (
            grad_in.astype(jnp.float32)
            + own_inverse * normed_grad
            - own_input * own_inverse**3 * mean_term
        )
        outgoing = grad_f.astype(jnp.bfloat16)
        old_input = lax.dynamic_index_in_dim(input_store, safe_index, 0, keepdims=False)
        input_store = lax.dynamic_update_index_in_dim(
            input_store, jnp.where(is_valid, outgoing, old_input), safe_index, 0
        )
        old_rows = lax.dynamic_index_in_dim(grad_store, safe_index, 0, keepdims=False)
        grad_store = lax.dynamic_update_index_in_dim(
            grad_store, jnp.where(is_valid, grad_rows, old_rows), safe_index, 0
        )
        old_pre = lax.dynamic_index_in_dim(pre_store, safe_index, 0, keepdims=False)
        pre_store = lax.dynamic_update_index_in_dim(
            pre_store, jnp.where(is_valid, pre_grad, old_pre), safe_index, 0
        )
        carry = passed_along(outgoing, "pipe", -1)
    preact_f = preact_all.astype(jnp.float32)
    hidden = (preact_f * jax.nn.sigmoid(preact_f)).astype(jnp.bfloat16)
    grad_blocks, normed_blocks = (
        lax.all_to_all(grad_store, "dp", split_axis=2, concat_axis=1, tiled=True),
        lax.all_to_all(normed, "dp", split_axis=2, concat_axis=1, tiled=True),
    )
    normed_all = lax.all_gather(normed_blocks, "tensor", axis=1, tiled=True)
    hidden_all, pre_groups_all = (
        lax.all_gather(hidden, "dp", axis=1, tiled=True),
        lax.all_gather(pre_store, "dp", axis=1, tiled=True),
    )
    pre_all = regroup(pre_groups_all, group_count, part_count)
    down_grad = jnp.einsum(
        "mkf,mkd->fd", hidden_all, grad_blocks, preferred_element_type=jnp.float32
    ).astype(jnp.bfloat16)
    up_grad = jnp.einsum(
        "mkd,mkf->df", normed_all, pre_all, preferred_element_type=jnp.float32
    ).astype(jnp.bfloat16)
    input_grad = input_store.reshape((1, micro_count, 1) + input_store.shape[1:])
    return (input_grad, up_grad[None], down_grad[None])


def solution(mesh):
    return jax.shard_map(
        per_device,
        mesh=mesh,
        in_specs=(
            P("pipe", None, "dp", "tensor", None),
            P("pipe", None, "dp", None, "tensor"),
            P(None, "dp", "tensor", None),
            P("pipe", "dp", "tensor"),
            P("pipe", "tensor", "dp"),
        ),
        out_specs=(
            P("pipe", None, "dp", "tensor", None),
            P("pipe", "dp", "tensor"),
            P("pipe", "tensor", "dp"),
        ),
        check_vma=False,
    )
```

profile of v0, /device:TPU:1, one launch (start us, length us, event | category | flops | bytes accessed | tf_op | source)
XLA Modules:
  0.0 1229.4 jit_solution(6780579457570471744)
XLA Ops:
  7.2 1.4 fusion.84
  8.7 0.7 all-gather.17.cloned.1.call-update
  9.5 0.7 all-gather.19.cloned.1.call-update
  10.2 86.6 %all-gather.21.cloned.1.call-done = bf16[32,4,6144]{2,1,0:T(4,128)(2,1)} async-done(((bf16[1,4,6144]{2,1,0:T(4,128)(2,1)}), bf16[32,4,6144]{2,1,0:T(4,128)(2,1)}) %all-gather.21.cloned.1.call-update) | async-done | bytes 1572880 | tf_op jit(solution)/shard_map/all_gather | solution.py:46
  96.8 2.7 reshape.249
  99.5 43.7 %all-gather.17.cloned.1.call-done = bf16[1,256,6144]{2,1,0:T(8,128)(2,1)} async-done(((bf16[1,256,1536]{2,1,0:T(8,128)(2,1)}), bf16[1,256,6144]{2,1,0:T(8,128)(2,1)}) %all-gather.17.cloned.1.call-update) | async-done | bytes 3145744 | tf_op jit(solution)/shard_map/all_gather | solution.py:34
  143.2 3.1 fusion.36
  146.3 42.5 %all-gather.19.cloned.1.call-done = bf16[1,6144,256]{2,1,0:T(8,128)(2,1)} async-done(((bf16[1,1536,256]{2,1,0:T(8,128)(2,1)}), bf16[1,6144,256]{2,1,0:T(8,128)(2,1)}) %all-gather.19.cloned.1.call-update) | async-done | bytes 3145744 | tf_op jit(solution)/shard_map/all_gather | solution.py:35
  188.8 4.2 convolution_convert_fusion.3
  193.1 1.3 dynamic-slice.9
  195.2 156.9 %all-reduce.9.cloned.1.call-done = bf16[128,6144]{1,0:T(8,128)(2,1)} async-done(((bf16[128,6144]{1,0:T(8,128)(2,1)}), bf16[128,6144]{1,0:T(8,128)(2,1)}) %all-reduce.9.cloned.1.call-update) | async-done | bytes 1572880
  352.1 1.1 fusion.78
  353.2 1.0 fusion.66
  354.8 1.3 collective-permute-start
  356.1 4.4 collective-permute-done
  360.6 0.6 fusion.85
  361.3 82.2 %all-gather.23.cloned.1.call-done = bf16[32,4,6144]{2,1,0:T(4,128)(2,1)} async-done(((bf16[1,4,6144]{2,1,0:T(4,128)(2,1)}), bf16[32,4,6144]{2,1,0:T(4,128)(2,1)}) %all-gather.23.cloned.1.call-update) | async-done | bytes 1572880 | tf_op jit(solution)/shard_map/all_gather | solution.py:46
  443.4 3.6 reshape.251
  447.1 3.7 fusion.33
  450.8 2.4 convolution_convert_fusion.2
  453.2 159.8 %all-reduce.11.cloned.1.call-done = bf16[128,6144]{1,0:T(8,128)(2,1)} async-done(((bf16[128,6144]{1,0:T(8,128)(2,1)}), bf16[128,6144]{1,0:T(8,128)(2,1)}) %all-reduce.11.cloned.1.call-update) | async-done | bytes 1572880
  613.0 1.1 fusion.79
  614.1 1.0 fusion.69
  615.7 1.3 collective-permute-start.1
  617.0 4.4 collective-permute-done.1
  621.4 0.6 fusion.86
  622.2 82.2 %all-gather.25.cloned.1.call-done = bf16[32,4,6144]{2,1,0:T(4,128)(2,1)} async-done(((bf16[1,4,6144]{2,1,0:T(4,128)(2,1)}), bf16[32,4,6144]{2,1,0:T(4,128)(2,1)}) %all-gather.25.cloned.1.call-update) | async-done | bytes 1572880 | tf_op jit(solution)/shard_map/all_gather | solution.py:46
  704.3 3.7 reshape.253
  708.0 3.5 fusion.30
  711.5 2.4 convolution_convert_fusion.1
  714.0 159.8 %all-reduce.13.cloned.1.call-done = bf16[128,6144]{1,0:T(8,128)(2,1)} async-done(((bf16[128,6144]{1,0:T(8,128)(2,1)}), bf16[128,6144]{1,0:T(8,128)(2,1)}) %all-reduce.13.cloned.1.call-update) | async-done | bytes 1572880
  873.8 1.1 fusion.80
  874.8 1.0 fusion.72
  875.9 1.3 collective-permute-start.2
  877.2 4.4 collective-permute-done.2
  883.1 0.8 fusion.77
  883.9 5.2 copy.25
  889.6 35.5 %reduce.1 = bf16[6144,4]{1,0:T(8,128)(2,1)} reduce(bf16[6144,1,4]{2,1,0:T(2,128)(2,1)} %bitcast.194, bf16[]{:T(256)} %broadcast.164), dimensions={1}, to_apply=%bitcast.177.reduce_sub_computation | reduce | bytes 98306
  925.2 3.9 reshape.260
  929.1 11.9 all_to_all.33
  941.0 5.5 reshape.261
  946.4 7.0 copy.26
  953.4 0.8 all_to_all.25
  954.9 1.4 all_to_all.27
  956.6 8.0 all-gather.27.cloned.1.call-done
  964.7 3.6 reshape.255
  968.3 4.2 select_select_fusion
  972.5 2.3 convolution_convert_fusion
  974.8 1.4 copy-done.2
  976.2 2.9 select_bitcast_fusion
  979.1 6.8 copy.29
  985.9 34.4 %reduce.2 = bf16[6144,128]{1,0:T(8,128)(2,1)} reduce(bf16[6144,1,128]{2,1,0:T(2,128)(2,1)S(1)} %bitcast.195, bf16[]{:T(256)} %broadcast.164), dimensions={1}, to_apply=%bitcast.179.reduce_sub_computation | reduce | bytes 3145730
  1020.3 3.7 reshape.262
  1024.1 9.5 all-to-all-start.1
  1033.6 22.1 %all_gather.35 = bf16[1,512,256]{2,1,0:T(8,128)(2,1)S(1)} all-gather(bf16[1,128,256]{2,1,0:T(8,128)(2,1)S(1)} %fusion.47), channel_id=1, replica_groups=mesh['pipe'=4,'tensor'=32,'dp'=4] {'dp'}, dimensions={1}, use_global_device_ids=true | all-gather | bytes 327680 | tf_op jit(solution)/shard_map/all_gather | solution.py:94
  1055.8 5.8 all-gather.2
  1061.9 2.9 fusion.12
  1064.9 147.6 %all-reduce.15.cloned.1.call-done = bf16[128,6144]{1,0:T(8,128)(2,1)} async-done(((bf16[128,6144]{1,0:T(8,128)(2,1)}), bf16[128,6144]{1,0:T(8,128)(2,1)}) %all-reduce.15.cloned.1.call-update) | async-done | bytes 1572880
  1212.4 1.1 fusion.81
  1213.6 1.7 fusion.83
  1215.2 3.1 reshape.263
  1218.3 1.4 copy.31
  1219.7 1.7 copy.30
  1221.4 1.5 fusion.13
  (72 shorter events, 5.3 us)
Async XLA Ops:
  7.2 89.6 %all-gather.21.cloned.1.call-start = ((), (), s32[]{:S(2)}) async-start(), calls=%async_computation.5 | async-start | bytes 1622016 | tf_op jit(solution)/shard_map/all_gather | solution.py:46
  8.7 134.5 %all-gather.17.cloned.1.call-start = ((), (), s32[]{:S(2)}) async-start(), calls=%async_computation.3 | async-start | bytes 3932160 | tf_op jit(solution)/shard_map/all_gather | solution.py:34
  9.4 179.4 %all-gather.19.cloned.1.call-start = ((), (), s32[]{:S(2)}) async-start(), calls=%async_computation.4 | async-start | bytes 3932160 | tf_op jit(solution)/shard_map/all_gather | solution.py:35
  10.2 133.0 %copy-start.5 = (bf16[1,1,1,128,256]{4,3,2,1,0:T(8,128)(2,1)S(1)}, bf16[1,1,1,128,256]{4,3,2,1,0:T(8,128)(2,1)}, u32[]{:S(2)}) copy-start(bf16[1,1,1,128,256]{4,3,2,1,0:T(8,128)(2,1)} %param.6) | copy-start | bytes 196612
  10.2 341.9 %all-reduce.9.cloned.1.call-start = ((), (), s32[]{:S(2)}) async-start(), calls=%async_computation.9 | async-start | bytes 3145728
  99.5 46.8 %copy-start.1 = (bf16[128,6144]{1,0:T(8,128)(2,1)}, bf16[128,6144]{1,0:T(8,128)(2,1)S(1)}, u32[]{:S(2)}) copy-start(bf16[128,6144]{1,0:T(8,128)(2,1)S(1)} %reshape.249) | copy-start | bytes 4718596
  193.0 2.0 copy-start.3
  193.0 160.2 %copy-start.4 = (bf16[1,1,4,6144]{3,2,1,0:T(4,128)(2,1)S(1)}, bf16[1,1,4,6144]{3,2,1,0:T(4,128)(2,1)}, u32[]{:S(2)}) copy-start(bf16[1,1,4,6144]{3,2,1,0:T(4,128)(2,1)} %param.7) | copy-start | bytes 147460
  193.0 250.4 %all-gather.23.cloned.1.call-start = ((), (), s32[]{:S(2)}) async-start(), calls=%async_computation.6 | async-start | bytes 1622016 | tf_op jit(solution)/shard_map/all_gather | solution.py:46
  195.2 418.9 %copy-start.15 = (f32[4]{0:T(128)}, f32[4]{0:T(128)S(1)}, u32[]{:S(2)}) copy-start(f32[4]{0:T(128)S(1)} %get-tuple-element.3) | copy-start | bytes 52
  195.2 418.9 %copy-start.17 = (f32[4]{0:T(128)}, f32[4]{0:T(128)S(1)}, u32[]{:S(2)}) copy-start(f32[4]{0:T(128)S(1)} %get-tuple-element.4) | copy-start | bytes 52
  354.2 0.6 copy-start.6
  354.8 5.7 collective-permute-start
  361.2 251.8 %all-reduce.11.cloned.1.call-start = ((), (), s32[]{:S(2)}) async-start(), calls=%async_computation.10 | async-start | bytes 3145728
  447.1 3.7 copy-start
  453.2 251.2 %all-gather.25.cloned.1.call-start = ((), (), s32[]{:S(2)}) async-start(), calls=%async_computation.7 | async-start | bytes 1622016 | tf_op jit(solution)/shard_map/all_gather | solution.py:46
  615.1 0.6 copy-start.10
  615.7 5.7 collective-permute-start.1
  622.1 251.7 %all-reduce.13.cloned.1.call-start = ((), (), s32[]{:S(2)}) async-start(), calls=%async_computation.11 | async-start | bytes 3145728
  713.9 250.7 %all-gather.27.cloned.1.call-start = ((), (), s32[]{:S(2)}) async-start(), calls=%async_computation.8 | async-start | bytes 1622016 | tf_op jit(solution)/shard_map/all_gather | solution.py:46
  875.9 5.7 copy-start.12
  875.9 5.7 collective-permute-start.2
  881.6 0.6 copy-start.8
  882.9 179.0 %all-gather.15.cloned.1.call-start = ((), (), s32[]{:S(2)}) async-start(), calls=%async_computation.2 | async-start | bytes 1622016 | tf_op jit(solution)/shard_map/all_gather | solution.py:92
  956.4 256.1 %all-reduce.15.cloned.1.call-start = ((), (), s32[]{:S(2)}) async-start(), calls=%async_computation.12 | async-start | bytes 3145728
  974.8 1.4 copy-start.2
  1024.1 31.7 %copy-start.14 = (bf16[128,256]{1,0:T(8,128)(2,1)S(1)}, bf16[128,256]{1,0:T(8,128)(2,1)}, u32[]{:S(2)}) copy-start(bf16[128,256]{1,0:T(8,128)(2,1)} %get-tuple-element.5) | copy-start | bytes 196612
  1024.1 191.2 %all-to-all-start.1 = ((bf16[4,2,98304]{2,1,0:T(2,128)(2,1)}), bf16[4,2,98304]{2,1,0:T(2,128)(2,1)}, u32[]{:S(2)}, u32[]{:S(2)}) async-start(bf16[4,2,98304]{2,1,0:T(2,128)(2,1)} %reshape.262), calls=%async_computation.1 | async-start | bytes 3145728 | tf_op jit(solution)/shard_map/all_to_all | solution.py:89
  1061.8 151.7 %copy-start.7 = (bf16[4,6144]{1,0:T(4,128)(2,1)S(1)}, bf16[4,6144]{1,0:T(4,128)(2,1)}, u32[]{:S(2)}) copy-start(bf16[4,6144]{1,0:T(4,128)(2,1)} %copy-done.6) | copy-start | bytes 147460
  1061.9 151.7 %copy-start.9 = (bf16[4,6144]{1,0:T(4,128)(2,1)S(1)}, bf16[4,6144]{1,0:T(4,128)(2,1)}, u32[]{:S(2)}) copy-start(bf16[4,6144]{1,0:T(4,128)(2,1)} %copy-done.8) | copy-start | bytes 147460
  1061.9 151.7 %copy-start.11 = (bf16[4,6144]{1,0:T(4,128)(2,1)S(1)}, bf16[4,6144]{1,0:T(4,128)(2,1)}, u32[]{:S(2)}) copy-start(bf16[4,6144]{1,0:T(4,128)(2,1)} %copy-done.10) | copy-start | bytes 147460
  1061.9 151.7 %copy-start.13 = (bf16[4,6144]{1,0:T(4,128)(2,1)S(1)}, bf16[4,6144]{1,0:T(4,128)(2,1)}, u32[]{:S(2)}) copy-start(bf16[4,6144]{1,0:T(4,128)(2,1)} %copy-done.12) | copy-start | bytes 147460
  1061.9 151.7 %copy-start.16 = (f32[4]{0:T(128)S(1)}, f32[4]{0:T(128)}, u32[]{:S(2)}) copy-start(f32[4]{0:T(128)} %copy-done.15) | copy-start | bytes 52
  1061.9 151.7 %copy-start.18 = (f32[4]{0:T(128)S(1)}, f32[4]{0:T(128)}, u32[]{:S(2)}) copy-start(f32[4]{0:T(128)} %copy-done.17) | copy-start | bytes 52
Sparse Core Ops, SparseCore 0:
  11.7 85.0 all-gather.20
  98.9 44.2 all-gather.16
  145.3 43.4 all-gather.18
  193.1 158.9 all-reduce.8
  361.3 82.0 all-gather.22
  453.3 159.6 all-reduce.10
  622.2 82.0 all-gather.24
  714.0 159.6 all-reduce.12
  883.0 81.5 all-gather.26
  968.1 80.6 all-gather.14
  1052.6 159.7 all-reduce.14
where the time goes:
time: 1230 us
  waiting for transfers between devices  984 us (80%)
  other arithmetic  86.2 us (7%)
  local copies, waits for them, and re-layouts  60.1 us (5%)
  blocking collectives  39.9 us (3%)
  matrix products  30.1 us (2%)
  between operations  14.9 us (1%)
  starting transfers between devices  14.2 us (1%)
    unnamed x15, waiting for transfers between devices  626 us
    all_gather x4, waiting for transfers between devices, per_device(): grad_rows = lax.all_gather(grad_in, 'tensor', axis=0, tiled=True)  259 us
    unnamed x6, other arithmetic  73.4 us
    all_gather x1, waiting for transfers between devices, per_device(): down_full = lax.all_gather(w_down[0], 'dp', axis=1, tiled=True)  43.7 us
    all_gather x1, waiting for transfers between devices, per_device(): up_full = lax.all_gather(w_up[0], 'dp', axis=0, tiled=True)  42.5 us
    unnamed x49, local copies, waits for them, and re-layouts  36.3 us
  transfers between devices with their start and end apart: 15, of which 13 were waited for; matrix products, arithmetic and copies ran while one was open for 11% of the time, Pallas kernels for 0%

commit v1 on v0

v1 whole, which is shorter than its diff:
```python
import jax
import jax.numpy as jnp
from jax import lax
from jax.sharding import PartitionSpec as P

epsilon = 1e-06
f32 = jnp.float32
bf16 = jnp.bfloat16
LANES = 128


def exchange(blocks, axis):
    shape = blocks.shape
    flat = blocks.reshape(shape[0], -1, LANES)
    return lax.all_to_all(flat, axis, 0, 0).reshape(shape)


def after(value, *others):
    return lax.optimization_barrier((value,) + others)[0]


def per_device(section_input, pre_act, cotangent, w_up, w_down):
    pipe = lax.axis_size("pipe")
    parts = lax.axis_size("tensor")
    groups = lax.axis_size("dp")
    pipe_index = lax.axis_index("pipe")
    own_rows, width = section_input.shape[-2:]
    block = width // groups
    rows, hidden_width = pre_act.shape[-2:]
    tokens = parts * groups

    x_own = section_input[0, 0, 0]
    u_own = pre_act[0, 0, 0]
    x_own_f = x_own.astype(f32)
    inverse_own = lax.rsqrt(jnp.mean(x_own_f * x_own_f, axis=-1, keepdims=True) + epsilon)
    normed_own = (x_own_f * inverse_own).astype(bf16)

    down_all = lax.all_gather(w_down[0], "pipe", axis=0)
    up_all = lax.all_gather(w_up[0], "pipe", axis=0)

    cot_row = lax.dynamic_index_in_dim(cotangent[0, 0], pipe_index, 0, keepdims=False)
    grad = exchange(cot_row.reshape(groups, block), "dp")

    x_blocks = exchange(x_own.reshape(pipe * groups, block), ("pipe", "dp"))
    x_blocks = x_blocks.reshape(pipe, groups, block).astype(f32)
    square = lax.psum(jnp.sum(x_blocks * x_blocks, axis=-1), "dp")
    inverse = lax.rsqrt(square / width + epsilon)[..., None]

    u_rows = jnp.swapaxes(u_own.reshape(parts, pipe, hidden_width), 0, 1)
    u_rows = exchange(u_rows, "pipe")
    u_rows = lax.all_gather(u_rows, "dp", axis=2)
    u_rows = u_rows.reshape(pipe, tokens, hidden_width).astype(f32)
    sigmoid_u = jax.nn.sigmoid(u_rows)
    slope = sigmoid_u * (1.0 + u_rows * (1.0 - sigmoid_u))

    u_f = u_own.astype(f32)
    hidden = (u_f * jax.nn.sigmoid(u_f)).astype(bf16)
    hidden_all = lax.all_gather(hidden, "dp", axis=0)

    normed_blocks = exchange(
        jnp.swapaxes(normed_own.reshape(own_rows, groups, block), 0, 1), "dp"
    )
    normed_blocks = after(normed_blocks, up_all, down_all)
    normed_all = lax.all_gather(normed_blocks, "tensor", axis=0)

    rows_store, pre_store, out_store = [], [], []
    for section in reversed(range(pipe)):
        spread = jnp.broadcast_to(grad[None], (parts,) + grad.shape)
        grad_rows = exchange(spread, "tensor").reshape(tokens, block)
        rows_store.append(grad_rows)
        partial = lax.dot_general(
            grad_rows, down_all[section], (((1,), (1,)), ((), ())), preferred_element_type=f32
        ).astype(bf16)
        partials = lax.all_gather(partial, "dp", axis=0)
        hidden_grad = jnp.sum(partials.astype(f32), axis=0)
        pre_grad = (hidden_grad * slope[section]).astype(bf16)
        pre_store.append(pre_grad)
        pieces = lax.dot_general(
            pre_grad, up_all[section], (((1,), (1,)), ((), ())), preferred_element_type=f32
        ).astype(bf16)
        pieces = exchange(pieces.reshape(parts, groups, block), "tensor")
        normed_grad = jnp.sum(pieces.astype(f32), axis=0)
        x_s = x_blocks[section]
        inv = inverse[section]
        mean_term = lax.psum(jnp.sum(normed_grad * x_s, axis=-1, keepdims=True), "dp") / width
        grad_f = grad.astype(f32) + inv * normed_grad - x_s * inv**3 * mean_term
        grad = grad_f.astype(bf16)
        out_store.append(grad)

    grads = exchange(jnp.stack(rows_store[::-1]), "pipe").reshape(-1, block)
    pres = exchange(jnp.stack(pre_store[::-1]), "pipe")
    hidden_all = jnp.transpose(
        hidden_all.reshape(groups, parts, pipe, hidden_width), (2, 1, 0, 3)
    ).reshape(-1, hidden_width)
    down_grad = lax.dot_general(
        hidden_all, grads, (((0,), (0,)), ((), ())), preferred_element_type=f32
    ).astype(bf16)
    pres = jnp.transpose(
        pres.reshape(pipe, parts, groups, hidden_width), (1, 2, 0, 3)
    ).reshape(-1, hidden_width)
    up_grad = lax.dot_general(
        normed_all.reshape(-1, block), pres, (((0,), (0,)), ((), ())), preferred_element_type=f32
    ).astype(bf16)

    outs = exchange(jnp.stack(out_store[::-1]).reshape(pipe * groups, block), ("pipe", "dp"))
    input_grad = outs.reshape(1, 1, 1, own_rows, width)
    return (input_grad, up_grad[None], down_grad[None])


def solution(mesh):
    return jax.shard_map(
        per_device,
        mesh=mesh,
        in_specs=(
            P("pipe", None, "dp", "tensor", None),
            P("pipe", None, "dp", None, "tensor"),
            P(None, "dp", "tensor", None),
            P("pipe", "dp", "tensor"),
            P("pipe", "tensor", "dp"),
        ),
        out_specs=(
            P("pipe", None, "dp", "tensor", None),
            P("pipe", "dp", "tensor"),
            P("pipe", "tensor", "dp"),
        ),
        check_vma=False,
    )
```

time: 1230 us -> 452 us (0.37)
  waiting for transfers between devices: 984 us -> 157 us
  blocking collectives: 39.9 us -> 155 us
  other arithmetic: 86.2 us -> 6.61 us
  starting transfers between devices: 14.2 us -> 81.8 us
  local copies, waits for them, and re-layouts: 60.1 us -> 16.4 us
  matrix products: 30.1 us -> 17.2 us
    unnamed x15 -> x3, waiting for transfers between devices: 626 us -> 1.39 us
    all_gather x7 -> x3, waiting for transfers between devices: 345 us -> 83.8 us  [the longest x1 62.4 us: per_device(): up_all = lax.all_gather(w_up[0], 'pipe', axis=0)]
    unnamed x6 -> x0, other arithmetic: 73.4 us -> none
    all_to_all x1 -> x13, starting transfers between devices: 9.51 us -> 81.7 us  [exchange(): return lax.all_to_all(flat, axis, 0, 0).reshape(shape)]
    all_to_all x1 -> x13, waiting for transfers between devices: 0.01 us -> 71.4 us  [exchange(): return lax.all_to_all(flat, axis, 0, 0).reshape(shape)]
    all_gather x2 -> x6, blocking collectives: 28 us -> 87.9 us  [the longest x4 33.8 us: per_device(): partials = lax.all_gather(partial, 'dp', axis=0)]
    unnamed x49 -> x6, local copies, waits for them, and re-layouts: 36.3 us -> 0.02 us
    psum x0 -> x4, blocking collectives: none -> 36.2 us  [per_device(): lax.psum(jnp.sum(normed_grad * x_s, axis=-1, keepdims=True), 'dp') / width]
  transfers between devices with their start and end apart: 15 -> 16, of which waited for: 13 -> 11; matrix products, arithmetic and copies ran while one was open for 11% -> 5% of each run, Pallas kernels for 0% -> 0%
where the time goes in v1:
time: 452 us; the launch traced here: 448 us
  waiting for transfers between devices  157 us (35%)
  blocking collectives  155 us (34%)
  starting transfers between devices  81.8 us (18%)
  matrix products  17.2 us (4%)
  local copies, waits for them, and re-layouts  16.4 us (4%)
  between operations  14.2 us (3%)
  other arithmetic  6.61 us (1%)
    all_to_all x13, starting transfers between devices, exchange(): return lax.all_to_all(flat, axis, 0, 0).reshape(shape)  81.7 us
    all_to_all x13, waiting for transfers between devices, exchange(): return lax.all_to_all(flat, axis, 0, 0).reshape(shape)  71.4 us
    all_gather x1, waiting for transfers between devices, per_device(): up_all = lax.all_gather(w_up[0], 'pipe', axis=0)  62.4 us
    psum x4, blocking collectives, per_device(): lax.psum(jnp.sum(normed_grad * x_s, axis=-1, keepdims=True), 'dp') / width  36.2 us
    all_gather x4, blocking collectives, per_device(): partials = lax.all_gather(partial, 'dp', axis=0)  33.8 us
    all_gather x1, blocking collectives, per_device(): hidden_all = lax.all_gather(hidden, 'dp', axis=0)  33 us
    all_to_all x2, blocking collectives, exchange(): return lax.all_to_all(flat, axis, 0, 0).reshape(shape)  30.8 us
    all_gather x1, blocking collectives, per_device(): u_rows = lax.all_gather(u_rows, 'dp', axis=2)  21.1 us
  transfers between devices with their start and end apart: 16, of which 11 were waited for; matrix products, arithmetic and copies ran while one was open for 5% of the time, Pallas kernels for 0%

profile of v1, /device:TPU:1, one launch (start us, length us, event | category | flops | bytes accessed | tf_op | source)
XLA Modules:
  0.0 447.6 jit_solution(18329061567899263568)
XLA Ops:
  7.2 0.7 all-gather.9.cloned.1.call-update
  8.0 0.7 all-gather.11.cloned.1.call-update
  8.8 0.6 reshape_reshape.40
  9.4 10.1 %all-to-all-start = ((bf16[4,12,128]{2,1,0:T(8,128)(2,1)}), bf16[4,12,128]{2,1,0:T(8,128)(2,1)S(1)}, u32[]{:S(2)}, u32[]{:S(2)}) async-start(bf16[4,12,128]{2,1,0:T(8,128)(2,1)} %reshape_reshape.40), calls=%async_computation | async-start | bytes 32768 | tf_op jit(solution)/shard_map/all_to_all | solution.py:15
  19.5 0.7 reshape.570
  20.2 2.4 all-to-all-done
  22.6 3.3 all-to-all-start.3
  25.9 6.8 %all-to-all-done.3 = bf16[4,64,128]{2,1,0:T(8,128)(2,1)S(1)} async-done(((bf16[4,64,128]{2,1,0:T(8,128)(2,1)}), bf16[4,64,128]{2,1,0:T(8,128)(2,1)S(1)}, u32[]{:S(2)}, u32[]{:S(2)}) %all-to-all-start.3) | async-done | bytes 65568 | tf_op jit(solution)/shard_map/all_to_all | solution.py:15
  32.8 0.8 broadcast_in_dim.52
  33.6 11.4 %all-to-all-start.2 = ((bf16[32,48,128]{2,1,0:T(8,128)(2,1)}), bf16[32,48,128]{2,1,0:T(8,128)(2,1)S(1)}, u32[]{:S(2)}, u32[]{:S(2)}) async-start(bf16[32,48,128]{2,1,0:T(8,128)(2,1)} %broadcast_in_dim.52), calls=%async_computation.2 | async-start | bytes 786432 | tf_op jit(solution)/shard_map/all_to_all | solution.py:15
  45.0 0.7 reshape_reshape_squeeze.3
  45.7 21.1 %all_gather.46 = bf16[4,32,4,256]{3,1,0,2:T(8,128)(2,1)S(1)} all-gather(bf16[4,32,1,256]{3,1,0,2:T(8,128)(2,1)S(1)} %all_gather_reshape.3), channel_id=1, replica_groups=mesh['pipe'=4,'tensor'=32,'dp'=4] {'dp'}, dimensions={2}, use_global_device_ids=true | all-gather | bytes 327680 | tf_op jit(solution)/shard_map/all_gather | solution.py:51
  67.4 3.7 all-to-all-start.1
  71.5 18.1 %all-gather.9.cloned.1.call-done = bf16[4,256,1536]{2,1,0:T(8,128)(2,1)} async-done(((bf16[1,256,1536]{2,1,0:T(8,128)(2,1)}), bf16[4,256,1536]{2,1,0:T(8,128)(2,1)}) %all-gather.9.cloned.1.call-update) | async-done | bytes 3145744 | tf_op jit(solution)/shard_map/all_gather | solution.py:38
  89.7 1.5 convolution_convert_fusion.8
  91.2 6.4 %all-gather = bf16[512,256]{1,0:T(8,128)(2,1)S(1)} all-gather(bf16[128,256]{1,0:T(8,128)(2,1)S(1)} %convolution_convert_fusion.8), channel_id=2, replica_groups=mesh['pipe'=4,'tensor'=32,'dp'=4] {'dp'}, dimensions={0}, use_global_device_ids=true | all-gather | bytes 327680 | tf_op jit(solution)/shard_map/all_gather | solution.py:74
  98.1 62.4 %all-gather.11.cloned.1.call-done = bf16[4,1536,256]{2,1,0:T(8,128)(2,1)} async-done(((bf16[1,1536,256]{2,1,0:T(8,128)(2,1)}), bf16[4,1536,256]{2,1,0:T(8,128)(2,1)}) %all-gather.11.cloned.1.call-update) | async-done | bytes 3145744 | tf_op jit(solution)/shard_map/all_gather | solution.py:39
  160.5 1.5 convolution_convert_fusion.4
  162.0 1.2 reshape_reshape.42
  163.2 9.3 %all-to-all-start.4 = ((bf16[32,48,128]{2,1,0:T(8,128)(2,1)}), bf16[32,48,128]{2,1,0:T(8,128)(2,1)S(1)}, u32[]{:S(2)}, u32[]{:S(2)}) async-start(bf16[32,48,128]{2,1,0:T(8,128)(2,1)} %reshape_reshape.42), calls=%async_computation.4 | async-start | bytes 786432 | tf_op jit(solution)/shard_map/all_to_all | solution.py:15
  172.9 11.3 %all-to-all-done.4 = bf16[32,48,128]{2,1,0:T(8,128)(2,1)S(1)} async-done(((bf16[32,48,128]{2,1,0:T(8,128)(2,1)}), bf16[32,48,128]{2,1,0:T(8,128)(2,1)S(1)}, u32[]{:S(2)}, u32[]{:S(2)}) %all-to-all-start.4) | async-done | bytes 393248 | tf_op jit(solution)/shard_map/all_to_all | solution.py:15
  184.6 11.5 %all-reduce = (f32[4,1]{0,1:T(1,128)S(1)}, f32[4,4]{1,0:T(4,128)S(1)}) all-reduce(f32[4,1]{0,1:T(1,128)S(1)} %bitcast.139, f32[4,4]{1,0:T(4,128)S(1)} %reduce_sum.173), channel_id=1, replica_groups=mesh['pipe'=4,'tensor'=32,'dp'=4] {'dp'}, use_global_device_ids=true, to_apply=%region_6.7 | all-reduce | flops 20 | bytes 160 | tf_op jit(solution)/shard_map/psum | solution.py:85
  196.3 15.2 %all_to_all.75 = bf16[32,48,128]{2,1,0:T(8,128)(2,1)S(1)} all-to-all(bf16[32,48,128]{2,1,0:T(8,128)(2,1)S(1)} %broadcast_in_dim.55), channel_id=1, replica_groups=mesh['pipe'=4,'tensor'=32,'dp'=4] {'tensor'}, dimensions={0} | all-to-all | bytes 786432 | tf_op jit(solution)/shard_map/all_to_all | solution.py:15
  212.0 1.5 convolution_convert_fusion.7
  213.5 10.6 %all-gather.1 = bf16[512,256]{1,0:T(8,128)(2,1)S(1)} all-gather(bf16[128,256]{1,0:T(8,128)(2,1)S(1)} %convolution_convert_fusion.7), channel_id=3, replica_groups=mesh['pipe'=4,'tensor'=32,'dp'=4] {'dp'}, dimensions={0}, use_global_device_ids=true | all-gather | bytes 327680 | tf_op jit(solution)/shard_map/all_gather | solution.py:74
  224.7 1.5 convolution_convert_fusion.3
  226.2 1.2 reshape_reshape.44
  227.4 4.8 %all-to-all-start.6 = ((bf16[32,48,128]{2,1,0:T(8,128)(2,1)}), bf16[32,48,128]{2,1,0:T(8,128)(2,1)S(1)}, u32[]{:S(2)}, u32[]{:S(2)}) async-start(bf16[32,48,128]{2,1,0:T(8,128)(2,1)} %reshape_reshape.44), calls=%async_computation.6 | async-start | bytes 786432 | tf_op jit(solution)/shard_map/all_to_all | solution.py:15
  232.3 12.1 %all-to-all-done.6 = bf16[32,48,128]{2,1,0:T(8,128)(2,1)S(1)} async-done(((bf16[32,48,128]{2,1,0:T(8,128)(2,1)}), bf16[32,48,128]{2,1,0:T(8,128)(2,1)S(1)}, u32[]{:S(2)}, u32[]{:S(2)}) %all-to-all-start.6) | async-done | bytes 393248 | tf_op jit(solution)/shard_map/all_to_all | solution.py:15
  244.8 7.9 %psum.37 = f32[4,1]{0,1:T(1,128)S(1)} all-reduce(f32[4,1]{0,1:T(1,128)S(1)} %bitcast.141), channel_id=1, replica_groups=mesh['pipe'=4,'tensor'=32,'dp'=4] {'dp'}, use_global_device_ids=true, to_apply=%region_11.12 | all-reduce | flops 4 | bytes 32 | tf_op jit(solution)/shard_map/psum | solution.py:85
  252.8 15.6 %all_to_all.76 = bf16[32,48,128]{2,1,0:T(8,128)(2,1)S(1)} all-to-all(bf16[32,48,128]{2,1,0:T(8,128)(2,1)S(1)} %broadcast_in_dim.58), channel_id=1, replica_groups=mesh['pipe'=4,'tensor'=32,'dp'=4] {'tensor'}, dimensions={0} | all-to-all | bytes 786432 | tf_op jit(solution)/shard_map/all_to_all | solution.py:15
  268.9 1.5 convolution_convert_fusion.6
  270.4 10.7 %all-gather.2 = bf16[512,256]{1,0:T(8,128)(2,1)S(1)} all-gather(bf16[128,256]{1,0:T(8,128)(2,1)S(1)} %convolution_convert_fusion.6), channel_id=4, replica_groups=mesh['pipe'=4,'tensor'=32,'dp'=4] {'dp'}, dimensions={0}, use_global_device_ids=true | all-gather | bytes 327680 | tf_op jit(solution)/shard_map/all_gather | solution.py:74
  281.6 1.5 convolution_convert_fusion.2
  283.2 1.2 reshape_reshape.46
  284.4 4.8 %all-to-all-start.8 = ((bf16[32,48,128]{2,1,0:T(8,128)(2,1)}), bf16[32,48,128]{2,1,0:T(8,128)(2,1)S(1)}, u32[]{:S(2)}, u32[]{:S(2)}) async-start(bf16[32,48,128]{2,1,0:T(8,128)(2,1)} %reshape_reshape.46), calls=%async_computation.8 | async-start | bytes 786432 | tf_op jit(solution)/shard_map/all_to_all | solution.py:15
  289.2 12.1 %all-to-all-done.8 = bf16[32,48,128]{2,1,0:T(8,128)(2,1)S(1)} async-done(((bf16[32,48,128]{2,1,0:T(8,128)(2,1)}), bf16[32,48,128]{2,1,0:T(8,128)(2,1)S(1)}, u32[]{:S(2)}, u32[]{:S(2)}) %all-to-all-start.8) | async-done | bytes 393248 | tf_op jit(solution)/shard_map/all_to_all | solution.py:15
  301.7 7.9 %psum.38 = f32[4,1]{0,1:T(1,128)S(1)} all-reduce(f32[4,1]{0,1:T(1,128)S(1)} %bitcast.142), channel_id=1, replica_groups=mesh['pipe'=4,'tensor'=32,'dp'=4] {'dp'}, use_global_device_ids=true, to_apply=%region_16.17 | all-reduce | flops 4 | bytes 32 | tf_op jit(solution)/shard_map/psum | solution.py:85
  309.7 0.8 broadcast_in_dim.61
  310.5 5.3 %all-to-all-start.9 = ((bf16[32,48,128]{2,1,0:T(8,128)(2,1)}), bf16[32,48,128]{2,1,0:T(8,128)(2,1)S(1)}, u32[]{:S(2)}, u32[]{:S(2)}) async-start(bf16[32,48,128]{2,1,0:T(8,128)(2,1)} %broadcast_in_dim.61), calls=%async_computation.9 | async-start | bytes 786432 | tf_op jit(solution)/shard_map/all_to_all | solution.py:15
  316.1 0.6 reshape.571
  316.8 9.6 %all-to-all-done.9 = bf16[32,48,128]{2,1,0:T(8,128)(2,1)S(1)} async-done(((bf16[32,48,128]{2,1,0:T(8,128)(2,1)}), bf16[32,48,128]{2,1,0:T(8,128)(2,1)S(1)}, u32[]{:S(2)}, u32[]{:S(2)}) %all-to-all-start.9) | async-done | bytes 393248 | tf_op jit(solution)/shard_map/all_to_all | solution.py:15
  326.3 8.1 %all-to-all-start.12 = ((bf16[4,48,128]{2,1,0:T(8,128)(2,1)}), bf16[4,48,128]{2,1,0:T(8,128)(2,1)S(1)}, u32[]{:S(2)}, u32[]{:S(2)}) async-start(bf16[4,48,128]{2,1,0:T(8,128)(2,1)} %reshape.571), calls=%async_computation.12 | async-start | bytes 98304 | tf_op jit(solution)/shard_map/all_to_all | solution.py:15
  334.9 1.5 convolution_convert_fusion.5
  336.4 6.1 %all-gather.3 = bf16[512,256]{1,0:T(8,128)(2,1)S(1)} all-gather(bf16[128,256]{1,0:T(8,128)(2,1)S(1)} %convolution_convert_fusion.5), channel_id=5, replica_groups=mesh['pipe'=4,'tensor'=32,'dp'=4] {'dp'}, dimensions={0}, use_global_device_ids=true | all-gather | bytes 327680 | tf_op jit(solution)/shard_map/all_gather | solution.py:74
  343.1 1.5 convolution_convert_fusion.1
  344.6 1.2 reshape_reshape.48
  345.8 5.0 %all-to-all-start.10 = ((bf16[32,48,128]{2,1,0:T(8,128)(2,1)}), bf16[32,48,128]{2,1,0:T(8,128)(2,1)S(1)}, u32[]{:S(2)}, u32[]{:S(2)}) async-start(bf16[32,48,128]{2,1,0:T(8,128)(2,1)} %reshape_reshape.48), calls=%async_computation.10 | async-start | bytes 786432 | tf_op jit(solution)/shard_map/all_to_all | solution.py:15
  350.8 0.6 reshape.572
  351.6 0.7 pad_maximum_fusion.1
  352.4 10.5 %all-to-all-done.10 = bf16[32,48,128]{2,1,0:T(8,128)(2,1)S(1)} async-done(((bf16[32,48,128]{2,1,0:T(8,128)(2,1)}), bf16[32,48,128]{2,1,0:T(8,128)(2,1)S(1)}, u32[]{:S(2)}, u32[]{:S(2)}) %all-to-all-start.10) | async-done | bytes 393248 | tf_op jit(solution)/shard_map/all_to_all | solution.py:15
  362.9 4.0 all-to-all-start.13
  367.3 8.9 %psum.39 = f32[4,1]{0,1:T(1,128)S(1)} all-reduce(f32[4,1]{0,1:T(1,128)S(1)} %bitcast.140), channel_id=1, replica_groups=mesh['pipe'=4,'tensor'=32,'dp'=4] {'dp'}, use_global_device_ids=true, to_apply=%region_21.22 | all-reduce | flops 4 | bytes 32 | tf_op jit(solution)/shard_map/psum | solution.py:85
  376.4 0.7 reshape_reshape.49
  377.1 8.3 %all-to-all-start.11 = ((bf16[16,12,128]{2,1,0:T(8,128)(2,1)}), bf16[16,12,128]{2,1,0:T(8,128)(2,1)S(1)}, u32[]{:S(2)}, u32[]{:S(2)}) async-start(bf16[16,12,128]{2,1,0:T(8,128)(2,1)} %reshape_reshape.49), calls=%async_computation.11 | async-start | bytes 131072 | tf_op jit(solution)/shard_map/all_to_all | solution.py:15
  385.4 1.3 pad_maximum_fusion
  386.7 6.5 %all-to-all-done.11 = bf16[16,12,128]{2,1,0:T(8,128)(2,1)S(1)} async-done(((bf16[16,12,128]{2,1,0:T(8,128)(2,1)}), bf16[16,12,128]{2,1,0:T(8,128)(2,1)S(1)}, u32[]{:S(2)}, u32[]{:S(2)}) %all-to-all-start.11) | async-done | bytes 49184 | tf_op jit(solution)/shard_map/all_to_all | solution.py:15
  393.2 3.6 all-to-all-start.14
  396.8 33.0 %all_gather.56 = bf16[4,128,256]{2,1,0:T(8,128)(2,1)S(1)} all-gather(bf16[1,128,256]{2,1,0:T(8,128)(2,1)S(1)} %fusion.14), channel_id=1, replica_groups=mesh['pipe'=4,'tensor'=32,'dp'=4] {'dp'}, dimensions={0}, use_global_device_ids=true | all-gather | bytes 327680 | tf_op jit(solution)/shard_map/all_gather | solution.py:58
  430.4 3.2 all-gather.13.cloned.1.call-done
  433.6 3.5 fusion.1
  437.2 0.6 reshape_reshape.50
  437.8 1.8 reshape_reshape.52
  439.6 1.5 fusion.2
  (95 shorter events, 8.2 us)
Async XLA Ops:
  7.2 1.5 copy-start
  7.2 12.3 %copy-start.2 = (bf16[1,1,1,128,256]{4,3,2,1,0:T(8,128)(2,1)S(1)}, bf16[1,1,1,128,256]{4,3,2,1,0:T(8,128)(2,1)}, u32[]{:S(2)}) copy-start(bf16[1,1,1,128,256]{4,3,2,1,0:T(8,128)(2,1)} %param.6) | copy-start | bytes 196612
  7.2 37.8 %copy-start.1 = (bf16[1,1,1,4,6144]{4,3,2,1,0:T(4,128)(2,1)S(1)}, bf16[1,1,1,4,6144]{4,3,2,1,0:T(4,128)(2,1)}, u32[]{:S(2)}) copy-start(bf16[1,1,1,4,6144]{4,3,2,1,0:T(4,128)(2,1)} %param.5) | copy-start | bytes 147460
  7.2 82.5 %all-gather.9.cloned.1.call-start = ((), (), s32[]{:S(2)}) async-start(), calls=%async_computation.15 | async-start | bytes 3932160 | tf_op jit(solution)/shard_map/all_gather | solution.py:38
  7.9 152.6 %all-gather.11.cloned.1.call-start = ((), (), s32[]{:S(2)}) async-start(), calls=%async_computation.16 | async-start | bytes 3932160 | tf_op jit(solution)/shard_map/all_gather | solution.py:39
  9.4 13.2 %all-to-all-start = ((bf16[4,12,128]{2,1,0:T(8,128)(2,1)}), bf16[4,12,128]{2,1,0:T(8,128)(2,1)S(1)}, u32[]{:S(2)}, u32[]{:S(2)}) async-start(bf16[4,12,128]{2,1,0:T(8,128)(2,1)} %reshape_reshape.40), calls=%async_computation | async-start | bytes 32768 | tf_op jit(solution)/shard_map/all_to_all | solution.py:15
  22.6 10.1 %all-to-all-start.3 = ((bf16[4,64,128]{2,1,0:T(8,128)(2,1)}), bf16[4,64,128]{2,1,0:T(8,128)(2,1)S(1)}, u32[]{:S(2)}, u32[]{:S(2)}) async-start(bf16[4,64,128]{2,1,0:T(8,128)(2,1)} %reshape.570), calls=%async_computation.3 | async-start | bytes 131072 | tf_op jit(solution)/shard_map/all_to_all | solution.py:15
  33.6 33.8 %all-to-all-start.2 = ((bf16[32,48,128]{2,1,0:T(8,128)(2,1)}), bf16[32,48,128]{2,1,0:T(8,128)(2,1)S(1)}, u32[]{:S(2)}, u32[]{:S(2)}) async-start(bf16[32,48,128]{2,1,0:T(8,128)(2,1)} %broadcast_in_dim.52), calls=%async_computation.2 | async-start | bytes 786432 | tf_op jit(solution)/shard_map/all_to_all | solution.py:15
  67.4 95.8 %all-to-all-start.1 = ((bf16[16,12,128]{2,1,0:T(8,128)(2,1)}), bf16[16,12,128]{2,1,0:T(8,128)(2,1)S(1)}, u32[]{:S(2)}, u32[]{:S(2)}) async-start(bf16[16,12,128]{2,1,0:T(8,128)(2,1)} %reshape_reshape_squeeze.3), calls=%async_computation.1 | async-start | bytes 131072 | tf_op jit(solution)/shard_map/all_to_all | solution.py:15
  163.2 21.0 %all-to-all-start.4 = ((bf16[32,48,128]{2,1,0:T(8,128)(2,1)}), bf16[32,48,128]{2,1,0:T(8,128)(2,1)S(1)}, u32[]{:S(2)}, u32[]{:S(2)}) async-start(bf16[32,48,128]{2,1,0:T(8,128)(2,1)} %reshape_reshape.42), calls=%async_computation.4 | async-start | bytes 786432 | tf_op jit(solution)/shard_map/all_to_all | solution.py:15
  227.4 17.0 %all-to-all-start.6 = ((bf16[32,48,128]{2,1,0:T(8,128)(2,1)}), bf16[32,48,128]{2,1,0:T(8,128)(2,1)S(1)}, u32[]{:S(2)}, u32[]{:S(2)}) async-start(bf16[32,48,128]{2,1,0:T(8,128)(2,1)} %reshape_reshape.44), calls=%async_computation.6 | async-start | bytes 786432 | tf_op jit(solution)/shard_map/all_to_all | solution.py:15
  284.4 17.0 %all-to-all-start.8 = ((bf16[32,48,128]{2,1,0:T(8,128)(2,1)}), bf16[32,48,128]{2,1,0:T(8,128)(2,1)S(1)}, u32[]{:S(2)}, u32[]{:S(2)}) async-start(bf16[32,48,128]{2,1,0:T(8,128)(2,1)} %reshape_reshape.46), calls=%async_computation.8 | async-start | bytes 786432 | tf_op jit(solution)/shard_map/all_to_all | solution.py:15
  310.5 15.8 %all-to-all-start.9 = ((bf16[32,48,128]{2,1,0:T(8,128)(2,1)}), bf16[32,48,128]{2,1,0:T(8,128)(2,1)S(1)}, u32[]{:S(2)}, u32[]{:S(2)}) async-start(bf16[32,48,128]{2,1,0:T(8,128)(2,1)} %broadcast_in_dim.61), calls=%async_computation.9 | async-start | bytes 786432 | tf_op jit(solution)/shard_map/all_to_all | solution.py:15
  326.3 19.5 %all-to-all-start.12 = ((bf16[4,48,128]{2,1,0:T(8,128)(2,1)}), bf16[4,48,128]{2,1,0:T(8,128)(2,1)S(1)}, u32[]{:S(2)}, u32[]{:S(2)}) async-start(bf16[4,48,128]{2,1,0:T(8,128)(2,1)} %reshape.571), calls=%async_computation.12 | async-start | bytes 98304 | tf_op jit(solution)/shard_map/all_to_all | solution.py:15
  345.8 17.1 %all-to-all-start.10 = ((bf16[32,48,128]{2,1,0:T(8,128)(2,1)}), bf16[32,48,128]{2,1,0:T(8,128)(2,1)S(1)}, u32[]{:S(2)}, u32[]{:S(2)}) async-start(bf16[32,48,128]{2,1,0:T(8,128)(2,1)} %reshape_reshape.48), calls=%async_computation.10 | async-start | bytes 786432 | tf_op jit(solution)/shard_map/all_to_all | solution.py:15
  350.8 82.9 %all-gather.13.cloned.1.call-start = ((), (), s32[]{:S(2)}) async-start(), calls=%async_computation.17 | async-start | bytes 1622016 | tf_op jit(solution)/shard_map/all_gather | solution.py:64
  362.9 14.2 %all-to-all-start.13 = ((bf16[4,256,128]{2,1,0:T(8,128)(2,1)}), bf16[4,256,128]{2,1,0:T(8,128)(2,1)S(1)}, u32[]{:S(2)}, u32[]{:S(2)}) async-start(bf16[4,256,128]{2,1,0:T(8,128)(2,1)} %pad_maximum_fusion.1), calls=%async_computation.13 | async-start | bytes 524288 | tf_op jit(solution)/shard_map/all_to_all | solution.py:15
  377.1 16.1 %all-to-all-start.11 = ((bf16[16,12,128]{2,1,0:T(8,128)(2,1)}), bf16[16,12,128]{2,1,0:T(8,128)(2,1)S(1)}, u32[]{:S(2)}, u32[]{:S(2)}) async-start(bf16[16,12,128]{2,1,0:T(8,128)(2,1)} %reshape_reshape.49), calls=%async_computation.11 | async-start | bytes 131072 | tf_op jit(solution)/shard_map/all_to_all | solution.py:15
  393.2 44.6 %all-to-all-start.14 = ((bf16[4,1536,128]{2,1,0:T(8,128)(2,1)}), bf16[4,1536,128]{2,1,0:T(8,128)(2,1)S(1)}, u32[]{:S(2)}, u32[]{:S(2)}) async-start(bf16[4,1536,128]{2,1,0:T(8,128)(2,1)} %pad_maximum_fusion), calls=%async_computation.14 | async-start | bytes 3145728 | tf_op jit(solution)/shard_map/all_to_all | solution.py:15
Sparse Core Ops, SparseCore 0:
  10.1 79.4 all-gather.8
  91.8 68.6 all-gather.10
  355.3 78.2 all-gather.12

commit v2 on v1

v2 whole, which is shorter than its diff:
```python
import jax
import jax.numpy as jnp
from jax import lax
from jax.sharding import PartitionSpec as P

epsilon = 1e-06
f32 = jnp.float32
bf16 = jnp.bfloat16
LANES = 128


def exchange(blocks, axis):
    shape = blocks.shape
    flat = blocks.reshape(shape[0], -1, LANES)
    return lax.all_to_all(flat, axis, 0, 0).reshape(shape)


def after(value, *others):
    return lax.optimization_barrier((value,) + others)[0]


def slope_of(u):
    sigmoid_u = jax.nn.sigmoid(u)
    return sigmoid_u * (1.0 + u * (1.0 - sigmoid_u))


def dot_nt(left, right):
    product = lax.dot_general(left, right, (((1,), (1,)), ((), ())), preferred_element_type=f32)
    return product.astype(bf16)


def dot_tn(left, right):
    product = lax.dot_general(left, right, (((0,), (0,)), ((), ())), preferred_element_type=f32)
    return product.astype(bf16)


def per_device(section_input, pre_act, cotangent, w_up, w_down):
    pipe = lax.axis_size("pipe")
    parts = lax.axis_size("tensor")
    groups = lax.axis_size("dp")
    pipe_index = lax.axis_index("pipe")
    own_rows, width = section_input.shape[-2:]
    block = width // groups
    rows, hidden_width = pre_act.shape[-2:]
    tokens = parts * groups

    x_own = section_input[0, 0, 0]
    u_own = pre_act[0, 0, 0]
    x_own_f = x_own.astype(f32)
    inverse_own = lax.rsqrt(jnp.mean(x_own_f * x_own_f, axis=-1, keepdims=True) + epsilon)
    normed_own = (x_own_f * inverse_own).astype(bf16)

    down_all = lax.all_gather(w_down[0], "pipe", axis=0)
    up_all = lax.all_gather(w_up[0], "pipe", axis=0)

    cot_blocks = exchange(jnp.swapaxes(cotangent[0, 0].reshape(own_rows, groups, block), 0, 1), "dp")
    cot_blocks = jnp.swapaxes(cot_blocks, 0, 1)
    normed_blocks = exchange(jnp.swapaxes(normed_own.reshape(own_rows, groups, block), 0, 1), "dp")
    normed_blocks = jnp.swapaxes(normed_blocks, 0, 1)

    x_blocks = exchange(x_own.reshape(pipe * groups, block), ("pipe", "dp"))
    x_blocks = x_blocks.reshape(pipe, groups, block).astype(f32)
    square = lax.psum(jnp.sum(x_blocks * x_blocks, axis=-1), "dp")
    inverse = lax.rsqrt(square / width + epsilon)[..., None]

    u_rows = jnp.swapaxes(u_own.reshape(parts, pipe, hidden_width), 0, 1)
    u_rows = exchange(u_rows, "pipe")
    u_rows = lax.all_gather(u_rows, "dp", axis=2)
    u_rows = u_rows.reshape(pipe, tokens, hidden_width).astype(f32)
    slope = slope_of(u_rows)

    u_f = u_own.astype(f32)
    slope_own = slope_of(u_f)
    hidden = (u_f * jax.nn.sigmoid(u_f)).astype(bf16)
    hidden_all = lax.all_gather(hidden, "dp", axis=0)
    hidden_all = hidden_all.reshape(groups, parts, pipe, hidden_width)

    last = pipe - 1
    is_last = pipe_index == last
    spread = jnp.broadcast_to(cot_blocks[None], (parts,) + cot_blocks.shape)
    cot_rows = exchange(spread, "tensor").reshape(-1, block)
    partial = dot_nt(cot_rows, w_down[0])
    partial = jnp.transpose(partial.reshape(parts, pipe, groups, hidden_width), (2, 0, 1, 3))
    hidden_grad = jnp.sum(exchange(partial, "dp").astype(f32), axis=0).reshape(rows, hidden_width)
    pre_last = lax.all_gather((hidden_grad * slope_own).astype(bf16), "dp", axis=0)
    pre_last = jnp.transpose(pre_last.reshape(groups, parts, pipe, hidden_width), (1, 2, 0, 3))
    pre_last = pre_last.reshape(-1, hidden_width)
    pieces = exchange(dot_nt(pre_last, w_up[0]).reshape(parts, pipe * groups, block), "tensor")
    sums = jnp.sum(pieces.astype(f32), axis=0).reshape(pipe, groups, block)
    normed_grad = exchange(sums, "pipe")[last]

    normed_blocks = after(normed_blocks, up_all, down_all)
    normed_all = lax.all_gather(normed_blocks.reshape(-1, block), "tensor", axis=0, tiled=True)

    def finish(section, grad, normed_grad):
        x_s = x_blocks[section]
        inv = inverse[section]
        mean_term = lax.psum(jnp.sum(normed_grad * x_s, axis=-1, keepdims=True), "dp") / width
        grad_f = grad.astype(f32) + inv * normed_grad - x_s * inv**3 * mean_term
        return grad_f.astype(bf16)

    grad = lax.dynamic_index_in_dim(cot_blocks, pipe_index, 0, keepdims=False)
    grad = finish(last, grad, normed_grad)
    out_store = [grad]
    rows_store = [jnp.zeros((tokens, block), bf16)]
    pre_store = [jnp.zeros((tokens, hidden_width), bf16)]
    for section in reversed(range(last)):
        if section == 0:
            grad, normed_all = lax.optimization_barrier((grad, normed_all))
        spread = jnp.broadcast_to(grad[None], (parts,) + grad.shape)
        grad_rows = exchange(spread, "tensor").reshape(tokens, block)
        rows_store.append(grad_rows)
        partials = lax.all_gather(dot_nt(grad_rows, down_all[section]), "dp", axis=0)
        hidden_grad = jnp.sum(partials.astype(f32), axis=0)
        pre_grad = (hidden_grad * slope[section]).astype(bf16)
        pre_store.append(pre_grad)
        pieces = dot_nt(pre_grad, up_all[section]).reshape(parts, groups, block)
        pieces = exchange(pieces, "tensor")
        grad = finish(section, grad, jnp.sum(pieces.astype(f32), axis=0))
        out_store.append(grad)

    grads = exchange(jnp.stack(rows_store[::-1]), "pipe").reshape(-1, block)
    grads = jnp.where(is_last, cot_rows, grads)
    hidden_all = jnp.where(
        is_last,
        jnp.transpose(hidden_all, (1, 2, 0, 3)).reshape(-1, hidden_width),
        jnp.transpose(hidden_all, (2, 1, 0, 3)).reshape(-1, hidden_width),
    )
    down_grad = dot_tn(hidden_all, grads)
    pres = exchange(jnp.stack(pre_store[::-1]), "pipe")
    pres = jnp.swapaxes(pres.reshape(pipe, parts, groups, hidden_width), 0, 1)
    pres = jnp.where(is_last, pre_last, pres.reshape(-1, hidden_width))
    up_grad = dot_tn(normed_all, pres)

    outs = exchange(jnp.stack(out_store[::-1]).reshape(pipe * groups, block), ("pipe", "dp"))
    input_grad = outs.reshape(1, 1, 1, own_rows, width)
    return (input_grad, up_grad[None], down_grad[None])


def solution(mesh):
    return jax.shard_map(
        per_device,
        mesh=mesh,
        in_specs=(
            P("pipe", None, "dp", "tensor", None),
            P("pipe", None, "dp", None, "tensor"),
            P(None, "dp", "tensor", None),
            P("pipe", "dp", "tensor"),
            P("pipe", "tensor", "dp"),
        ),
        out_specs=(
            P("pipe", None, "dp", "tensor", None),
            P("pipe", "dp", "tensor"),
            P("pipe", "tensor", "dp"),
        ),
        check_vma=False,
    )
```

time: 452 us -> 515 us (1.14)
  local copies, waits for them, and re-layouts: 16.4 us -> 37.2 us
  waiting for transfers between devices: 157 us -> 170 us
  blocking collectives: 155 us -> 165 us
  other arithmetic: 6.61 us -> 15.8 us
  starting transfers between devices: 81.8 us -> 87 us
    all_to_all x13 -> x14, waiting for transfers between devices: 71.4 us -> 138 us  [exchange(): return lax.all_to_all(flat, axis, 0, 0).reshape(shape)]
    all_gather x1, waiting for transfers between devices: 62.4 us -> 0.02 us  [per_device(): up_all = lax.all_gather(w_up[0], 'pipe', axis=0)]
    all_gather x1, waiting for transfers between devices: 3.23 us -> 30 us  [per_device(): lax.all_gather(normed_blocks.reshape(-1, block), 'tensor', axis=0, tiled=...]
    all_to_all x2 -> x3, blocking collectives: 30.8 us -> 55.6 us  [exchange(): return lax.all_to_all(flat, axis, 0, 0).reshape(shape)]
    all_gather x1, waiting for transfers between devices: 18.1 us -> 0.02 us  [per_device(): down_all = lax.all_gather(w_down[0], 'pipe', axis=0)]
    all_gather x1, blocking collectives: 21.1 us -> 7.08 us  [per_device(): u_rows = lax.all_gather(u_rows, 'dp', axis=2)]
    psum x4, blocking collectives: 36.2 us -> 27.4 us  [finish(): lax.psum(jnp.sum(normed_grad * x_s, axis=-1, keepdims=True), 'dp') / width]
    all_gather x4, blocking collectives: 33.8 us -> 41.5 us  [the longest x3 33.5 us: per_device(): lax.all_gather(dot_nt(grad_rows, down_all[section]), 'dp', axis=0)]
  transfers between devices with their start and end apart: 16 -> 17, of which waited for: 11 -> 11; matrix products, arithmetic and copies ran while one was open for 5% -> 10% of each run, Pallas kernels for 0% -> 0%
where the time goes in v2:
time: 515 us; the launch traced here: 508 us
  waiting for transfers between devices  170 us (33%)
  blocking collectives  165 us (32%)
  starting transfers between devices  87 us (17%)
  local copies, waits for them, and re-layouts  37.2 us (7%)
  matrix products  18.7 us (4%)
  other arithmetic  15.8 us (3%)
  between operations  14.5 us (3%)
    all_to_all x14, waiting for transfers between devices, exchange(): return lax.all_to_all(flat, axis, 0, 0).reshape(shape)  138 us
    all_to_all x14, starting transfers between devices, exchange(): return lax.all_to_all(flat, axis, 0, 0).reshape(shape)  86.9 us
    all_to_all x3, blocking collectives, exchange(): return lax.all_to_all(flat, axis, 0, 0).reshape(shape)  55.6 us
    all_gather x3, blocking collectives, per_device(): lax.all_gather(dot_nt(grad_rows, down_all[section]), 'dp', axis=0)  33.5 us
    all_gather x1, blocking collectives, per_device(): hidden_all = lax.all_gather(hidden, 'dp', axis=0)  33.1 us
    all_gather x1, waiting for transfers between devices, per_device(): lax.all_gather(normed_blocks.reshape(-1, block), 'tensor', axis=0, tiled=...  30 us
    psum x4, blocking collectives, finish(): lax.psum(jnp.sum(normed_grad * x_s, axis=-1, keepdims=True), 'dp') / width  27.4 us
    dot_general x8, matrix products, dot_nt(): lax.dot_general(left, right, (((1,), (1,)), ((), ())), preferred_element_...  14.3 us
  transfers between devices with their start and end apart: 17, of which 11 were waited for; matrix products, arithmetic and copies ran while one was open for 10% of the time, Pallas kernels for 0%

profile of v2, /device:TPU:1, one launch (start us, length us, event | category | flops | bytes accessed | tf_op | source)
XLA Modules:
  0.0 507.7 jit_solution(14999905097132515606)
XLA Ops:
  8.0 12.5 %all_to_all.85 = bf16[4,48,128]{2,1,0:T(8,128)(2,1)S(1)} all-to-all(bf16[4,48,128]{2,1,0:T(8,128)(2,1)S(1)} %reshape.512), channel_id=1, replica_groups=mesh['pipe'=4,'tensor'=32,'dp'=4] {'dp'}, dimensions={0} | all-to-all | bytes 98304 | tf_op jit(solution)/shard_map/all_to_all | solution.py:15
  20.5 1.5 broadcast_in_dim.53
  22.0 7.8 %all-to-all-start.2 = ((bf16[32,192,128]{2,1,0:T(8,128)(2,1)}), bf16[32,192,128]{2,1,0:T(8,128)(2,1)S(1)}, u32[]{:S(2)}, u32[]{:S(2)}) async-start(bf16[32,192,128]{2,1,0:T(8,128)(2,1)} %broadcast_in_dim.53), calls=%async_computation.2 | async-start | bytes 3145728 | tf_op jit(solution)/shard_map/all_to_all | solution.py:15
  30.6 35.9 %all-to-all-done.2 = bf16[32,192,128]{2,1,0:T(8,128)(2,1)S(1)} async-done(((bf16[32,192,128]{2,1,0:T(8,128)(2,1)}), bf16[32,192,128]{2,1,0:T(8,128)(2,1)S(1)}, u32[]{:S(2)}, u32[]{:S(2)}) %all-to-all-start.2) | async-done | bytes 1572896 | tf_op jit(solution)/shard_map/all_to_all | solution.py:15
  66.5 1.8 reshape_reshape.40
  68.3 2.4 convolution_convert_fusion.6
  72.0 28.2 %all_to_all.86 = bf16[4,256,128]{2,1,0:T(8,128)(2,1)S(1)} all-to-all(bf16[4,256,128]{2,1,0:T(8,128)(2,1)S(1)} %reshape.515), channel_id=1, replica_groups=mesh['pipe'=4,'tensor'=32,'dp'=4] {'dp'}, dimensions={0} | all-to-all | bytes 524288 | tf_op jit(solution)/shard_map/all_to_all | solution.py:15
  100.9 8.0 %all_gather.38 = bf16[4,128,256]{2,1,0:T(8,128)(2,1)S(1)} all-gather(bf16[1,128,256]{2,1,0:T(8,128)(2,1)S(1)} %get-tuple-element.29), channel_id=1, replica_groups=mesh['pipe'=4,'tensor'=32,'dp'=4] {'dp'}, dimensions={0}, use_global_device_ids=true | all-gather | bytes 327680 | tf_op jit(solution)/shard_map/all_gather | solution.py:85
  109.3 1.8 convolution_convert_fusion
  111.1 2.7 reshape_reshape.41
  113.8 7.2 %all-to-all-start.4 = ((bf16[32,192,128]{2,1,0:T(8,128)(2,1)}), bf16[32,192,128]{2,1,0:T(8,128)(2,1)S(1)}, u32[]{:S(2)}, u32[]{:S(2)}) async-start(bf16[32,192,128]{2,1,0:T(8,128)(2,1)} %reshape_reshape.41), calls=%async_computation.4 | async-start | bytes 3145728 | tf_op jit(solution)/shard_map/all_to_all | solution.py:15
  124.0 33.5 %all-to-all-done.4 = bf16[32,192,128]{2,1,0:T(8,128)(2,1)S(1)} async-done(((bf16[32,192,128]{2,1,0:T(8,128)(2,1)}), bf16[32,192,128]{2,1,0:T(8,128)(2,1)S(1)}, u32[]{:S(2)}, u32[]{:S(2)}) %all-to-all-start.4) | async-done | bytes 1572896 | tf_op jit(solution)/shard_map/all_to_all | solution.py:15
  157.5 12.0 %all-to-all-start.1 = ((bf16[16,12,128]{2,1,0:T(8,128)(2,1)}), bf16[16,12,128]{2,1,0:T(8,128)(2,1)S(1)}, u32[]{:S(2)}, u32[]{:S(2)}) async-start(bf16[16,12,128]{2,1,0:T(8,128)(2,1)} %reshape_reshape_squeeze.3), calls=%async_computation.1 | async-start | bytes 131072 | tf_op jit(solution)/shard_map/all_to_all | solution.py:15
  170.3 9.2 %all-to-all-done.1 = bf16[16,12,128]{2,1,0:T(8,128)(2,1)S(1)} async-done(((bf16[16,12,128]{2,1,0:T(8,128)(2,1)}), bf16[16,12,128]{2,1,0:T(8,128)(2,1)S(1)}, u32[]{:S(2)}, u32[]{:S(2)}) %all-to-all-start.1) | async-done | bytes 49184 | tf_op jit(solution)/shard_map/all_to_all | solution.py:15
  179.5 3.3 all-to-all-start.5
  183.8 10.4 %all-to-all-done.5 = f32[4,48,128]{2,1,0:T(8,128)S(1)} async-done(((f32[4,48,128]{2,1,0:T(8,128)}), f32[4,48,128]{2,1,0:T(8,128)S(1)}, u32[]{:S(2)}, u32[]{:S(2)}) %all-to-all-start.5) | async-done | bytes 98336 | tf_op jit(solution)/shard_map/all_to_all | solution.py:15
  194.2 3.3 all-to-all-start.7
  197.8 6.0 %all-reduce = (f32[4,1]{0,1:T(1,128)S(1)}, f32[4,4]{1,0:T(4,128)S(1)}) all-reduce(f32[4,1]{0,1:T(1,128)S(1)} %bitcast.223, f32[4,4]{1,0:T(4,128)S(1)} %reduce_sum.173), channel_id=1, replica_groups=mesh['pipe'=4,'tensor'=32,'dp'=4] {'dp'}, use_global_device_ids=true, to_apply=%region_6.7 | all-reduce | flops 20 | bytes 160 | tf_op jit(solution)/shard_map/psum | solution.py:98
  206.5 8.0 %all-to-all-start.6 = ((bf16[32,48,128]{2,1,0:T(8,128)(2,1)}), bf16[32,48,128]{2,1,0:T(8,128)(2,1)S(1)}, u32[]{:S(2)}, u32[]{:S(2)}) async-start(bf16[32,48,128]{2,1,0:T(8,128)(2,1)} %broadcast_in_dim.56), calls=%async_computation.6 | async-start | bytes 786432 | tf_op jit(solution)/shard_map/all_to_all | solution.py:15
  214.6 7.1 %all_gather.42 = bf16[4,32,4,256]{3,1,0,2:T(8,128)(2,1)S(1)} all-gather(bf16[4,32,1,256]{3,1,0,2:T(8,128)(2,1)S(1)} %all_gather_reshape.3), channel_id=1, replica_groups=mesh['pipe'=4,'tensor'=32,'dp'=4] {'dp'}, dimensions={2}, use_global_device_ids=true | all-gather | bytes 327680 | tf_op jit(solution)/shard_map/all_gather | solution.py:68
  222.2 3.0 all-to-all-done.6
  225.8 1.5 convolution_convert_fusion.9
  227.3 10.3 %all-gather = bf16[512,256]{1,0:T(8,128)(2,1)S(1)} all-gather(bf16[128,256]{1,0:T(8,128)(2,1)S(1)} %convolution_convert_fusion.9), channel_id=2, replica_groups=mesh['pipe'=4,'tensor'=32,'dp'=4] {'dp'}, dimensions={0}, use_global_device_ids=true | all-gather | bytes 327680 | tf_op jit(solution)/shard_map/all_gather | solution.py:113
  238.1 1.5 convolution_convert_fusion.5
  239.6 1.2 reshape_reshape.44
  240.9 4.9 all-to-all-start.8
  246.8 11.2 %all-to-all-done.8 = bf16[32,48,128]{2,1,0:T(8,128)(2,1)S(1)} async-done(((bf16[32,48,128]{2,1,0:T(8,128)(2,1)}), bf16[32,48,128]{2,1,0:T(8,128)(2,1)S(1)}, u32[]{:S(2)}, u32[]{:S(2)}) %all-to-all-start.8) | async-done | bytes 393248 | tf_op jit(solution)/shard_map/all_to_all | solution.py:15
  258.0 6.1 %all-to-all-start.11 = ((bf16[4,48,128]{2,1,0:T(8,128)(2,1)}), bf16[4,48,128]{2,1,0:T(8,128)(2,1)S(1)}, u32[]{:S(2)}, u32[]{:S(2)}) async-start(bf16[4,48,128]{2,1,0:T(8,128)(2,1)} %reshape.520), calls=%async_computation.11 | async-start | bytes 98304 | tf_op jit(solution)/shard_map/all_to_all | solution.py:15
  264.4 5.4 %psum.37 = f32[4,1]{0,1:T(1,128)S(1)} all-reduce(f32[4,1]{0,1:T(1,128)S(1)} %bitcast.225), channel_id=1, replica_groups=mesh['pipe'=4,'tensor'=32,'dp'=4] {'dp'}, use_global_device_ids=true, to_apply=%region_11.12 | all-reduce | flops 4 | bytes 32 | tf_op jit(solution)/shard_map/psum | solution.py:98
  271.2 5.5 %all-to-all-start.9 = ((bf16[32,48,128]{2,1,0:T(8,128)(2,1)}), bf16[32,48,128]{2,1,0:T(8,128)(2,1)S(1)}, u32[]{:S(2)}, u32[]{:S(2)}) async-start(bf16[32,48,128]{2,1,0:T(8,128)(2,1)} %broadcast_in_dim.59), calls=%async_computation.9 | async-start | bytes 786432 | tf_op jit(solution)/shard_map/all_to_all | solution.py:15
  277.5 9.5 %all-to-all-done.9 = bf16[32,48,128]{2,1,0:T(8,128)(2,1)S(1)} async-done(((bf16[32,48,128]{2,1,0:T(8,128)(2,1)}), bf16[32,48,128]{2,1,0:T(8,128)(2,1)S(1)}, u32[]{:S(2)}, u32[]{:S(2)}) %all-to-all-start.9) | async-done | bytes 393248 | tf_op jit(solution)/shard_map/all_to_all | solution.py:15
  287.4 1.5 convolution_convert_fusion.8
  289.0 11.0 %all-gather.1 = bf16[512,256]{1,0:T(8,128)(2,1)S(1)} all-gather(bf16[128,256]{1,0:T(8,128)(2,1)S(1)} %convolution_convert_fusion.8), channel_id=3, replica_groups=mesh['pipe'=4,'tensor'=32,'dp'=4] {'dp'}, dimensions={0}, use_global_device_ids=true | all-gather | bytes 327680 | tf_op jit(solution)/shard_map/all_gather | solution.py:113
  300.5 2.3 convolution_convert_fusion.4
  302.9 2.2 reshape_reshape.46
  305.1 4.9 all-to-all-start.10
  310.7 12.1 %all-to-all-done.10 = bf16[32,48,128]{2,1,0:T(8,128)(2,1)} async-done(((bf16[32,48,128]{2,1,0:T(8,128)(2,1)}), bf16[32,48,128]{2,1,0:T(8,128)(2,1)}, u32[]{:S(2)}, u32[]{:S(2)}) %all-to-all-start.10) | async-done | bytes 393248 | tf_op jit(solution)/shard_map/all_to_all | solution.py:15
  322.8 1.1 convert_reduce_fusion.2
  324.1 7.8 %psum.38 = f32[4,1]{0,1:T(1,128)S(1)} all-reduce(f32[4,1]{0,1:T(1,128)S(1)} %bitcast.226), channel_id=1, replica_groups=mesh['pipe'=4,'tensor'=32,'dp'=4] {'dp'}, use_global_device_ids=true, to_apply=%region_16.17 | all-reduce | flops 4 | bytes 32 | tf_op jit(solution)/shard_map/psum | solution.py:98
  332.2 30.0 %all-gather.11.cloned.1.call-done = bf16[512,1536]{1,0:T(8,128)(2,1)} async-done(((bf16[16,1536]{1,0:T(8,128)(2,1)}), bf16[512,1536]{1,0:T(8,128)(2,1)}) %all-gather.11.cloned.1.call-update) | async-done | bytes 1572880 | tf_op jit(solution)/shard_map/all_gather | solution.py:93
  362.3 14.9 %all_to_all.87 = bf16[32,48,128]{2,1,0:T(8,128)(2,1)S(1)} all-to-all(bf16[32,48,128]{2,1,0:T(8,128)(2,1)S(1)} %broadcast_in_dim.62), channel_id=1, replica_groups=mesh['pipe'=4,'tensor'=32,'dp'=4] {'tensor'}, dimensions={0} | all-to-all | bytes 786432 | tf_op jit(solution)/shard_map/all_to_all | solution.py:15
  377.2 1.2 reshape_reshape.47
  378.4 1.6 convolution_convert_fusion.7
  380.1 12.2 %all-gather.2 = bf16[512,256]{1,0:T(8,128)(2,1)S(1)} all-gather(bf16[128,256]{1,0:T(8,128)(2,1)S(1)} %convolution_convert_fusion.7), channel_id=4, replica_groups=mesh['pipe'=4,'tensor'=32,'dp'=4] {'dp'}, dimensions={0}, use_global_device_ids=true | all-gather | bytes 327680 | tf_op jit(solution)/shard_map/all_gather | solution.py:113
  392.8 1.5 convolution_convert_fusion.3
  394.3 1.2 reshape_reshape.48
  395.5 5.2 %all-to-all-start.13 = ((bf16[32,48,128]{2,1,0:T(8,128)(2,1)}), bf16[32,48,128]{2,1,0:T(8,128)(2,1)S(1)}, u32[]{:S(2)}, u32[]{:S(2)}) async-start(bf16[32,48,128]{2,1,0:T(8,128)(2,1)} %reshape_reshape.48), calls=%async_computation.13 | async-start | bytes 786432 | tf_op jit(solution)/shard_map/all_to_all | solution.py:15
  402.7 1.5 subtract_convert_fusion
  404.2 1.5 maximum_maximum_fusion.1
  405.8 7.1 %all-to-all-done.13 = bf16[32,48,128]{2,1,0:T(8,128)(2,1)S(1)} async-done(((bf16[32,48,128]{2,1,0:T(8,128)(2,1)}), bf16[32,48,128]{2,1,0:T(8,128)(2,1)S(1)}, u32[]{:S(2)}, u32[]{:S(2)}) %all-to-all-start.13) | async-done | bytes 393248 | tf_op jit(solution)/shard_map/all_to_all | solution.py:15
  412.9 6.5 %all-to-all-start.15 = ((bf16[4,256,128]{2,1,0:T(8,128)(2,1)}), bf16[4,256,128]{2,1,0:T(8,128)(2,1)S(1)}, u32[]{:S(2)}, u32[]{:S(2)}) async-start(bf16[4,256,128]{2,1,0:T(8,128)(2,1)} %maximum_maximum_fusion.1), calls=%async_computation.15 | async-start | bytes 524288 | tf_op jit(solution)/shard_map/all_to_all | solution.py:15
  419.7 8.2 %psum.39 = f32[4,1]{0,1:T(1,128)S(1)} all-reduce(f32[4,1]{0,1:T(1,128)S(1)} %bitcast.224), channel_id=1, replica_groups=mesh['pipe'=4,'tensor'=32,'dp'=4] {'dp'}, use_global_device_ids=true, to_apply=%region_22.23 | all-reduce | flops 4 | bytes 32 | tf_op jit(solution)/shard_map/psum | solution.py:98
  430.4 8.7 %all-to-all-start.14 = ((bf16[16,12,128]{2,1,0:T(8,128)(2,1)}), bf16[16,12,128]{2,1,0:T(8,128)(2,1)S(1)}, u32[]{:S(2)}, u32[]{:S(2)}) async-start(bf16[16,12,128]{2,1,0:T(8,128)(2,1)} %reshape_reshape.49), calls=%async_computation.14 | async-start | bytes 131072 | tf_op jit(solution)/shard_map/all_to_all | solution.py:15
  439.0 1.4 maximum_maximum_fusion
  440.4 6.4 %all-to-all-done.14 = bf16[16,12,128]{2,1,0:T(8,128)(2,1)S(1)} async-done(((bf16[16,12,128]{2,1,0:T(8,128)(2,1)}), bf16[16,12,128]{2,1,0:T(8,128)(2,1)S(1)}, u32[]{:S(2)}, u32[]{:S(2)}) %all-to-all-start.14) | async-done | bytes 49184 | tf_op jit(solution)/shard_map/all_to_all | solution.py:15
  447.4 3.6 all-to-all-start.16
  451.0 33.1 %all_gather.49 = bf16[4,128,256]{2,1,0:T(8,128)(2,1)S(1)} all-gather(bf16[1,128,256]{2,1,0:T(8,128)(2,1)S(1)} %copy-done.6), channel_id=1, replica_groups=mesh['pipe'=4,'tensor'=32,'dp'=4] {'dp'}, dimensions={0}, use_global_device_ids=true | all-gather | bytes 327680 | tf_op jit(solution)/shard_map/all_gather | solution.py:75
  486.2 1.8 reshape_reshape.51
  488.0 1.7 copy.63
  489.7 1.7 reshape.523
  491.5 3.0 fusion
  495.1 1.3 broadcast_select_fusion
  496.4 3.3 select_n.40
  499.7 1.5 fusion.1
  (171 shorter events, 27.5 us)
Async XLA Ops:
  22.0 44.4 %all-to-all-start.2 = ((bf16[32,192,128]{2,1,0:T(8,128)(2,1)}), bf16[32,192,128]{2,1,0:T(8,128)(2,1)S(1)}, u32[]{:S(2)}, u32[]{:S(2)}) async-start(bf16[32,192,128]{2,1,0:T(8,128)(2,1)} %broadcast_in_dim.53), calls=%async_computation.2 | async-start | bytes 3145728 | tf_op jit(solution)/shard_map/all_to_all | solution.py:15
  29.8 195.9 %all-gather.7.cloned.1.call-start = ((), (), s32[]{:S(2)}) async-start(), calls=%async_computation.17 | async-start | bytes 3932160 | tf_op jit(solution)/shard_map/all_gather | solution.py:53
  70.7 29.5 %copy-start.7 = (bf16[1,1,1,128,256]{4,3,2,1,0:T(8,128)(2,1)S(1)}, bf16[1,1,1,128,256]{4,3,2,1,0:T(8,128)(2,1)}, u32[]{:S(2)}) copy-start(bf16[1,1,1,128,256]{4,3,2,1,0:T(8,128)(2,1)} %param.6) | copy-start | bytes 196612
  109.3 4.6 copy-start.2
  113.8 8.8 %copy-start.4 = (bf16[1,1,1,4,6144]{4,3,2,1,0:T(4,128)(2,1)S(1)}, bf16[1,1,1,4,6144]{4,3,2,1,0:T(4,128)(2,1)}, u32[]{:S(2)}) copy-start(bf16[1,1,1,4,6144]{4,3,2,1,0:T(4,128)(2,1)} %param.5) | copy-start | bytes 147460
  113.8 43.7 %all-to-all-start.4 = ((bf16[32,192,128]{2,1,0:T(8,128)(2,1)}), bf16[32,192,128]{2,1,0:T(8,128)(2,1)S(1)}, u32[]{:S(2)}, u32[]{:S(2)}) async-start(bf16[32,192,128]{2,1,0:T(8,128)(2,1)} %reshape_reshape.41), calls=%async_computation.4 | async-start | bytes 3145728 | tf_op jit(solution)/shard_map/all_to_all | solution.py:15
  121.0 117.1 %all-gather.9.cloned.1.call-start = ((), (), s32[]{:S(2)}) async-start(), calls=%async_computation.18 | async-start | bytes 3932160 | tf_op jit(solution)/shard_map/all_gather | solution.py:54
  157.5 22.0 %all-to-all-start.1 = ((bf16[16,12,128]{2,1,0:T(8,128)(2,1)}), bf16[16,12,128]{2,1,0:T(8,128)(2,1)S(1)}, u32[]{:S(2)}, u32[]{:S(2)}) async-start(bf16[16,12,128]{2,1,0:T(8,128)(2,1)} %reshape_reshape_squeeze.3), calls=%async_computation.1 | async-start | bytes 131072 | tf_op jit(solution)/shard_map/all_to_all | solution.py:15
  179.5 27.0 %copy-start = (bf16[16,12,128]{2,1,0:T(8,128)(2,1)}, bf16[16,12,128]{2,1,0:T(8,128)(2,1)S(1)}, u32[]{:S(2)}) copy-start(bf16[16,12,128]{2,1,0:T(8,128)(2,1)S(1)} %all-to-all-done.1) | copy-start | bytes 147460
  179.5 14.7 %all-to-all-start.5 = ((f32[4,48,128]{2,1,0:T(8,128)}), f32[4,48,128]{2,1,0:T(8,128)S(1)}, u32[]{:S(2)}, u32[]{:S(2)}) async-start(f32[4,48,128]{2,1,0:T(8,128)} %bitcast.11), calls=%async_computation.5 | async-start | bytes 196608 | tf_op jit(solution)/shard_map/all_to_all | solution.py:15
  194.2 11.5 %all-to-all-start.7 = ((bf16[4,64,128]{2,1,0:T(8,128)(2,1)}), bf16[4,64,128]{2,1,0:T(8,128)(2,1)S(1)}, u32[]{:S(2)}, u32[]{:S(2)}) async-start(bf16[4,64,128]{2,1,0:T(8,128)(2,1)} %reshape.519), calls=%async_computation.7 | async-start | bytes 131072 | tf_op jit(solution)/shard_map/all_to_all | solution.py:15
  203.8 1.8 copy-start.26
  204.3 1.3 copy-start.20
  204.3 65.5 %copy-start.18 = (f32[4]{0:T(128)}, f32[4]{0:T(128)S(1)}, u32[]{:S(2)}) copy-start(f32[4]{0:T(128)S(1)} %get-tuple-element.40) | copy-start | bytes 52
  204.3 127.7 %copy-start.16 = (f32[4]{0:T(128)}, f32[4]{0:T(128)S(1)}, u32[]{:S(2)}) copy-start(f32[4]{0:T(128)S(1)} %get-tuple-element.39) | copy-start | bytes 52
  204.9 0.8 copy-start.24
  204.9 65.0 %copy-start.22 = (f32[4]{0:T(128)}, f32[4]{0:T(128)S(1)}, u32[]{:S(2)}) copy-start(f32[4]{0:T(128)S(1)} %get-tuple-element.36) | copy-start | bytes 52
  205.7 64.2 %copy-start.10 = (bf16[1,4,1536]{2,0,1:T(2,128)(2,1)}, bf16[1,4,1536]{2,0,1:T(2,128)(2,1)S(1)}, u32[]{:S(2)}) copy-start(bf16[1,4,1536]{2,0,1:T(2,128)(2,1)S(1)} %get-tuple-element.20) | copy-start | bytes 36868
  206.5 18.8 %all-to-all-start.6 = ((bf16[32,48,128]{2,1,0:T(8,128)(2,1)}), bf16[32,48,128]{2,1,0:T(8,128)(2,1)S(1)}, u32[]{:S(2)}, u32[]{:S(2)}) async-start(bf16[32,48,128]{2,1,0:T(8,128)(2,1)} %broadcast_in_dim.56), calls=%async_computation.6 | async-start | bytes 786432 | tf_op jit(solution)/shard_map/all_to_all | solution.py:15
  237.6 8.2 %copy-start.5 = (bf16[1,1,1,4,6144]{4,3,2,1,0:T(4,128)(2,1)S(1)}, bf16[1,1,1,4,6144]{4,3,2,1,0:T(4,128)(2,1)}, u32[]{:S(2)}) copy-start(bf16[1,1,1,4,6144]{4,3,2,1,0:T(4,128)(2,1)} %param.5) | copy-start | bytes 147460
  240.9 17.1 %all-to-all-start.8 = ((bf16[32,48,128]{2,1,0:T(8,128)(2,1)}), bf16[32,48,128]{2,1,0:T(8,128)(2,1)S(1)}, u32[]{:S(2)}, u32[]{:S(2)}) async-start(bf16[32,48,128]{2,1,0:T(8,128)(2,1)} %reshape_reshape.44), calls=%async_computation.8 | async-start | bytes 786432 | tf_op jit(solution)/shard_map/all_to_all | solution.py:15
  258.0 12.5 %all-to-all-start.11 = ((bf16[4,48,128]{2,1,0:T(8,128)(2,1)}), bf16[4,48,128]{2,1,0:T(8,128)(2,1)S(1)}, u32[]{:S(2)}, u32[]{:S(2)}) async-start(bf16[4,48,128]{2,1,0:T(8,128)(2,1)} %reshape.520), calls=%async_computation.11 | async-start | bytes 98304 | tf_op jit(solution)/shard_map/all_to_all | solution.py:15
  269.9 0.5 copy-start.28
  271.2 15.8 %all-to-all-start.9 = ((bf16[32,48,128]{2,1,0:T(8,128)(2,1)}), bf16[32,48,128]{2,1,0:T(8,128)(2,1)S(1)}, u32[]{:S(2)}, u32[]{:S(2)}) async-start(bf16[32,48,128]{2,1,0:T(8,128)(2,1)} %broadcast_in_dim.59), calls=%async_computation.9 | async-start | bytes 786432 | tf_op jit(solution)/shard_map/all_to_all | solution.py:15
  276.7 85.5 %all-gather.11.cloned.1.call-start = ((), (), s32[]{:S(2)}) async-start(), calls=%async_computation.19 | async-start | bytes 1622016 | tf_op jit(solution)/shard_map/all_gather | solution.py:93
  300.0 9.9 %copy-start.1 = (bf16[16,12,128]{2,1,0:T(8,128)(2,1)S(1)}, bf16[16,12,128]{2,1,0:T(8,128)(2,1)}, u32[]{:S(2)}) copy-start(bf16[16,12,128]{2,1,0:T(8,128)(2,1)} %copy-done) | copy-start | bytes 147460
  302.8 29.2 %copy-start.15 = (f32[4,1,1536]{2,1,0:T(1,128)S(1)}, f32[4,1,1536]{2,1,0:T(1,128)}, u32[]{:S(2)}) copy-start(f32[4,1,1536]{2,1,0:T(1,128)} %get-tuple-element.21) | copy-start | bytes 73732
  302.8 29.2 %copy-start.17 = (f32[4]{0:T(128)S(1)}, f32[4]{0:T(128)}, u32[]{:S(2)}) copy-start(f32[4]{0:T(128)} %get-tuple-element.35) | copy-start | bytes 52
  302.8 29.2 %copy-start.19 = (f32[4]{0:T(128)S(1)}, f32[4]{0:T(128)}, u32[]{:S(2)}) copy-start(f32[4]{0:T(128)} %copy-done.18) | copy-start | bytes 52
  302.8 29.2 %copy-start.21 = (f32[4]{0:T(128)S(1)}, f32[4]{0:T(128)}, u32[]{:S(2)}) copy-start(f32[4]{0:T(128)} %copy-done.20) | copy-start | bytes 52
  302.8 29.2 %copy-start.23 = (f32[4]{0:T(128)S(1)}, f32[4]{0:T(128)}, u32[]{:S(2)}) copy-start(f32[4]{0:T(128)} %copy-done.22) | copy-start | bytes 52
  302.8 29.2 %copy-start.25 = (f32[4]{0:T(128)S(1)}, f32[4]{0:T(128)}, u32[]{:S(2)}) copy-start(f32[4]{0:T(128)} %copy-done.24) | copy-start | bytes 52
  302.8 29.2 %copy-start.27 = (f32[4]{0:T(128)S(1)}, f32[4]{0:T(128)}, u32[]{:S(2)}) copy-start(f32[4]{0:T(128)} %copy-done.26) | copy-start | bytes 52
  302.8 29.2 %copy-start.29 = (f32[4]{0:T(128)S(1)}, f32[4]{0:T(128)}, u32[]{:S(2)}) copy-start(f32[4]{0:T(128)} %copy-done.28) | copy-start | bytes 52
  305.1 17.7 %all-to-all-start.10 = ((bf16[32,48,128]{2,1,0:T(8,128)(2,1)}), bf16[32,48,128]{2,1,0:T(8,128)(2,1)}, u32[]{:S(2)}, u32[]{:S(2)}) async-start(bf16[32,48,128]{2,1,0:T(8,128)(2,1)} %reshape_reshape.46), calls=%async_computation.10 | async-start | bytes 786432 | tf_op jit(solution)/shard_map/all_to_all | solution.py:15
  332.0 48.1 %copy-start.30 = (f32[4]{0:T(128)}, f32[4]{0:T(128)S(1)}, u32[]{:S(2)}) copy-start(f32[4]{0:T(128)S(1)} %multiply_bitcast_fusion.1) | copy-start | bytes 52
  332.2 47.9 %copy-start.12 = (bf16[4,1536]{1,0:T(4,128)(2,1)}, bf16[4,1536]{1,0:T(4,128)(2,1)S(1)}, u32[]{:S(2)}) copy-start(bf16[4,1536]{1,0:T(4,128)(2,1)S(1)} %fusion.34) | copy-start | bytes 36868
  392.8 9.3 %copy-start.11 = (f32[4,12,128]{2,1,0:T(8,128)S(1)}, f32[4,12,128]{2,1,0:T(8,128)}, u32[]{:S(2)}) copy-start(f32[4,12,128]{2,1,0:T(8,128)} %get-tuple-element.30) | copy-start | bytes 73732
  395.5 17.4 %all-to-all-start.13 = ((bf16[32,48,128]{2,1,0:T(8,128)(2,1)}), bf16[32,48,128]{2,1,0:T(8,128)(2,1)S(1)}, u32[]{:S(2)}, u32[]{:S(2)}) async-start(bf16[32,48,128]{2,1,0:T(8,128)(2,1)} %reshape_reshape.48), calls=%async_computation.13 | async-start | bytes 786432 | tf_op jit(solution)/shard_map/all_to_all | solution.py:15
  402.7 16.7 %copy-start.14 = (f32[48,128]{1,0:T(8,128)S(1)}, f32[48,128]{1,0:T(8,128)}, u32[]{:S(2)}) copy-start(f32[48,128]{1,0:T(8,128)} %squeeze.77) | copy-start | bytes 73732
  404.2 24.6 %copy-start.13 = (bf16[1,4,1536]{2,0,1:T(2,128)(2,1)S(1)}, bf16[1,4,1536]{2,0,1:T(2,128)(2,1)}, u32[]{:S(2)}) copy-start(bf16[1,4,1536]{2,0,1:T(2,128)(2,1)} %subtract_convert_fusion) | copy-start | bytes 36868
  404.2 34.8 %copy-start.31 = (bf16[4]{0:T(256)(128)(2,1)S(1)}, bf16[4]{0:T(256)(128)(2,1)}, u32[]{:S(2)}) copy-start(bf16[4]{0:T(256)(128)(2,1)} %pad.7.clone) | copy-start | bytes 28
  412.9 17.5 %all-to-all-start.15 = ((bf16[4,256,128]{2,1,0:T(8,128)(2,1)}), bf16[4,256,128]{2,1,0:T(8,128)(2,1)S(1)}, u32[]{:S(2)}, u32[]{:S(2)}) async-start(bf16[4,256,128]{2,1,0:T(8,128)(2,1)} %maximum_maximum_fusion.1), calls=%async_computation.15 | async-start | bytes 524288 | tf_op jit(solution)/shard_map/all_to_all | solution.py:15
  430.4 16.5 %copy-start.3 = (bf16[4,256,128]{2,1,0:T(8,128)(2,1)}, bf16[4,256,128]{2,1,0:T(8,128)(2,1)S(1)}, u32[]{:S(2)}) copy-start(bf16[4,256,128]{2,1,0:T(8,128)(2,1)S(1)} %all-to-all-done.15) | copy-start | bytes 786436
  430.4 16.5 %all-to-all-start.14 = ((bf16[16,12,128]{2,1,0:T(8,128)(2,1)}), bf16[16,12,128]{2,1,0:T(8,128)(2,1)S(1)}, u32[]{:S(2)}, u32[]{:S(2)}) async-start(bf16[16,12,128]{2,1,0:T(8,128)(2,1)} %reshape_reshape.49), calls=%async_computation.14 | async-start | bytes 131072 | tf_op jit(solution)/shard_map/all_to_all | solution.py:15
  440.4 10.6 %copy-start.6 = (bf16[1,128,256]{2,1,0:T(8,128)(2,1)S(1)}, bf16[1,128,256]{2,1,0:T(8,128)(2,1)}, u32[]{:S(2)}) copy-start(bf16[1,128,256]{2,1,0:T(8,128)(2,1)} %get-tuple-element.28) | copy-start | bytes 196612
  446.8 0.6 copy-start.8
  447.4 47.6 %all-to-all-start.16 = ((bf16[4,1536,128]{2,1,0:T(8,128)(2,1)}), bf16[4,1536,128]{2,1,0:T(8,128)(2,1)S(1)}, u32[]{:S(2)}, u32[]{:S(2)}) async-start(bf16[4,1536,128]{2,1,0:T(8,128)(2,1)} %maximum_maximum_fusion), calls=%async_computation.16 | async-start | bytes 3145728 | tf_op jit(solution)/shard_map/all_to_all | solution.py:15
  491.5 3.0 copy-start.9
Sparse Core Ops, SparseCore 0:
  32.8 76.4 all-gather.6
  124.0 76.2 all-gather.8
  281.3 80.8 all-gather.10

commit v3 on v1

v3 whole, which is shorter than its diff:
```python
import jax
import jax.numpy as jnp
from jax import lax
from jax.sharding import PartitionSpec as P

epsilon = 1e-06
f32 = jnp.float32
bf16 = jnp.bfloat16
LANES = 128


def exchange(blocks, axis, count):
    flat = blocks.reshape(count, -1, LANES)
    return lax.all_to_all(flat, axis, 0, 0).reshape(blocks.shape)


def after(value, *others):
    return lax.optimization_barrier((value,) + others)[0]


def shifted(value, steps):
    count = lax.axis_size("pipe")
    return lax.ppermute(value, "pipe", [(i, (i + steps) % count) for i in range(count)])


def choose(index, options):
    result = options[-1]
    for k in reversed(range(len(options) - 1)):
        result = jnp.where(index == k, options[k], result)
    return result


def slope_of(u):
    sigmoid_u = jax.nn.sigmoid(u)
    return sigmoid_u * (1.0 + u * (1.0 - sigmoid_u))


def dot_nt(left, right):
    product = lax.dot_general(left, right, (((1,), (1,)), ((), ())), preferred_element_type=f32)
    return product.astype(bf16)


def dot_tn(left, right):
    product = lax.dot_general(left, right, (((0,), (0,)), ((), ())), preferred_element_type=f32)
    return product.astype(bf16)


def per_device(section_input, pre_act, cotangent, w_up, w_down):
    pipe = lax.axis_size("pipe")
    parts = lax.axis_size("tensor")
    groups = lax.axis_size("dp")
    pipe_index = lax.axis_index("pipe")
    own_rows, width = section_input.shape[-2:]
    block = width // groups
    rows, hidden_width = pre_act.shape[-2:]
    tokens = parts * groups

    x_own = section_input[0, 0, 0]
    u_own = pre_act[0, 0, 0]
    x_own_f = x_own.astype(f32)
    inverse_own = lax.rsqrt(jnp.mean(x_own_f * x_own_f, axis=-1, keepdims=True) + epsilon)
    normed_own = (x_own_f * inverse_own).astype(bf16)

    down_own, up_own = w_down[0], w_up[0]
    down_prev, up_next = shifted(down_own, 1), shifted(up_own, -1)
    down_next, up_prev = shifted(down_own, -1), shifted(up_own, 1)
    down_all = (down_own, down_next, shifted(down_prev, 1), down_prev)
    up_all = (up_own, up_next, shifted(up_next, -1), up_prev)

    inverse_high = inverse_own.astype(bf16)
    inverse_low = (inverse_own - inverse_high.astype(f32)).astype(bf16)
    lanes = jnp.concatenate(
        [inverse_high, inverse_low, jnp.zeros((own_rows, LANES - 2), bf16)], axis=-1
    )
    lanes = jnp.broadcast_to(lanes[:, None, None], (own_rows, groups, 1, LANES))
    u_spread = jnp.swapaxes(u_own.reshape(parts, pipe, hidden_width), 0, 1)
    u_spread = jnp.broadcast_to(
        u_spread.reshape(pipe, 1, -1, LANES), (pipe, groups, parts * hidden_width // LANES, LANES)
    )
    lines = block // LANES
    mixed = [
        x_own.reshape(own_rows, groups, lines, LANES),
        cotangent[0, 0].reshape(own_rows, groups, lines, LANES),
        u_spread,
        lanes,
    ]
    mixed = after(jnp.concatenate(mixed, 2), down_prev, up_next)
    mixed = exchange(mixed, ("pipe", "dp"), pipe * groups)
    mixed = mixed.reshape(pipe, groups, -1, LANES)
    x_blocks = mixed[:, :, :lines].reshape(pipe, groups, block).astype(f32)
    grad = mixed[0, :, lines : 2 * lines].reshape(groups, block)
    u_rows = jnp.swapaxes(mixed[:, :, 2 * lines : -1].reshape(pipe, groups, parts, hidden_width), 1, 2)
    slope = slope_of(u_rows.reshape(pipe, tokens, hidden_width).astype(f32))
    inverse = mixed[:, :, -1, :1].astype(f32) + mixed[:, :, -1, 1:2].astype(f32)

    normed_blocks = jnp.swapaxes(normed_own.reshape(own_rows, groups, block), 0, 1)
    normed_blocks = jnp.swapaxes(exchange(normed_blocks, "dp", groups), 0, 1).reshape(-1, block)
    normed_all = lax.all_gather(normed_blocks, "tensor", axis=0, tiled=True)

    u_f = u_own.astype(f32)
    hidden = lax.all_gather((u_f * jax.nn.sigmoid(u_f)).astype(bf16), "dp", axis=0)
    hidden = jnp.transpose(hidden.reshape(groups, parts, pipe, hidden_width), (2, 1, 0, 3))
    hidden = hidden.reshape(pipe, tokens, hidden_width)
    hidden = jnp.concatenate(
        [choose(pipe_index, [hidden[(p - k) % pipe] for p in range(pipe)]) for k in range(pipe)], 0
    )

    stores, out_store = [None] * pipe, [None] * pipe
    for section in reversed(range(pipe)):
        place = jnp.remainder(section - pipe_index, pipe)
        if section == 1:
            grad = after(grad, hidden)
        spread = jnp.broadcast_to(grad[None], (parts,) + grad.shape)
        grad_rows = exchange(spread, "tensor", parts).reshape(tokens, block)
        partials = lax.all_gather(dot_nt(grad_rows, choose(place, down_all)), "dp", axis=0)
        hidden_grad = jnp.sum(partials.astype(f32), axis=0)
        pre_grad = (hidden_grad * slope[section]).astype(bf16)
        stores[section] = jnp.concatenate([grad_rows, pre_grad], -1)
        pieces = dot_nt(pre_grad, choose(place, up_all)).reshape(parts, groups, block)
        pieces = exchange(pieces, "tensor", parts)
        if section == pipe - 1:
            pieces = after(pieces, normed_all)
        normed_grad = jnp.sum(pieces.astype(f32), axis=0)
        if section == 0:
            out_store[0] = normed_grad.astype(bf16)
            break
        x_s, inv = x_blocks[section], inverse[section]
        mean_term = lax.psum(jnp.sum(normed_grad * x_s, axis=-1, keepdims=True), "dp") / width
        grad_f = grad.astype(f32) + inv * normed_grad - x_s * inv**3 * mean_term
        grad = grad_f.astype(bf16)
        out_store[section] = grad

    outs = jnp.stack([jnp.stack(out_store), jnp.broadcast_to(grad, (pipe,) + grad.shape)], 2)
    outs = exchange(outs, ("pipe", "dp"), pipe * groups)
    outs = outs.reshape(own_rows, groups, 2, block)
    whole = outs[:, :, 0].reshape(own_rows, width)
    normed_grad = whole.astype(f32)
    above = outs[:, :, 1].reshape(own_rows, width).astype(f32)
    mean_term = jnp.mean(normed_grad * x_own_f, axis=-1, keepdims=True)
    grad_f = above + inverse_own * normed_grad - x_own_f * inverse_own**3 * mean_term
    input_grad = jnp.where(pipe_index == 0, grad_f.astype(bf16), whole)
    input_grad = input_grad.reshape(1, 1, 1, own_rows, width)

    moved = [choose(pipe_index, stores)]
    for k in range(1, pipe):
        chosen = choose(pipe_index, [stores[(p + k) % pipe] for p in range(pipe)])
        moved.append(shifted(chosen, k))
    moved = lax.optimization_barrier((moved, outs))[0]
    grads = jnp.concatenate([piece[:, :block] for piece in moved], 0)
    down_grad = dot_tn(hidden, grads)
    pres = [piece[:, block:] for piece in moved]
    pres = [choose(pipe_index, [pres[(p - i) % pipe] for p in range(pipe)]) for i in range(pipe)]
    pres = jnp.stack([piece.reshape(parts, groups, hidden_width) for piece in pres], 1)
    up_grad = dot_tn(normed_all, pres.reshape(-1, hidden_width))
    return (input_grad, up_grad[None], down_grad[None])


def solution(mesh):
    return jax.shard_map(
        per_device,
        mesh=mesh,
        in_specs=(
            P("pipe", None, "dp", "tensor", None),
            P("pipe", None, "dp", None, "tensor"),
            P(None, "dp", "tensor", None),
            P("pipe", "dp", "tensor"),
            P("pipe", "tensor", "dp"),
        ),
        out_specs=(
            P("pipe", None, "dp", "tensor", None),
            P("pipe", "dp", "tensor"),
            P("pipe", "tensor", "dp"),
        ),
        check_vma=False,
    )
```

time: 452 us -> 401 us (0.89)
  blocking collectives: 155 us -> 92.8 us
  starting transfers between devices: 81.8 us -> 113 us
  waiting for transfers between devices: 157 us -> 128 us
  local copies, waits for them, and re-layouts: 16.4 us -> 21.3 us
    all_gather x3 -> x1, waiting for transfers between devices: 83.8 us -> 0.02 us  [per_device(): normed_all = lax.all_gather(normed_blocks, 'tensor', axis=0, tiled=True)]
    ppermute x0 -> x9, starting transfers between devices: none -> 36.7 us  [shifted(): lax.ppermute(value, 'pipe', [(i, (i + steps) % count) for i in range(coun...]
    all_to_all x2 -> x0, blocking collectives: 30.8 us -> none  [exchange(): return lax.all_to_all(flat, axis, 0, 0).reshape(shape)]
    ppermute x0 -> x9, waiting for transfers between devices: none -> 28.1 us  [shifted(): lax.ppermute(value, 'pipe', [(i, (i + steps) % count) for i in range(coun...]
    all_to_all x13 -> x11, waiting for transfers between devices: 71.4 us -> 99.4 us  [exchange(): return lax.all_to_all(flat, axis, 0, 0).reshape(blocks.shape)]
    all_gather x6 -> x5, blocking collectives: 87.9 us -> 68.6 us  [the longest x4 61.3 us: per_device(): lax.all_gather(dot_nt(grad_rows, choose(place, down_all)), 'dp', axis=0)]
    psum x4 -> x3, blocking collectives: 36.2 us -> 24.3 us  [per_device(): lax.psum(jnp.sum(normed_grad * x_s, axis=-1, keepdims=True), 'dp') / width]
    all_to_all x13 -> x11, starting transfers between devices: 81.7 us -> 76.4 us  [exchange(): return lax.all_to_all(flat, axis, 0, 0).reshape(blocks.shape)]
  transfers between devices with their start and end apart: 16 -> 21, of which waited for: 11 -> 12; matrix products, arithmetic and copies ran while one was open for 5% -> 5% of each run, Pallas kernels for 0% -> 0%
where the time goes in v3:
time: 401 us; the launch traced here: 398 us
  waiting for transfers between devices  128 us (32%)
  starting transfers between devices  113 us (28%)
  blocking collectives  92.8 us (23%)
  local copies, waits for them, and re-layouts  21.3 us (5%)
  matrix products  16.8 us (4%)
  between operations  15.1 us (4%)
  other arithmetic  11.1 us (3%)
    all_to_all x11, waiting for transfers between devices, exchange(): return lax.all_to_all(flat, axis, 0, 0).reshape(blocks.shape)  99.4 us
    all_to_all x11, starting transfers between devices, exchange(): return lax.all_to_all(flat, axis, 0, 0).reshape(blocks.shape)  76.4 us
    all_gather x4, blocking collectives, per_device(): lax.all_gather(dot_nt(grad_rows, choose(place, down_all)), 'dp', axis=0)  61.3 us
    ppermute x9, starting transfers between devices, shifted(): lax.ppermute(value, 'pipe', [(i, (i + steps) % count) for i in range(coun...  36.7 us
    ppermute x9, waiting for transfers between devices, shifted(): lax.ppermute(value, 'pipe', [(i, (i + steps) % count) for i in range(coun...  28.1 us
    psum x3, blocking collectives, per_device(): lax.psum(jnp.sum(normed_grad * x_s, axis=-1, keepdims=True), 'dp') / width  24.3 us
    dot_general x8, matrix products, dot_nt(): lax.dot_general(left, right, (((1,), (1,)), ((), ())), preferred_element_...  13.8 us
  transfers between devices with their start and end apart: 21, of which 12 were waited for; matrix products, arithmetic and copies ran while one was open for 5% of the time, Pallas kernels for 0%

profile of v3, /device:TPU:1, one launch (start us, length us, event | category | flops | bytes accessed | tf_op | source)
XLA Modules:
  0.0 397.8 jit_solution(51955686732739460)
XLA Ops:
  7.2 5.0 %collective-permute-start = (bf16[256,1536]{1,0:T(8,128)(2,1)}, bf16[256,1536]{1,0:T(8,128)(2,1)}, u32[]{:S(2)}, u32[]{:S(2)}) collective-permute-start(bf16[256,1536]{1,0:T(8,128)(2,1)} %bitcast.218), channel_id=1, source_target_pairs={{0,128},{128,256},{256,384},{384,0},{1,129},{129,257},{257,385},{3... | collective-permute-start | bytes 2359304 | tf_op jit(solution)/shard_map/ppermute | solution.py:23
  12.2 3.6 collective-permute-start.1
  15.8 1.0 multiply_reduce_fusion.1
  16.8 0.8 convert_element_type.268
  18.4 9.4 %all-to-all-start.3 = ((bf16[4,48,128]{2,1,0:T(8,128)(2,1)}), bf16[4,48,128]{2,1,0:T(8,128)(2,1)S(1)}, u32[]{:S(2)}, u32[]{:S(2)}) async-start(bf16[4,48,128]{2,1,0:T(8,128)(2,1)} %reshape.493), calls=%async_computation.3 | async-start | bytes 98304 | tf_op jit(solution)/shard_map/all_to_all | solution.py:14
  27.8 0.9 reshape_squeeze.14
  28.9 0.9 reshape_squeeze.16
  29.8 0.9 reshape_squeeze.15
  31.7 4.8 %collective-permute-done = bf16[256,1536]{1,0:T(8,128)(2,1)} collective-permute-done((bf16[256,1536]{1,0:T(8,128)(2,1)}, bf16[256,1536]{1,0:T(8,128)(2,1)}, u32[]{:S(2)}, u32[]{:S(2)}) %collective-permute-start) | collective-permute-done | bytes 786464 | tf_op jit(solution)/shard_map/ppermute | solution.py:23
  36.5 16.1 %collective-permute-done.1 = bf16[1536,256]{1,0:T(8,128)(2,1)S(1)} collective-permute-done((bf16[1536,256]{1,0:T(8,128)(2,1)}, bf16[1536,256]{1,0:T(8,128)(2,1)S(1)}, u32[]{:S(2)}, u32[]{:S(2)}) %collective-permute-start.1) | collective-permute-done | bytes 786464 | tf_op jit(solution)/shard_map/ppermute | solution.py:23
  52.6 6.2 %all-to-all-start = ((bf16[16,89,128]{2,1,0:T(8,128)(2,1)}), bf16[16,89,128]{2,1,0:T(8,128)(2,1)S(1)}, u32[]{:S(2)}, u32[]{:S(2)}) async-start(bf16[16,89,128]{2,1,0:T(8,128)(2,1)} %bitcast.4), calls=%async_computation | async-start | bytes 786432 | tf_op jit(solution)/shard_map/all_to_all | solution.py:14
  59.5 5.4 %collective-permute-start.2 = (bf16[256,1536]{1,0:T(8,128)(2,1)S(1)}, bf16[256,1536]{1,0:T(8,128)(2,1)}, u32[]{:S(2)}, u32[]{:S(2)}) collective-permute-start(bf16[256,1536]{1,0:T(8,128)(2,1)S(1)} %bitcast.219), channel_id=1, source_target_pairs={{0,384},{128,0},{256,128},{384,256},{1,385},{129,1},{257,129},{385... | collective-permute-start | bytes 2359304 | tf_op jit(solution)/shard_map/ppermute | solution.py:23
  65.0 1.9 collective-permute-start.3
  66.9 6.0 %all-to-all-done = bf16[16,89,128]{2,1,0:T(8,128)(2,1)S(1)} async-done(((bf16[16,89,128]{2,1,0:T(8,128)(2,1)}), bf16[16,89,128]{2,1,0:T(8,128)(2,1)S(1)}, u32[]{:S(2)}, u32[]{:S(2)}) %all-to-all-start) | async-done | bytes 364576 | tf_op jit(solution)/shard_map/all_to_all | solution.py:14
  73.9 12.9 %all-to-all-start.1 = ((bf16[32,48,128]{2,1,0:T(8,128)(2,1)}), bf16[32,48,128]{2,1,0:T(8,128)(2,1)S(1)}, u32[]{:S(2)}, u32[]{:S(2)}) async-start(bf16[32,48,128]{2,1,0:T(8,128)(2,1)} %broadcast_in_dim.71), calls=%async_computation.1 | async-start | bytes 786432 | tf_op jit(solution)/shard_map/all_to_all | solution.py:14
  86.8 2.3 collective-permute-start.5
  89.1 5.1 %collective-permute-start.4 = (bf16[1536,256]{1,0:T(8,128)(2,1)}, bf16[1536,256]{1,0:T(8,128)(2,1)}, u32[]{:S(2)}, u32[]{:S(2)}) collective-permute-start(bf16[1536,256]{1,0:T(8,128)(2,1)} %copy-done.13), channel_id=1, source_target_pairs={{0,384},{128,0},{256,128},{384,256},{1,385},{129,1},{257,129},{385... | collective-permute-start | bytes 2359304 | tf_op jit(solution)/shard_map/ppermute | solution.py:23
  95.7 5.2 %all-to-all-done.1 = bf16[32,48,128]{2,1,0:T(8,128)(2,1)S(1)} async-done(((bf16[32,48,128]{2,1,0:T(8,128)(2,1)}), bf16[32,48,128]{2,1,0:T(8,128)(2,1)S(1)}, u32[]{:S(2)}, u32[]{:S(2)}) %all-to-all-start.1) | async-done | bytes 393248 | tf_op jit(solution)/shard_map/all_to_all | solution.py:14
  101.4 7.3 %collective-permute-done.2 = bf16[256,1536]{1,0:T(8,128)(2,1)} collective-permute-done((bf16[256,1536]{1,0:T(8,128)(2,1)S(1)}, bf16[256,1536]{1,0:T(8,128)(2,1)}, u32[]{:S(2)}, u32[]{:S(2)}) %collective-permute-start.2) | collective-permute-done | bytes 786464 | tf_op jit(solution)/shard_map/ppermute | solution.py:23
  108.6 1.5 convolution_convert_fusion.9
  110.2 29.8 %all-gather = bf16[512,256]{1,0:T(8,128)(2,1)S(1)} all-gather(bf16[128,256]{1,0:T(8,128)(2,1)S(1)} %convolution_convert_fusion.9), channel_id=2, replica_groups=mesh['pipe'=4,'tensor'=32,'dp'=4] {'dp'}, dimensions={0}, use_global_device_ids=true | all-gather | bytes 327680 | tf_op jit(solution)/shard_map/all_gather | solution.py:115
  140.1 1.6 convolution_convert_fusion.5
  141.6 1.2 reshape_reshape.25
  142.9 12.9 %all-to-all-start.2 = ((bf16[32,48,128]{2,1,0:T(8,128)(2,1)}), bf16[32,48,128]{2,1,0:T(8,128)(2,1)S(1)}, u32[]{:S(2)}, u32[]{:S(2)}) async-start(bf16[32,48,128]{2,1,0:T(8,128)(2,1)} %reshape_reshape.25), calls=%async_computation.2 | async-start | bytes 786432 | tf_op jit(solution)/shard_map/all_to_all | solution.py:14
  156.0 11.5 %all-to-all-done.2 = bf16[32,48,128]{2,1,0:T(8,128)(2,1)S(1)} async-done(((bf16[32,48,128]{2,1,0:T(8,128)(2,1)}), bf16[32,48,128]{2,1,0:T(8,128)(2,1)S(1)}, u32[]{:S(2)}, u32[]{:S(2)}) %all-to-all-start.2) | async-done | bytes 393248 | tf_op jit(solution)/shard_map/all_to_all | solution.py:14
  167.9 8.5 %psum.21 = f32[4,1]{0,1:T(1,128)S(1)} all-reduce(f32[4,1]{0,1:T(1,128)S(1)} %bitcast.215), channel_id=1, replica_groups=mesh['pipe'=4,'tensor'=32,'dp'=4] {'dp'}, use_global_device_ids=true, to_apply=%region_4.5 | all-reduce | flops 4 | bytes 32 | tf_op jit(solution)/shard_map/psum | solution.py:128
  177.4 5.1 %all-to-all-start.4 = ((bf16[32,48,128]{2,1,0:T(8,128)(2,1)}), bf16[32,48,128]{2,1,0:T(8,128)(2,1)S(1)}, u32[]{:S(2)}, u32[]{:S(2)}) async-start(bf16[32,48,128]{2,1,0:T(8,128)(2,1)} %broadcast_in_dim.74), calls=%async_computation.4 | async-start | bytes 786432 | tf_op jit(solution)/shard_map/all_to_all | solution.py:14
  182.5 10.6 %all-to-all-done.4 = bf16[32,48,128]{2,1,0:T(8,128)(2,1)S(1)} async-done(((bf16[32,48,128]{2,1,0:T(8,128)(2,1)}), bf16[32,48,128]{2,1,0:T(8,128)(2,1)S(1)}, u32[]{:S(2)}, u32[]{:S(2)}) %all-to-all-start.4) | async-done | bytes 393248 | tf_op jit(solution)/shard_map/all_to_all | solution.py:14
  193.6 1.9 convolution_convert_fusion.8
  195.5 10.5 %all-gather.1 = bf16[512,256]{1,0:T(8,128)(2,1)S(1)} all-gather(bf16[128,256]{1,0:T(8,128)(2,1)S(1)} %convolution_convert_fusion.8), channel_id=3, replica_groups=mesh['pipe'=4,'tensor'=32,'dp'=4] {'dp'}, dimensions={0}, use_global_device_ids=true | all-gather | bytes 327680 | tf_op jit(solution)/shard_map/all_gather | solution.py:115
  206.0 1.6 convolution_convert_fusion.4
  207.6 1.2 reshape_reshape.27
  208.8 4.9 %all-to-all-start.5 = ((bf16[32,48,128]{2,1,0:T(8,128)(2,1)}), bf16[32,48,128]{2,1,0:T(8,128)(2,1)S(1)}, u32[]{:S(2)}, u32[]{:S(2)}) async-start(bf16[32,48,128]{2,1,0:T(8,128)(2,1)} %reshape_reshape.27), calls=%async_computation.5 | async-start | bytes 786432 | tf_op jit(solution)/shard_map/all_to_all | solution.py:14
  213.8 12.1 %all-to-all-done.5 = bf16[32,48,128]{2,1,0:T(8,128)(2,1)S(1)} async-done(((bf16[32,48,128]{2,1,0:T(8,128)(2,1)}), bf16[32,48,128]{2,1,0:T(8,128)(2,1)S(1)}, u32[]{:S(2)}, u32[]{:S(2)}) %all-to-all-start.5) | async-done | bytes 393248 | tf_op jit(solution)/shard_map/all_to_all | solution.py:14
  226.3 7.9 %psum.22 = f32[4,1]{0,1:T(1,128)S(1)} all-reduce(f32[4,1]{0,1:T(1,128)S(1)} %bitcast.217), channel_id=1, replica_groups=mesh['pipe'=4,'tensor'=32,'dp'=4] {'dp'}, use_global_device_ids=true, to_apply=%region_9.10 | all-reduce | flops 4 | bytes 32 | tf_op jit(solution)/shard_map/psum | solution.py:128
  235.0 5.3 %all-to-all-start.6 = ((bf16[32,48,128]{2,1,0:T(8,128)(2,1)}), bf16[32,48,128]{2,1,0:T(8,128)(2,1)S(1)}, u32[]{:S(2)}, u32[]{:S(2)}) async-start(bf16[32,48,128]{2,1,0:T(8,128)(2,1)} %broadcast_in_dim.77), calls=%async_computation.6 | async-start | bytes 786432 | tf_op jit(solution)/shard_map/all_to_all | solution.py:14
  240.4 10.6 %all-to-all-done.6 = bf16[32,48,128]{2,1,0:T(8,128)(2,1)S(1)} async-done(((bf16[32,48,128]{2,1,0:T(8,128)(2,1)}), bf16[32,48,128]{2,1,0:T(8,128)(2,1)S(1)}, u32[]{:S(2)}, u32[]{:S(2)}) %all-to-all-start.6) | async-done | bytes 393248 | tf_op jit(solution)/shard_map/all_to_all | solution.py:14
  251.5 2.1 convolution_convert_fusion.7
  253.6 10.6 %all-gather.2 = bf16[512,256]{1,0:T(8,128)(2,1)S(1)} all-gather(bf16[128,256]{1,0:T(8,128)(2,1)S(1)} %convolution_convert_fusion.7), channel_id=4, replica_groups=mesh['pipe'=4,'tensor'=32,'dp'=4] {'dp'}, dimensions={0}, use_global_device_ids=true | all-gather | bytes 327680 | tf_op jit(solution)/shard_map/all_gather | solution.py:115
  264.3 1.6 convolution_convert_fusion.3
  265.9 1.2 reshape_reshape.29
  267.2 5.0 %all-to-all-start.7 = ((bf16[32,48,128]{2,1,0:T(8,128)(2,1)}), bf16[32,48,128]{2,1,0:T(8,128)(2,1)S(1)}, u32[]{:S(2)}, u32[]{:S(2)}) async-start(bf16[32,48,128]{2,1,0:T(8,128)(2,1)} %reshape_reshape.29), calls=%async_computation.7 | async-start | bytes 786432 | tf_op jit(solution)/shard_map/all_to_all | solution.py:14
  272.2 12.1 %all-to-all-done.7 = bf16[32,48,128]{2,1,0:T(8,128)(2,1)S(1)} async-done(((bf16[32,48,128]{2,1,0:T(8,128)(2,1)}), bf16[32,48,128]{2,1,0:T(8,128)(2,1)S(1)}, u32[]{:S(2)}, u32[]{:S(2)}) %all-to-all-start.7) | async-done | bytes 393248 | tf_op jit(solution)/shard_map/all_to_all | solution.py:14
  284.7 7.9 %psum.23 = f32[4,1]{0,1:T(1,128)S(1)} all-reduce(f32[4,1]{0,1:T(1,128)S(1)} %bitcast.216), channel_id=1, replica_groups=mesh['pipe'=4,'tensor'=32,'dp'=4] {'dp'}, use_global_device_ids=true, to_apply=%region_14.15 | all-reduce | flops 4 | bytes 32 | tf_op jit(solution)/shard_map/psum | solution.py:128
  293.5 5.3 %all-to-all-start.8 = ((bf16[32,48,128]{2,1,0:T(8,128)(2,1)}), bf16[32,48,128]{2,1,0:T(8,128)(2,1)S(1)}, u32[]{:S(2)}, u32[]{:S(2)}) async-start(bf16[32,48,128]{2,1,0:T(8,128)(2,1)} %broadcast_in_dim.80), calls=%async_computation.8 | async-start | bytes 786432 | tf_op jit(solution)/shard_map/all_to_all | solution.py:14
  299.1 7.2 %all_gather.36 = bf16[4,128,256]{2,1,0:T(8,128)(2,1)S(1)} all-gather(bf16[1,128,256]{2,1,0:T(8,128)(2,1)S(1)} %fusion.65), channel_id=1, replica_groups=mesh['pipe'=4,'tensor'=32,'dp'=4] {'dp'}, dimensions={0}, use_global_device_ids=true | all-gather | bytes 327680 | tf_op jit(solution)/shard_map/all_gather | solution.py:101
  308.0 1.5 all-to-all-done.8
  310.0 1.9 convolution_convert_fusion.6
  311.8 10.5 %all-gather.3 = bf16[512,256]{1,0:T(8,128)(2,1)S(1)} all-gather(bf16[128,256]{1,0:T(8,128)(2,1)S(1)} %convolution_convert_fusion.6), channel_id=5, replica_groups=mesh['pipe'=4,'tensor'=32,'dp'=4] {'dp'}, dimensions={0}, use_global_device_ids=true | all-gather | bytes 327680 | tf_op jit(solution)/shard_map/all_gather | solution.py:115
  322.4 1.6 convolution_convert_fusion.2
  324.0 1.2 reshape_reshape.31
  325.2 4.9 %all-to-all-start.9 = ((bf16[32,48,128]{2,1,0:T(8,128)(2,1)}), bf16[32,48,128]{2,1,0:T(8,128)(2,1)S(1)}, u32[]{:S(2)}, u32[]{:S(2)}) async-start(bf16[32,48,128]{2,1,0:T(8,128)(2,1)} %reshape_reshape.31), calls=%async_computation.9 | async-start | bytes 786432 | tf_op jit(solution)/shard_map/all_to_all | solution.py:14
  330.8 1.2 select_select_fusion
  332.0 3.2 collective-permute-start.6
  335.2 4.3 %collective-permute-start.8 = (bf16[128,1792]{1,0:T(8,128)(2,1)}, bf16[128,1792]{1,0:T(8,128)(2,1)}, u32[]{:S(2)}, u32[]{:S(2)}) collective-permute-start(bf16[128,1792]{1,0:T(8,128)(2,1)} %get-tuple-element.28), channel_id=1, source_target_pairs={{0,384},{128,0},{256,128},{384,256},{1,385},{129,1},{257,129},{385... | collective-permute-start | bytes 1376264 | tf_op jit(solution)/shard_map/ppermute | solution.py:23
  339.6 1.1 select_select_fusion.1
  340.7 5.8 %collective-permute-start.7 = (bf16[128,1792]{1,0:T(8,128)(2,1)}, bf16[128,1792]{1,0:T(8,128)(2,1)S(1)}, u32[]{:S(2)}, u32[]{:S(2)}) collective-permute-start(bf16[128,1792]{1,0:T(8,128)(2,1)} %get-tuple-element.30), channel_id=1, source_target_pairs={{0,256},{128,384},{256,0},{384,128},{1,257},{129,385},{257,1},{385... | collective-permute-start | bytes 1376264 | tf_op jit(solution)/shard_map/ppermute | solution.py:23
  347.6 4.6 %all-to-all-start.10 = ((bf16[16,24,128]{2,1,0:T(8,128)(2,1)}), bf16[16,24,128]{2,1,0:T(8,128)(2,1)S(1)}, u32[]{:S(2)}, u32[]{:S(2)}) async-start(bf16[16,24,128]{2,1,0:T(8,128)(2,1)} %reshape.497), calls=%async_computation.10 | async-start | bytes 196608 | tf_op jit(solution)/shard_map/all_to_all | solution.py:14
  352.2 0.9 select_select_fusion.11
  353.1 29.8 %all-to-all-done.10 = bf16[16,24,128]{2,1,0:T(8,128)(2,1)S(1)} async-done(((bf16[16,24,128]{2,1,0:T(8,128)(2,1)}), bf16[16,24,128]{2,1,0:T(8,128)(2,1)S(1)}, u32[]{:S(2)}, u32[]{:S(2)}) %all-to-all-start.10) | async-done | bytes 98336 | tf_op jit(solution)/shard_map/all_to_all | solution.py:14
  383.0 2.1 slice.143
  385.1 0.9 select_select_fusion.7
  388.0 1.5 fusion.1
  389.5 1.5 fusion
  (160 shorter events, 17.0 us)
Async XLA Ops:
  7.2 29.3 %collective-permute-start = (bf16[256,1536]{1,0:T(8,128)(2,1)}, bf16[256,1536]{1,0:T(8,128)(2,1)}, u32[]{:S(2)}, u32[]{:S(2)}) collective-permute-start(bf16[256,1536]{1,0:T(8,128)(2,1)} %bitcast.218), channel_id=1, source_target_pairs={{0,128},{128,256},{256,384},{384,0},{1,129},{129,257},{257,385},{3... | collective-permute-start | bytes 2359304 | tf_op jit(solution)/shard_map/ppermute | solution.py:23
  12.2 40.4 %collective-permute-start.1 = (bf16[1536,256]{1,0:T(8,128)(2,1)}, bf16[1536,256]{1,0:T(8,128)(2,1)S(1)}, u32[]{:S(2)}, u32[]{:S(2)}) collective-permute-start(bf16[1536,256]{1,0:T(8,128)(2,1)} %bitcast.220), channel_id=1, source_target_pairs={{0,384},{128,0},{256,128},{384,256},{1,385},{129,1},{257,129},{385... | collective-permute-start | bytes 2359304 | tf_op jit(solution)/shard_map/ppermute | solution.py:23
  17.7 41.8 %copy-start.8 = (bf16[1,256,1536]{2,1,0:T(8,128)(2,1)S(1)}, bf16[1,256,1536]{2,1,0:T(8,128)(2,1)}, u32[]{:S(2)}) copy-start(bf16[1,256,1536]{2,1,0:T(8,128)(2,1)} %param.9) | copy-start | bytes 2359300
  18.4 34.2 %all-to-all-start.3 = ((bf16[4,48,128]{2,1,0:T(8,128)(2,1)}), bf16[4,48,128]{2,1,0:T(8,128)(2,1)S(1)}, u32[]{:S(2)}, u32[]{:S(2)}) async-start(bf16[4,48,128]{2,1,0:T(8,128)(2,1)} %reshape.493), calls=%async_computation.3 | async-start | bytes 98304 | tf_op jit(solution)/shard_map/all_to_all | solution.py:14
  52.6 6.2 %copy-start.13 = (bf16[1536,256]{1,0:T(8,128)(2,1)}, bf16[1536,256]{1,0:T(8,128)(2,1)S(1)}, u32[]{:S(2)}) copy-start(bf16[1536,256]{1,0:T(8,128)(2,1)S(1)} %collective-permute-done.1) | copy-start | bytes 2359300
  52.6 20.3 %all-to-all-start = ((bf16[16,89,128]{2,1,0:T(8,128)(2,1)}), bf16[16,89,128]{2,1,0:T(8,128)(2,1)S(1)}, u32[]{:S(2)}, u32[]{:S(2)}) async-start(bf16[16,89,128]{2,1,0:T(8,128)(2,1)} %bitcast.4), calls=%async_computation | async-start | bytes 786432 | tf_op jit(solution)/shard_map/all_to_all | solution.py:14
  58.8 108.9 %all-gather.6.cloned.1.call-start = ((), (), s32[]{:S(2)}) async-start(), calls=%async_computation.11 | async-start | bytes 1622016 | tf_op jit(solution)/shard_map/all_gather | solution.py:98
  59.5 49.1 %collective-permute-start.2 = (bf16[256,1536]{1,0:T(8,128)(2,1)S(1)}, bf16[256,1536]{1,0:T(8,128)(2,1)}, u32[]{:S(2)}, u32[]{:S(2)}) collective-permute-start(bf16[256,1536]{1,0:T(8,128)(2,1)S(1)} %bitcast.219), channel_id=1, source_target_pairs={{0,384},{128,0},{256,128},{384,256},{1,385},{129,1},{257,129},{385... | collective-permute-start | bytes 2359304 | tf_op jit(solution)/shard_map/ppermute | solution.py:23
  65.0 43.7 %collective-permute-start.3 = (bf16[256,1536]{1,0:T(8,128)(2,1)}, bf16[256,1536]{1,0:T(8,128)(2,1)}, u32[]{:S(2)}, u32[]{:S(2)}) collective-permute-start(bf16[256,1536]{1,0:T(8,128)(2,1)} %collective-permute-done), channel_id=1, source_target_pairs={{0,128},{128,256},{256,384},{384,0},{1,129},{129,257},{257,385},{3... | collective-permute-start | bytes 2359304 | tf_op jit(solution)/shard_map/ppermute | solution.py:23
  73.9 27.0 %all-to-all-start.1 = ((bf16[32,48,128]{2,1,0:T(8,128)(2,1)}), bf16[32,48,128]{2,1,0:T(8,128)(2,1)S(1)}, u32[]{:S(2)}, u32[]{:S(2)}) async-start(bf16[32,48,128]{2,1,0:T(8,128)(2,1)} %broadcast_in_dim.71), calls=%async_computation.1 | async-start | bytes 786432 | tf_op jit(solution)/shard_map/all_to_all | solution.py:14
  86.8 53.2 %collective-permute-start.5 = (bf16[1536,256]{1,0:T(8,128)(2,1)}, bf16[1536,256]{1,0:T(8,128)(2,1)}, u32[]{:S(2)}, u32[]{:S(2)}) collective-permute-start(bf16[1536,256]{1,0:T(8,128)(2,1)} %bitcast.221), channel_id=1, source_target_pairs={{0,128},{128,256},{256,384},{384,0},{1,129},{129,257},{257,385},{3... | collective-permute-start | bytes 2359304 | tf_op jit(solution)/shard_map/ppermute | solution.py:23
  89.1 50.9 %collective-permute-start.4 = (bf16[1536,256]{1,0:T(8,128)(2,1)}, bf16[1536,256]{1,0:T(8,128)(2,1)}, u32[]{:S(2)}, u32[]{:S(2)}) collective-permute-start(bf16[1536,256]{1,0:T(8,128)(2,1)} %copy-done.13), channel_id=1, source_target_pairs={{0,384},{128,0},{256,128},{384,256},{1,385},{129,1},{257,129},{385... | collective-permute-start | bytes 2359304 | tf_op jit(solution)/shard_map/ppermute | solution.py:23
  101.4 38.7 %copy-start.9 = (bf16[1,1536,256]{2,1,0:T(8,128)(2,1)S(1)}, bf16[1,1536,256]{2,1,0:T(8,128)(2,1)}, u32[]{:S(2)}) copy-start(bf16[1,1536,256]{2,1,0:T(8,128)(2,1)} %param.8) | copy-start | bytes 2359300
  101.4 38.7 %copy-start.14 = (bf16[1536,256]{1,0:T(8,128)(2,1)S(1)}, bf16[1536,256]{1,0:T(8,128)(2,1)}, u32[]{:S(2)}) copy-start(bf16[1536,256]{1,0:T(8,128)(2,1)} %copy-done.13) | copy-start | bytes 2359300
  142.9 24.6 %all-to-all-start.2 = ((bf16[32,48,128]{2,1,0:T(8,128)(2,1)}), bf16[32,48,128]{2,1,0:T(8,128)(2,1)S(1)}, u32[]{:S(2)}, u32[]{:S(2)}) async-start(bf16[32,48,128]{2,1,0:T(8,128)(2,1)} %reshape_reshape.25), calls=%async_computation.2 | async-start | bytes 786432 | tf_op jit(solution)/shard_map/all_to_all | solution.py:14
  177.4 15.7 %all-to-all-start.4 = ((bf16[32,48,128]{2,1,0:T(8,128)(2,1)}), bf16[32,48,128]{2,1,0:T(8,128)(2,1)S(1)}, u32[]{:S(2)}, u32[]{:S(2)}) async-start(bf16[32,48,128]{2,1,0:T(8,128)(2,1)} %broadcast_in_dim.74), calls=%async_computation.4 | async-start | bytes 786432 | tf_op jit(solution)/shard_map/all_to_all | solution.py:14
  193.6 12.4 %copy-start.10 = (bf16[1,1536,256]{2,1,0:T(8,128)(2,1)S(1)}, bf16[1,1536,256]{2,1,0:T(8,128)(2,1)}, u32[]{:S(2)}) copy-start(bf16[1,1536,256]{2,1,0:T(8,128)(2,1)} %param.8) | copy-start | bytes 2359300
  193.6 12.4 %copy-start.15 = (bf16[1536,256]{1,0:T(8,128)(2,1)S(1)}, bf16[1536,256]{1,0:T(8,128)(2,1)}, u32[]{:S(2)}) copy-start(bf16[1536,256]{1,0:T(8,128)(2,1)} %copy-done.13) | copy-start | bytes 2359300
  208.8 17.0 %all-to-all-start.5 = ((bf16[32,48,128]{2,1,0:T(8,128)(2,1)}), bf16[32,48,128]{2,1,0:T(8,128)(2,1)S(1)}, u32[]{:S(2)}, u32[]{:S(2)}) async-start(bf16[32,48,128]{2,1,0:T(8,128)(2,1)} %reshape_reshape.27), calls=%async_computation.5 | async-start | bytes 786432 | tf_op jit(solution)/shard_map/all_to_all | solution.py:14
  235.0 16.0 %all-to-all-start.6 = ((bf16[32,48,128]{2,1,0:T(8,128)(2,1)}), bf16[32,48,128]{2,1,0:T(8,128)(2,1)S(1)}, u32[]{:S(2)}, u32[]{:S(2)}) async-start(bf16[32,48,128]{2,1,0:T(8,128)(2,1)} %broadcast_in_dim.77), calls=%async_computation.6 | async-start | bytes 786432 | tf_op jit(solution)/shard_map/all_to_all | solution.py:14
  251.5 12.8 %copy-start.11 = (bf16[1,1536,256]{2,1,0:T(8,128)(2,1)S(1)}, bf16[1,1536,256]{2,1,0:T(8,128)(2,1)}, u32[]{:S(2)}) copy-start(bf16[1,1536,256]{2,1,0:T(8,128)(2,1)} %param.8) | copy-start | bytes 2359300
  251.5 12.8 %copy-start.16 = (bf16[1536,256]{1,0:T(8,128)(2,1)S(1)}, bf16[1536,256]{1,0:T(8,128)(2,1)}, u32[]{:S(2)}) copy-start(bf16[1536,256]{1,0:T(8,128)(2,1)} %copy-done.13) | copy-start | bytes 2359300
  267.1 31.7 %copy-start = (bf16[1,1,1,4,6144]{4,3,2,1,0:T(4,128)(2,1)S(1)}, bf16[1,1,1,4,6144]{4,3,2,1,0:T(4,128)(2,1)}, u32[]{:S(2)}) copy-start(bf16[1,1,1,4,6144]{4,3,2,1,0:T(4,128)(2,1)} %param.5) | copy-start | bytes 147460
  267.1 31.8 %copy-start.5 = (bf16[1,1,1,128,256]{4,3,2,1,0:T(8,128)(2,1)S(1)}, bf16[1,1,1,128,256]{4,3,2,1,0:T(8,128)(2,1)}, u32[]{:S(2)}) copy-start(bf16[1,1,1,128,256]{4,3,2,1,0:T(8,128)(2,1)} %param.6) | copy-start | bytes 196612
  267.2 17.2 %all-to-all-start.7 = ((bf16[32,48,128]{2,1,0:T(8,128)(2,1)}), bf16[32,48,128]{2,1,0:T(8,128)(2,1)S(1)}, u32[]{:S(2)}, u32[]{:S(2)}) async-start(bf16[32,48,128]{2,1,0:T(8,128)(2,1)} %reshape_reshape.29), calls=%async_computation.7 | async-start | bytes 786432 | tf_op jit(solution)/shard_map/all_to_all | solution.py:14
  293.5 16.0 %all-to-all-start.8 = ((bf16[32,48,128]{2,1,0:T(8,128)(2,1)}), bf16[32,48,128]{2,1,0:T(8,128)(2,1)S(1)}, u32[]{:S(2)}, u32[]{:S(2)}) async-start(bf16[32,48,128]{2,1,0:T(8,128)(2,1)} %broadcast_in_dim.80), calls=%async_computation.8 | async-start | bytes 786432 | tf_op jit(solution)/shard_map/all_to_all | solution.py:14
  309.9 12.4 %copy-start.12 = (bf16[1,1536,256]{2,1,0:T(8,128)(2,1)S(1)}, bf16[1,1536,256]{2,1,0:T(8,128)(2,1)}, u32[]{:S(2)}) copy-start(bf16[1,1536,256]{2,1,0:T(8,128)(2,1)} %param.8) | copy-start | bytes 2359300
  309.9 12.4 %copy-start.17 = (bf16[1536,256]{1,0:T(8,128)(2,1)S(1)}, bf16[1536,256]{1,0:T(8,128)(2,1)}, u32[]{:S(2)}) copy-start(bf16[1536,256]{1,0:T(8,128)(2,1)} %copy-done.13) | copy-start | bytes 2359300
  325.2 21.3 %all-to-all-start.9 = ((bf16[32,48,128]{2,1,0:T(8,128)(2,1)}), bf16[32,48,128]{2,1,0:T(8,128)(2,1)S(1)}, u32[]{:S(2)}, u32[]{:S(2)}) async-start(bf16[32,48,128]{2,1,0:T(8,128)(2,1)} %reshape_reshape.31), calls=%async_computation.9 | async-start | bytes 786432 | tf_op jit(solution)/shard_map/all_to_all | solution.py:14
  332.0 50.9 %collective-permute-start.6 = (bf16[128,1792]{1,0:T(8,128)(2,1)}, bf16[128,1792]{1,0:T(8,128)(2,1)S(1)}, u32[]{:S(2)}, u32[]{:S(2)}) collective-permute-start(bf16[128,1792]{1,0:T(8,128)(2,1)} %get-tuple-element.29), channel_id=1, source_target_pairs={{0,128},{128,256},{256,384},{384,0},{1,129},{129,257},{257,385},{3... | collective-permute-start | bytes 1376264 | tf_op jit(solution)/shard_map/ppermute | solution.py:23
  335.2 11.4 %copy-start.6 = (bf16[1,4,1536]{2,1,0:T(4,128)(2,1)S(1)}, bf16[1,4,1536]{2,1,0:T(4,128)(2,1)}, u32[]{:S(2)}) copy-start(bf16[1,4,1536]{2,1,0:T(4,128)(2,1)} %fusion.81) | copy-start | bytes 36868
  335.2 16.9 %copy-start.4 = (bf16[128,256]{1,0:T(8,128)(2,1)S(1)}, bf16[128,256]{1,0:T(8,128)(2,1)}, u32[]{:S(2)}) copy-start(bf16[128,256]{1,0:T(8,128)(2,1)} %squeeze.71) | copy-start | bytes 196612
  335.2 47.7 %collective-permute-start.8 = (bf16[128,1792]{1,0:T(8,128)(2,1)}, bf16[128,1792]{1,0:T(8,128)(2,1)}, u32[]{:S(2)}, u32[]{:S(2)}) collective-permute-start(bf16[128,1792]{1,0:T(8,128)(2,1)} %get-tuple-element.28), channel_id=1, source_target_pairs={{0,384},{128,0},{256,128},{384,256},{1,385},{129,1},{257,129},{385... | collective-permute-start | bytes 1376264 | tf_op jit(solution)/shard_map/ppermute | solution.py:23
  340.7 42.2 %collective-permute-start.7 = (bf16[128,1792]{1,0:T(8,128)(2,1)}, bf16[128,1792]{1,0:T(8,128)(2,1)S(1)}, u32[]{:S(2)}, u32[]{:S(2)}) collective-permute-start(bf16[128,1792]{1,0:T(8,128)(2,1)} %get-tuple-element.30), channel_id=1, source_target_pairs={{0,256},{128,384},{256,0},{384,128},{1,257},{129,385},{257,1},{385... | collective-permute-start | bytes 1376264 | tf_op jit(solution)/shard_map/ppermute | solution.py:23
  347.6 35.3 %all-to-all-start.10 = ((bf16[16,24,128]{2,1,0:T(8,128)(2,1)}), bf16[16,24,128]{2,1,0:T(8,128)(2,1)S(1)}, u32[]{:S(2)}, u32[]{:S(2)}) async-start(bf16[16,24,128]{2,1,0:T(8,128)(2,1)} %reshape.497), calls=%async_computation.10 | async-start | bytes 196608 | tf_op jit(solution)/shard_map/all_to_all | solution.py:14
  382.9 2.2 copy-start.1
  382.9 2.1 copy-start.2
  385.9 2.0 slice-start
  386.0 2.0 slice-start.1
  386.0 2.0 copy-start.3
  388.0 1.5 copy-start.7
Sparse Core Ops, SparseCore 0:
  63.3 84.7 all-gather.5

commit v4 on v3

--- a/solution.py
+++ b/solution.py
@@ -10,7 +10,7 @@
 
 
 def exchange(blocks, axis, count):
-    flat = blocks.reshape(count, -1, LANES)
+    flat = blocks if blocks.shape[0] == count else blocks.reshape(count, -1, LANES)
     return lax.all_to_all(flat, axis, 0, 0).reshape(blocks.shape)
 
 
@@ -146,8 +146,7 @@
         chosen = choose(pipe_index, [stores[(p + k) % pipe] for p in range(pipe)])
         moved.append(shifted(chosen, k))
     moved = lax.optimization_barrier((moved, outs))[0]
-    grads = jnp.concatenate([piece[:, :block] for piece in moved], 0)
-    down_grad = dot_tn(hidden, grads)
+    down_grad = dot_tn(hidden, jnp.concatenate(moved, 0))[:, :block]
     pres = [piece[:, block:] for piece in moved]
     pres = [choose(pipe_index, [pres[(p - i) % pipe] for p in range(pipe)]) for i in range(pipe)]
     pres = jnp.stack([piece.reshape(parts, groups, hidden_width) for piece in pres], 1)

time: 401 us -> 399 us (level)
  local copies, waits for them, and re-layouts: 21.3 us -> 15.7 us
    another operation x9 -> x1, local copies, waits for them, and re-layouts: 6.71 us -> 0.01 us  [per_device(): grad = mixed[0, :, lines:2 * lines].reshape(groups, block)]
where the time goes in v4:
time: 399 us; the launch traced here: 396 us
  waiting for transfers between devices  128 us (32%)
  starting transfers between devices  113 us (28%)
  blocking collectives  91.9 us (23%)
  matrix products  19.7 us (5%)
  local copies, waits for them, and re-layouts  15.7 us (4%)
  between operations  14.8 us (4%)
  other arithmetic  12.3 us (3%)
    all_to_all x11, waiting for transfers between devices, exchange(): return lax.all_to_all(flat, axis, 0, 0).reshape(blocks.shape)  100 us
    all_to_all x11, starting transfers between devices, exchange(): return lax.all_to_all(flat, axis, 0, 0).reshape(blocks.shape)  76.4 us
    all_gather x4, blocking collectives, per_device(): lax.all_gather(dot_nt(grad_rows, choose(place, down_all)), 'dp', axis=0)  60.5 us
    ppermute x9, starting transfers between devices, shifted(): lax.ppermute(value, 'pipe', [(i, (i + steps) % count) for i in range(coun...  36.6 us
    ppermute x9, waiting for transfers between devices, shifted(): lax.ppermute(value, 'pipe', [(i, (i + steps) % count) for i in range(coun...  28 us
    psum x3, blocking collectives, per_device(): lax.psum(jnp.sum(normed_grad * x_s, axis=-1, keepdims=True), 'dp') / width  24.2 us
    dot_general x8, matrix products, dot_nt(): lax.dot_general(left, right, (((1,), (1,)), ((), ())), preferred_element_...  14.9 us
  transfers between devices with their start and end apart: 21, of which 12 were waited for; matrix products, arithmetic and copies ran while one was open for 5% of the time, Pallas kernels for 0%

profile of v4, /device:TPU:1, one launch (start us, length us, event | category | flops | bytes accessed | tf_op | source)
XLA Modules:
  0.0 395.8 jit_solution(142817345537302186)
XLA Ops:
  7.2 5.0 %collective-permute-start = (bf16[256,1536]{1,0:T(8,128)(2,1)}, bf16[256,1536]{1,0:T(8,128)(2,1)}, u32[]{:S(2)}, u32[]{:S(2)}) collective-permute-start(bf16[256,1536]{1,0:T(8,128)(2,1)} %bitcast.2), channel_id=1, source_target_pairs={{0,128},{128,256},{256,384},{384,0},{1,129},{129,257},{257,385},{3... | collective-permute-start | bytes 2359304 | tf_op jit(solution)/shard_map/ppermute | solution.py:23
  12.2 3.6 collective-permute-start.1
  15.8 1.0 multiply_reduce_fusion.1
  18.9 9.4 %all-to-all-start.3 = ((bf16[4,4,1536]{2,1,0:T(4,128)(2,1)}), bf16[4,4,1536]{2,1,0:T(4,128)(2,1)S(1)}, u32[]{:S(2)}, u32[]{:S(2)}) async-start(bf16[4,4,1536]{2,1,0:T(4,128)(2,1)} %fusion.73), calls=%async_computation.3 | async-start | bytes 98304 | tf_op jit(solution)/shard_map/all_to_all | solution.py:14
  28.3 0.9 reshape_squeeze.16
  29.4 0.9 reshape_squeeze.18
  30.3 0.9 reshape_squeeze.17
  32.2 4.3 %collective-permute-done = bf16[256,1536]{1,0:T(8,128)(2,1)} collective-permute-done((bf16[256,1536]{1,0:T(8,128)(2,1)}, bf16[256,1536]{1,0:T(8,128)(2,1)}, u32[]{:S(2)}, u32[]{:S(2)}) %collective-permute-start) | collective-permute-done | bytes 786464 | tf_op jit(solution)/shard_map/ppermute | solution.py:23
  36.5 16.2 %collective-permute-done.1 = bf16[1536,256]{1,0:T(8,128)(2,1)} collective-permute-done((bf16[1536,256]{1,0:T(8,128)(2,1)}, bf16[1536,256]{1,0:T(8,128)(2,1)}, u32[]{:S(2)}, u32[]{:S(2)}) %collective-permute-start.1) | collective-permute-done | bytes 786464 | tf_op jit(solution)/shard_map/ppermute | solution.py:23
  52.7 6.1 %all-to-all-start = ((bf16[16,89,128]{2,1,0:T(8,128)(2,1)}), bf16[16,89,128]{2,1,0:T(8,128)(2,1)S(1)}, u32[]{:S(2)}, u32[]{:S(2)}) async-start(bf16[16,89,128]{2,1,0:T(8,128)(2,1)} %bitcast.4), calls=%async_computation | async-start | bytes 786432 | tf_op jit(solution)/shard_map/all_to_all | solution.py:14
  58.8 5.4 %collective-permute-start.2 = (bf16[256,1536]{1,0:T(8,128)(2,1)}, bf16[256,1536]{1,0:T(8,128)(2,1)}, u32[]{:S(2)}, u32[]{:S(2)}) collective-permute-start(bf16[256,1536]{1,0:T(8,128)(2,1)} %bitcast.2), channel_id=1, source_target_pairs={{0,384},{128,0},{256,128},{384,256},{1,385},{129,1},{257,129},{385... | collective-permute-start | bytes 2359304 | tf_op jit(solution)/shard_map/ppermute | solution.py:23
  64.9 1.9 collective-permute-start.3
  66.8 6.1 %all-to-all-done = bf16[16,89,128]{2,1,0:T(8,128)(2,1)S(1)} async-done(((bf16[16,89,128]{2,1,0:T(8,128)(2,1)}), bf16[16,89,128]{2,1,0:T(8,128)(2,1)S(1)}, u32[]{:S(2)}, u32[]{:S(2)}) %all-to-all-start) | async-done | bytes 364576 | tf_op jit(solution)/shard_map/all_to_all | solution.py:14
  73.1 0.8 broadcast_in_dim.64
  73.9 12.9 %all-to-all-start.1 = ((bf16[32,4,1536]{2,1,0:T(4,128)(2,1)}), bf16[32,4,1536]{2,1,0:T(4,128)(2,1)S(1)}, u32[]{:S(2)}, u32[]{:S(2)}) async-start(bf16[32,4,1536]{2,1,0:T(4,128)(2,1)} %broadcast_in_dim.64), calls=%async_computation.1 | async-start | bytes 786432 | tf_op jit(solution)/shard_map/all_to_all | solution.py:14
  86.8 2.3 collective-permute-start.5
  89.2 5.1 %collective-permute-start.4 = (bf16[1536,256]{1,0:T(8,128)(2,1)}, bf16[1536,256]{1,0:T(8,128)(2,1)}, u32[]{:S(2)}, u32[]{:S(2)}) collective-permute-start(bf16[1536,256]{1,0:T(8,128)(2,1)} %collective-permute-done.1), channel_id=1, source_target_pairs={{0,384},{128,0},{256,128},{384,256},{1,385},{129,1},{257,129},{385... | collective-permute-start | bytes 2359304 | tf_op jit(solution)/shard_map/ppermute | solution.py:23
  95.7 5.3 %all-to-all-done.1 = bf16[32,4,1536]{2,1,0:T(4,128)(2,1)S(1)} async-done(((bf16[32,4,1536]{2,1,0:T(4,128)(2,1)}), bf16[32,4,1536]{2,1,0:T(4,128)(2,1)S(1)}, u32[]{:S(2)}, u32[]{:S(2)}) %all-to-all-start.1) | async-done | bytes 393248 | tf_op jit(solution)/shard_map/all_to_all | solution.py:14
  101.1 7.5 %collective-permute-done.2 = bf16[256,1536]{1,0:T(8,128)(2,1)} collective-permute-done((bf16[256,1536]{1,0:T(8,128)(2,1)}, bf16[256,1536]{1,0:T(8,128)(2,1)}, u32[]{:S(2)}, u32[]{:S(2)}) %collective-permute-start.2) | collective-permute-done | bytes 786464 | tf_op jit(solution)/shard_map/ppermute | solution.py:23
  108.6 1.8 convolution_convert_fusion.8
  110.4 29.5 %all-gather = bf16[512,256]{1,0:T(8,128)(2,1)S(1)} all-gather(bf16[128,256]{1,0:T(8,128)(2,1)S(1)} %convolution_convert_fusion.8), channel_id=2, replica_groups=mesh['pipe'=4,'tensor'=32,'dp'=4] {'dp'}, dimensions={0}, use_global_device_ids=true | all-gather | bytes 327680 | tf_op jit(solution)/shard_map/all_gather | solution.py:115
  140.0 1.8 convolution_convert_fusion.4
  141.9 0.8 reshape.471
  142.7 12.9 %all-to-all-start.2 = ((bf16[32,4,1536]{2,1,0:T(4,128)(2,1)}), bf16[32,4,1536]{2,1,0:T(4,128)(2,1)S(1)}, u32[]{:S(2)}, u32[]{:S(2)}) async-start(bf16[32,4,1536]{2,1,0:T(4,128)(2,1)} %reshape.471), calls=%async_computation.2 | async-start | bytes 786432 | tf_op jit(solution)/shard_map/all_to_all | solution.py:14
  155.9 11.5 %all-to-all-done.2 = bf16[32,4,1536]{2,1,0:T(4,128)(2,1)S(1)} async-done(((bf16[32,4,1536]{2,1,0:T(4,128)(2,1)}), bf16[32,4,1536]{2,1,0:T(4,128)(2,1)S(1)}, u32[]{:S(2)}, u32[]{:S(2)}) %all-to-all-start.2) | async-done | bytes 393248 | tf_op jit(solution)/shard_map/all_to_all | solution.py:14
  167.7 8.4 %psum.21 = f32[4,1]{0,1:T(1,128)S(1)} all-reduce(f32[4,1]{0,1:T(1,128)S(1)} %bitcast.215), channel_id=1, replica_groups=mesh['pipe'=4,'tensor'=32,'dp'=4] {'dp'}, use_global_device_ids=true, to_apply=%region_4.5 | all-reduce | flops 4 | bytes 32 | tf_op jit(solution)/shard_map/psum | solution.py:128
  176.2 0.8 broadcast_in_dim.67
  177.1 5.1 %all-to-all-start.4 = ((bf16[32,4,1536]{2,1,0:T(4,128)(2,1)}), bf16[32,4,1536]{2,1,0:T(4,128)(2,1)S(1)}, u32[]{:S(2)}, u32[]{:S(2)}) async-start(bf16[32,4,1536]{2,1,0:T(4,128)(2,1)} %broadcast_in_dim.67), calls=%async_computation.4 | async-start | bytes 786432 | tf_op jit(solution)/shard_map/all_to_all | solution.py:14
  182.3 11.0 %all-to-all-done.4 = bf16[32,4,1536]{2,1,0:T(4,128)(2,1)S(1)} async-done(((bf16[32,4,1536]{2,1,0:T(4,128)(2,1)}), bf16[32,4,1536]{2,1,0:T(4,128)(2,1)S(1)}, u32[]{:S(2)}, u32[]{:S(2)}) %all-to-all-start.4) | async-done | bytes 393248 | tf_op jit(solution)/shard_map/all_to_all | solution.py:14
  193.4 1.8 convolution_convert_fusion.7
  195.2 10.1 %all-gather.1 = bf16[512,256]{1,0:T(8,128)(2,1)S(1)} all-gather(bf16[128,256]{1,0:T(8,128)(2,1)S(1)} %convolution_convert_fusion.7), channel_id=3, replica_groups=mesh['pipe'=4,'tensor'=32,'dp'=4] {'dp'}, dimensions={0}, use_global_device_ids=true | all-gather | bytes 327680 | tf_op jit(solution)/shard_map/all_gather | solution.py:115
  205.3 1.8 convolution_convert_fusion.3
  207.2 0.8 reshape.474
  208.0 4.8 %all-to-all-start.5 = ((bf16[32,4,1536]{2,1,0:T(4,128)(2,1)}), bf16[32,4,1536]{2,1,0:T(4,128)(2,1)S(1)}, u32[]{:S(2)}, u32[]{:S(2)}) async-start(bf16[32,4,1536]{2,1,0:T(4,128)(2,1)} %reshape.474), calls=%async_computation.5 | async-start | bytes 786432 | tf_op jit(solution)/shard_map/all_to_all | solution.py:14
  212.8 12.1 %all-to-all-done.5 = bf16[32,4,1536]{2,1,0:T(4,128)(2,1)S(1)} async-done(((bf16[32,4,1536]{2,1,0:T(4,128)(2,1)}), bf16[32,4,1536]{2,1,0:T(4,128)(2,1)S(1)}, u32[]{:S(2)}, u32[]{:S(2)}) %all-to-all-start.5) | async-done | bytes 393248 | tf_op jit(solution)/shard_map/all_to_all | solution.py:14
  225.3 7.9 %psum.22 = f32[4,1]{0,1:T(1,128)S(1)} all-reduce(f32[4,1]{0,1:T(1,128)S(1)} %bitcast.216), channel_id=1, replica_groups=mesh['pipe'=4,'tensor'=32,'dp'=4] {'dp'}, use_global_device_ids=true, to_apply=%region_8.9 | all-reduce | flops 4 | bytes 32 | tf_op jit(solution)/shard_map/psum | solution.py:128
  233.2 0.8 broadcast_in_dim.69
  234.1 5.3 %all-to-all-start.6 = ((bf16[32,4,1536]{2,1,0:T(4,128)(2,1)}), bf16[32,4,1536]{2,1,0:T(4,128)(2,1)S(1)}, u32[]{:S(2)}, u32[]{:S(2)}) async-start(bf16[32,4,1536]{2,1,0:T(4,128)(2,1)} %broadcast_in_dim.69), calls=%async_computation.6 | async-start | bytes 786432 | tf_op jit(solution)/shard_map/all_to_all | solution.py:14
  239.4 10.6 %all-to-all-done.6 = bf16[32,4,1536]{2,1,0:T(4,128)(2,1)S(1)} async-done(((bf16[32,4,1536]{2,1,0:T(4,128)(2,1)}), bf16[32,4,1536]{2,1,0:T(4,128)(2,1)S(1)}, u32[]{:S(2)}, u32[]{:S(2)}) %all-to-all-start.6) | async-done | bytes 393248 | tf_op jit(solution)/shard_map/all_to_all | solution.py:14
  250.1 2.0 convolution_convert_fusion.6
  252.2 10.4 %all-gather.2 = bf16[512,256]{1,0:T(8,128)(2,1)S(1)} all-gather(bf16[128,256]{1,0:T(8,128)(2,1)S(1)} %convolution_convert_fusion.6), channel_id=4, replica_groups=mesh['pipe'=4,'tensor'=32,'dp'=4] {'dp'}, dimensions={0}, use_global_device_ids=true | all-gather | bytes 327680 | tf_op jit(solution)/shard_map/all_gather | solution.py:115
  262.7 2.1 convolution_convert_fusion.2
  265.6 4.9 %all-to-all-start.7 = ((bf16[32,4,1536]{2,1,0:T(4,128)(2,1)}), bf16[32,4,1536]{2,1,0:T(4,128)(2,1)S(1)}, u32[]{:S(2)}, u32[]{:S(2)}) async-start(bf16[32,4,1536]{2,1,0:T(4,128)(2,1)} %reshape.477), calls=%async_computation.7 | async-start | bytes 786432 | tf_op jit(solution)/shard_map/all_to_all | solution.py:14
  270.5 12.1 %all-to-all-done.7 = bf16[32,4,1536]{2,1,0:T(4,128)(2,1)S(1)} async-done(((bf16[32,4,1536]{2,1,0:T(4,128)(2,1)}), bf16[32,4,1536]{2,1,0:T(4,128)(2,1)S(1)}, u32[]{:S(2)}, u32[]{:S(2)}) %all-to-all-start.7) | async-done | bytes 393248 | tf_op jit(solution)/shard_map/all_to_all | solution.py:14
  282.9 7.9 %psum.23 = f32[4,1]{0,1:T(1,128)S(1)} all-reduce(f32[4,1]{0,1:T(1,128)S(1)} %bitcast.217), channel_id=1, replica_groups=mesh['pipe'=4,'tensor'=32,'dp'=4] {'dp'}, use_global_device_ids=true, to_apply=%region_12.13 | all-reduce | flops 4 | bytes 32 | tf_op jit(solution)/shard_map/psum | solution.py:128
  290.9 0.8 broadcast_in_dim.71
  291.8 5.5 %all-to-all-start.8 = ((bf16[32,4,1536]{2,1,0:T(4,128)(2,1)}), bf16[32,4,1536]{2,1,0:T(4,128)(2,1)S(1)}, u32[]{:S(2)}, u32[]{:S(2)}) async-start(bf16[32,4,1536]{2,1,0:T(4,128)(2,1)} %broadcast_in_dim.71), calls=%async_computation.8 | async-start | bytes 786432 | tf_op jit(solution)/shard_map/all_to_all | solution.py:14
  297.5 7.2 %all_gather.36 = bf16[4,128,256]{2,1,0:T(8,128)(2,1)S(1)} all-gather(bf16[1,128,256]{2,1,0:T(8,128)(2,1)S(1)} %fusion.66), channel_id=1, replica_groups=mesh['pipe'=4,'tensor'=32,'dp'=4] {'dp'}, dimensions={0}, use_global_device_ids=true | all-gather | bytes 327680 | tf_op jit(solution)/shard_map/all_gather | solution.py:101
  305.2 2.5 all-to-all-done.8
  307.8 1.8 convolution_convert_fusion.5
  309.6 10.4 %all-gather.3 = bf16[512,256]{1,0:T(8,128)(2,1)S(1)} all-gather(bf16[128,256]{1,0:T(8,128)(2,1)S(1)} %convolution_convert_fusion.5), channel_id=5, replica_groups=mesh['pipe'=4,'tensor'=32,'dp'=4] {'dp'}, dimensions={0}, use_global_device_ids=true | all-gather | bytes 327680 | tf_op jit(solution)/shard_map/all_gather | solution.py:115
  320.1 1.8 convolution_convert_fusion.1
  322.8 4.9 %all-to-all-start.9 = ((bf16[32,4,1536]{2,1,0:T(4,128)(2,1)}), bf16[32,4,1536]{2,1,0:T(4,128)(2,1)S(1)}, u32[]{:S(2)}, u32[]{:S(2)}) async-start(bf16[32,4,1536]{2,1,0:T(4,128)(2,1)} %reshape.479), calls=%async_computation.9 | async-start | bytes 786432 | tf_op jit(solution)/shard_map/all_to_all | solution.py:14
  328.4 1.1 select_select_fusion
  329.5 3.2 collective-permute-start.6
  332.7 4.2 %collective-permute-start.8 = (bf16[128,1792]{1,0:T(8,128)(2,1)S(1)}, bf16[128,1792]{1,0:T(8,128)(2,1)}, u32[]{:S(2)}, u32[]{:S(2)}) collective-permute-start(bf16[128,1792]{1,0:T(8,128)(2,1)S(1)} %get-tuple-element.28), channel_id=1, source_target_pairs={{0,384},{128,0},{256,128},{384,256},{1,385},{129,1},{257,129},{385... | collective-permute-start | bytes 1376264 | tf_op jit(solution)/shard_map/ppermute | solution.py:23
  336.9 1.1 select_select_fusion.1
  338.0 5.8 %collective-permute-start.7 = (bf16[128,1792]{1,0:T(8,128)(2,1)}, bf16[128,1792]{1,0:T(8,128)(2,1)S(1)}, u32[]{:S(2)}, u32[]{:S(2)}) collective-permute-start(bf16[128,1792]{1,0:T(8,128)(2,1)} %get-tuple-element.30), channel_id=1, source_target_pairs={{0,256},{128,384},{256,0},{384,128},{1,257},{129,385},{257,1},{385... | collective-permute-start | bytes 1376264 | tf_op jit(solution)/shard_map/ppermute | solution.py:23
  346.4 4.6 %all-to-all-start.10 = ((bf16[16,24,128]{2,1,0:T(8,128)(2,1)}), bf16[16,24,128]{2,1,0:T(8,128)(2,1)S(1)}, u32[]{:S(2)}, u32[]{:S(2)}) async-start(bf16[16,24,128]{2,1,0:T(8,128)(2,1)} %reshape.480), calls=%async_computation.10 | async-start | bytes 196608 | tf_op jit(solution)/shard_map/all_to_all | solution.py:14
  351.0 28.9 %all-to-all-done.10 = bf16[16,24,128]{2,1,0:T(8,128)(2,1)S(1)} async-done(((bf16[16,24,128]{2,1,0:T(8,128)(2,1)}), bf16[16,24,128]{2,1,0:T(8,128)(2,1)S(1)}, u32[]{:S(2)}, u32[]{:S(2)}) %all-to-all-start.10) | async-done | bytes 98336 | tf_op jit(solution)/shard_map/all_to_all | solution.py:14
  380.3 1.1 select_select_fusion.7
  381.4 2.0 fusion.1
  383.4 0.9 fusion.9
  386.1 2.9 fusion
  (114 shorter events, 15.2 us)
Async XLA Ops:
  7.2 29.3 %collective-permute-start = (bf16[256,1536]{1,0:T(8,128)(2,1)}, bf16[256,1536]{1,0:T(8,128)(2,1)}, u32[]{:S(2)}, u32[]{:S(2)}) collective-permute-start(bf16[256,1536]{1,0:T(8,128)(2,1)} %bitcast.2), channel_id=1, source_target_pairs={{0,128},{128,256},{256,384},{384,0},{1,129},{129,257},{257,385},{3... | collective-permute-start | bytes 2359304 | tf_op jit(solution)/shard_map/ppermute | solution.py:23
  12.2 40.5 %collective-permute-start.1 = (bf16[1536,256]{1,0:T(8,128)(2,1)}, bf16[1536,256]{1,0:T(8,128)(2,1)}, u32[]{:S(2)}, u32[]{:S(2)}) collective-permute-start(bf16[1536,256]{1,0:T(8,128)(2,1)} %bitcast.3), channel_id=1, source_target_pairs={{0,384},{128,0},{256,128},{384,256},{1,385},{129,1},{257,129},{385... | collective-permute-start | bytes 2359304 | tf_op jit(solution)/shard_map/ppermute | solution.py:23
  18.1 11.2 %copy-start.5 = (f32[4]{0:T(128)}, f32[4]{0:T(128)S(1)}, u32[]{:S(2)}) copy-start(f32[4]{0:T(128)S(1)} %get-tuple-element.23) | copy-start | bytes 52
  18.9 33.8 %all-to-all-start.3 = ((bf16[4,4,1536]{2,1,0:T(4,128)(2,1)}), bf16[4,4,1536]{2,1,0:T(4,128)(2,1)S(1)}, u32[]{:S(2)}, u32[]{:S(2)}) async-start(bf16[4,4,1536]{2,1,0:T(4,128)(2,1)} %fusion.73), calls=%async_computation.3 | async-start | bytes 98304 | tf_op jit(solution)/shard_map/all_to_all | solution.py:14
  52.7 20.2 %all-to-all-start = ((bf16[16,89,128]{2,1,0:T(8,128)(2,1)}), bf16[16,89,128]{2,1,0:T(8,128)(2,1)S(1)}, u32[]{:S(2)}, u32[]{:S(2)}) async-start(bf16[16,89,128]{2,1,0:T(8,128)(2,1)} %bitcast.4), calls=%async_computation | async-start | bytes 786432 | tf_op jit(solution)/shard_map/all_to_all | solution.py:14
  58.8 108.6 %all-gather.6.cloned.1.call-start = ((), (), s32[]{:S(2)}) async-start(), calls=%async_computation.11 | async-start | bytes 1622016 | tf_op jit(solution)/shard_map/all_gather | solution.py:98
  58.8 49.8 %collective-permute-start.2 = (bf16[256,1536]{1,0:T(8,128)(2,1)}, bf16[256,1536]{1,0:T(8,128)(2,1)}, u32[]{:S(2)}, u32[]{:S(2)}) collective-permute-start(bf16[256,1536]{1,0:T(8,128)(2,1)} %bitcast.2), channel_id=1, source_target_pairs={{0,384},{128,0},{256,128},{384,256},{1,385},{129,1},{257,129},{385... | collective-permute-start | bytes 2359304 | tf_op jit(solution)/shard_map/ppermute | solution.py:23
  64.9 43.7 %collective-permute-start.3 = (bf16[256,1536]{1,0:T(8,128)(2,1)}, bf16[256,1536]{1,0:T(8,128)(2,1)}, u32[]{:S(2)}, u32[]{:S(2)}) collective-permute-start(bf16[256,1536]{1,0:T(8,128)(2,1)} %collective-permute-done), channel_id=1, source_target_pairs={{0,128},{128,256},{256,384},{384,0},{1,129},{129,257},{257,385},{3... | collective-permute-start | bytes 2359304 | tf_op jit(solution)/shard_map/ppermute | solution.py:23
  73.9 27.1 %all-to-all-start.1 = ((bf16[32,4,1536]{2,1,0:T(4,128)(2,1)}), bf16[32,4,1536]{2,1,0:T(4,128)(2,1)S(1)}, u32[]{:S(2)}, u32[]{:S(2)}) async-start(bf16[32,4,1536]{2,1,0:T(4,128)(2,1)} %broadcast_in_dim.64), calls=%async_computation.1 | async-start | bytes 786432 | tf_op jit(solution)/shard_map/all_to_all | solution.py:14
  86.8 53.2 %collective-permute-start.5 = (bf16[1536,256]{1,0:T(8,128)(2,1)}, bf16[1536,256]{1,0:T(8,128)(2,1)}, u32[]{:S(2)}, u32[]{:S(2)}) collective-permute-start(bf16[1536,256]{1,0:T(8,128)(2,1)} %bitcast.3), channel_id=1, source_target_pairs={{0,128},{128,256},{256,384},{384,0},{1,129},{129,257},{257,385},{3... | collective-permute-start | bytes 2359304 | tf_op jit(solution)/shard_map/ppermute | solution.py:23
  89.2 50.9 %collective-permute-start.4 = (bf16[1536,256]{1,0:T(8,128)(2,1)}, bf16[1536,256]{1,0:T(8,128)(2,1)}, u32[]{:S(2)}, u32[]{:S(2)}) collective-permute-start(bf16[1536,256]{1,0:T(8,128)(2,1)} %collective-permute-done.1), channel_id=1, source_target_pairs={{0,384},{128,0},{256,128},{384,256},{1,385},{129,1},{257,129},{385... | collective-permute-start | bytes 2359304 | tf_op jit(solution)/shard_map/ppermute | solution.py:23
  142.7 24.6 %all-to-all-start.2 = ((bf16[32,4,1536]{2,1,0:T(4,128)(2,1)}), bf16[32,4,1536]{2,1,0:T(4,128)(2,1)S(1)}, u32[]{:S(2)}, u32[]{:S(2)}) async-start(bf16[32,4,1536]{2,1,0:T(4,128)(2,1)} %reshape.471), calls=%async_computation.2 | async-start | bytes 786432 | tf_op jit(solution)/shard_map/all_to_all | solution.py:14
  176.2 151.5 %copy-start.2 = (bf16[1,4,1536]{2,1,0:T(4,128)(2,1)}, bf16[1,4,1536]{2,1,0:T(4,128)(2,1)S(1)}, u32[]{:S(2)}) copy-start(bf16[1,4,1536]{2,1,0:T(4,128)(2,1)S(1)} %fusion.75) | copy-start | bytes 36868
  177.1 16.2 %all-to-all-start.4 = ((bf16[32,4,1536]{2,1,0:T(4,128)(2,1)}), bf16[32,4,1536]{2,1,0:T(4,128)(2,1)S(1)}, u32[]{:S(2)}, u32[]{:S(2)}) async-start(bf16[32,4,1536]{2,1,0:T(4,128)(2,1)} %broadcast_in_dim.67), calls=%async_computation.4 | async-start | bytes 786432 | tf_op jit(solution)/shard_map/all_to_all | solution.py:14
  208.0 17.0 %all-to-all-start.5 = ((bf16[32,4,1536]{2,1,0:T(4,128)(2,1)}), bf16[32,4,1536]{2,1,0:T(4,128)(2,1)S(1)}, u32[]{:S(2)}, u32[]{:S(2)}) async-start(bf16[32,4,1536]{2,1,0:T(4,128)(2,1)} %reshape.474), calls=%async_computation.5 | async-start | bytes 786432 | tf_op jit(solution)/shard_map/all_to_all | solution.py:14
  234.1 16.0 %all-to-all-start.6 = ((bf16[32,4,1536]{2,1,0:T(4,128)(2,1)}), bf16[32,4,1536]{2,1,0:T(4,128)(2,1)S(1)}, u32[]{:S(2)}, u32[]{:S(2)}) async-start(bf16[32,4,1536]{2,1,0:T(4,128)(2,1)} %broadcast_in_dim.69), calls=%async_computation.6 | async-start | bytes 786432 | tf_op jit(solution)/shard_map/all_to_all | solution.py:14
  264.7 32.6 %copy-start = (bf16[1,1,1,4,6144]{4,3,2,1,0:T(4,128)(2,1)S(1)}, bf16[1,1,1,4,6144]{4,3,2,1,0:T(4,128)(2,1)}, u32[]{:S(2)}) copy-start(bf16[1,1,1,4,6144]{4,3,2,1,0:T(4,128)(2,1)} %param.5) | copy-start | bytes 147460
  264.7 32.7 %copy-start.1 = (bf16[1,1,1,128,256]{4,3,2,1,0:T(8,128)(2,1)S(1)}, bf16[1,1,1,128,256]{4,3,2,1,0:T(8,128)(2,1)}, u32[]{:S(2)}) copy-start(bf16[1,1,1,128,256]{4,3,2,1,0:T(8,128)(2,1)} %param.6) | copy-start | bytes 196612
  265.6 17.1 %all-to-all-start.7 = ((bf16[32,4,1536]{2,1,0:T(4,128)(2,1)}), bf16[32,4,1536]{2,1,0:T(4,128)(2,1)S(1)}, u32[]{:S(2)}, u32[]{:S(2)}) async-start(bf16[32,4,1536]{2,1,0:T(4,128)(2,1)} %reshape.477), calls=%async_computation.7 | async-start | bytes 786432 | tf_op jit(solution)/shard_map/all_to_all | solution.py:14
  290.9 6.4 %copy-start.3 = (bf16[4,1536]{1,0:T(4,128)(2,1)}, bf16[4,1536]{1,0:T(4,128)(2,1)S(1)}, u32[]{:S(2)}) copy-start(bf16[4,1536]{1,0:T(4,128)(2,1)S(1)} %subtract_convert_fusion.1) | copy-start | bytes 36868
  291.8 16.0 %all-to-all-start.8 = ((bf16[32,4,1536]{2,1,0:T(4,128)(2,1)}), bf16[32,4,1536]{2,1,0:T(4,128)(2,1)S(1)}, u32[]{:S(2)}, u32[]{:S(2)}) async-start(bf16[32,4,1536]{2,1,0:T(4,128)(2,1)} %broadcast_in_dim.71), calls=%async_computation.8 | async-start | bytes 786432 | tf_op jit(solution)/shard_map/all_to_all | solution.py:14
  322.8 21.0 %all-to-all-start.9 = ((bf16[32,4,1536]{2,1,0:T(4,128)(2,1)}), bf16[32,4,1536]{2,1,0:T(4,128)(2,1)S(1)}, u32[]{:S(2)}, u32[]{:S(2)}) async-start(bf16[32,4,1536]{2,1,0:T(4,128)(2,1)} %reshape.479), calls=%async_computation.9 | async-start | bytes 786432 | tf_op jit(solution)/shard_map/all_to_all | solution.py:14
  329.5 50.8 %collective-permute-start.6 = (bf16[128,1792]{1,0:T(8,128)(2,1)}, bf16[128,1792]{1,0:T(8,128)(2,1)}, u32[]{:S(2)}, u32[]{:S(2)}) collective-permute-start(bf16[128,1792]{1,0:T(8,128)(2,1)} %get-tuple-element.29), channel_id=1, source_target_pairs={{0,128},{128,256},{256,384},{384,0},{1,129},{129,257},{257,385},{3... | collective-permute-start | bytes 1376264 | tf_op jit(solution)/shard_map/ppermute | solution.py:23
  332.7 47.6 %collective-permute-start.8 = (bf16[128,1792]{1,0:T(8,128)(2,1)S(1)}, bf16[128,1792]{1,0:T(8,128)(2,1)}, u32[]{:S(2)}, u32[]{:S(2)}) collective-permute-start(bf16[128,1792]{1,0:T(8,128)(2,1)S(1)} %get-tuple-element.28), channel_id=1, source_target_pairs={{0,384},{128,0},{256,128},{384,256},{1,385},{129,1},{257,129},{385... | collective-permute-start | bytes 1376264 | tf_op jit(solution)/shard_map/ppermute | solution.py:23
  338.0 42.3 %collective-permute-start.7 = (bf16[128,1792]{1,0:T(8,128)(2,1)}, bf16[128,1792]{1,0:T(8,128)(2,1)S(1)}, u32[]{:S(2)}, u32[]{:S(2)}) collective-permute-start(bf16[128,1792]{1,0:T(8,128)(2,1)} %get-tuple-element.30), channel_id=1, source_target_pairs={{0,256},{128,384},{256,0},{384,128},{1,257},{129,385},{257,1},{385... | collective-permute-start | bytes 1376264 | tf_op jit(solution)/shard_map/ppermute | solution.py:23
  346.4 33.6 %all-to-all-start.10 = ((bf16[16,24,128]{2,1,0:T(8,128)(2,1)}), bf16[16,24,128]{2,1,0:T(8,128)(2,1)S(1)}, u32[]{:S(2)}, u32[]{:S(2)}) async-start(bf16[16,24,128]{2,1,0:T(8,128)(2,1)} %reshape.480), calls=%async_computation.10 | async-start | bytes 196608 | tf_op jit(solution)/shard_map/all_to_all | solution.py:14
  380.3 1.1 copy-start.4
  383.4 1.9 copy-start.6
  383.4 1.9 copy-start.7
Sparse Core Ops, SparseCore 0:
  65.0 83.1 all-gather.5

commit v5 on v4

--- a/solution.py
+++ b/solution.py
@@ -21,6 +21,11 @@
 def shifted(value, steps):
     count = lax.axis_size("pipe")
     return lax.ppermute(value, "pipe", [(i, (i + steps) % count) for i in range(count)])
+
+
+def across(stores, section):
+    source = (section + 2) % len(stores)
+    return lax.ppermute(stores[section], "pipe", [(source, section)])
 
 
 def choose(index, options):
@@ -97,27 +102,32 @@
     normed_blocks = jnp.swapaxes(exchange(normed_blocks, "dp", groups), 0, 1).reshape(-1, block)
     normed_all = lax.all_gather(normed_blocks, "tensor", axis=0, tiled=True)
 
-    u_f = u_own.astype(f32)
-    hidden = lax.all_gather((u_f * jax.nn.sigmoid(u_f)).astype(bf16), "dp", axis=0)
-    hidden = jnp.transpose(hidden.reshape(groups, parts, pipe, hidden_width), (2, 1, 0, 3))
-    hidden = hidden.reshape(pipe, tokens, hidden_width)
-    hidden = jnp.concatenate(
-        [choose(pipe_index, [hidden[(p - k) % pipe] for p in range(pipe)]) for k in range(pipe)], 0
-    )
-
-    stores, out_store = [None] * pipe, [None] * pipe
+    stores, out_store, opposite = [None] * pipe, [None] * pipe, []
     for section in reversed(range(pipe)):
         place = jnp.remainder(section - pipe_index, pipe)
-        if section == 1:
-            grad = after(grad, hidden)
+        if section == pipe - 2:
+            grad, u_late = lax.optimization_barrier((grad, u_own))
+            u_late = u_late.astype(f32)
+            hidden_own = (u_late * jax.nn.sigmoid(u_late)).astype(bf16)
+            hidden = lax.all_gather(hidden_own, "dp", axis=0)
         spread = jnp.broadcast_to(grad[None], (parts,) + grad.shape)
         grad_rows = exchange(spread, "tensor", parts).reshape(tokens, block)
+        if section < pipe - 2:
+            far = across(stores, 3 if section == 1 else 1)
+            opposite.append(far)
+            grad_rows = after(grad_rows, far)
         partials = lax.all_gather(dot_nt(grad_rows, choose(place, down_all)), "dp", axis=0)
         hidden_grad = jnp.sum(partials.astype(f32), axis=0)
         pre_grad = (hidden_grad * slope[section]).astype(bf16)
         stores[section] = jnp.concatenate([grad_rows, pre_grad], -1)
         pieces = dot_nt(pre_grad, choose(place, up_all)).reshape(parts, groups, block)
         pieces = exchange(pieces, "tensor", parts)
+        if section == pipe - 2:
+            pieces, hidden = lax.optimization_barrier((pieces, hidden))
+        if section == 1:
+            far = across(stores, 2)
+            opposite.append(far)
+            pieces = after(pieces, far)
         if section == pipe - 1:
             pieces = after(pieces, normed_all)
         normed_grad = jnp.sum(pieces.astype(f32), axis=0)
@@ -142,10 +152,17 @@
     input_grad = input_grad.reshape(1, 1, 1, own_rows, width)
 
     moved = [choose(pipe_index, stores)]
-    for k in range(1, pipe):
+    for k in (1, 3):
         chosen = choose(pipe_index, [stores[(p + k) % pipe] for p in range(pipe)])
         moved.append(shifted(chosen, k))
+    third, second, first = opposite
+    moved.insert(2, choose(pipe_index, [across(stores, 0), first, second, third]))
     moved = lax.optimization_barrier((moved, outs))[0]
+    hidden = jnp.transpose(hidden.reshape(groups, parts, pipe, hidden_width), (2, 1, 0, 3))
+    hidden = hidden.reshape(pipe, tokens, hidden_width)
+    hidden = jnp.concatenate(
+        [choose(pipe_index, [hidden[(p - k) % pipe] for p in range(pipe)]) for k in range(pipe)], 0
+    )
     down_grad = dot_tn(hidden, jnp.concatenate(moved, 0))[:, :block]
     pres = [piece[:, block:] for piece in moved]
     pres = [choose(pipe_index, [pres[(p - i) % pipe] for p in range(pipe)]) for i in range(pipe)]

time: 399 us -> 396 us (level)
  waiting for transfers between devices: 128 us -> 109 us
  starting transfers between devices: 113 us -> 130 us
    all_to_all x11, waiting for transfers between devices: 100 us -> 72.4 us  [exchange(): return lax.all_to_all(flat, axis, 0, 0).reshape(blocks.shape)]
    all_to_all x11, starting transfers between devices: 76.4 us -> 87.3 us  [exchange(): return lax.all_to_all(flat, axis, 0, 0).reshape(blocks.shape)]
    ppermute x0 -> x4, waiting for transfers between devices: none -> 8.66 us  [across(): return lax.ppermute(stores[section], 'pipe', [(source, section)])]
    ppermute x0 -> x4, starting transfers between devices: none -> 7.14 us  [across(): return lax.ppermute(stores[section], 'pipe', [(source, section)])]
    ppermute x9 -> x8, starting transfers between devices: 36.6 us -> 35.9 us  [shifted(): lax.ppermute(value, 'pipe', [(i, (i + steps) % count) for i in range(coun...]
    ppermute x9 -> x8, waiting for transfers between devices: 28 us -> 27.5 us  [shifted(): lax.ppermute(value, 'pipe', [(i, (i + steps) % count) for i in range(coun...]
  transfers between devices with their start and end apart: 21 -> 24, of which waited for: 12 -> 12; matrix products, arithmetic and copies ran while one was open for 5% -> 6% of each run, Pallas kernels for 0% -> 0%
where the time goes in v5:
time: 396 us; the launch traced here: 394 us
  starting transfers between devices  130 us (33%)
  waiting for transfers between devices  109 us (28%)
  blocking collectives  90.7 us (23%)
  matrix products  18.2 us (5%)
  other arithmetic  15.6 us (4%)
  local copies, waits for them, and re-layouts  15.6 us (4%)
  between operations  14.9 us (4%)
    all_to_all x11, starting transfers between devices, exchange(): return lax.all_to_all(flat, axis, 0, 0).reshape(blocks.shape)  87.3 us
    all_to_all x11, waiting for transfers between devices, exchange(): return lax.all_to_all(flat, axis, 0, 0).reshape(blocks.shape)  72.4 us
    all_gather x4, blocking collectives, per_device(): lax.all_gather(dot_nt(grad_rows, choose(place, down_all)), 'dp', axis=0)  60.4 us
    ppermute x8, starting transfers between devices, shifted(): lax.ppermute(value, 'pipe', [(i, (i + steps) % count) for i in range(coun...  35.9 us
    ppermute x8, waiting for transfers between devices, shifted(): lax.ppermute(value, 'pipe', [(i, (i + steps) % count) for i in range(coun...  27.5 us
    psum x3, blocking collectives, per_device(): lax.psum(jnp.sum(normed_grad * x_s, axis=-1, keepdims=True), 'dp') / width  24.2 us
    dot_general x8, matrix products, dot_nt(): lax.dot_general(left, right, (((1,), (1,)), ((), ())), preferred_element_...  14.9 us
    ppermute x4, waiting for transfers between devices, across(): return lax.ppermute(stores[section], 'pipe', [(source, section)])  8.66 us
  transfers between devices with their start and end apart: 24, of which 12 were waited for; matrix products, arithmetic and copies ran while one was open for 6% of the time, Pallas kernels for 0%

profile of v5, /device:TPU:1, one launch (start us, length us, event | category | flops | bytes accessed | tf_op | source)
XLA Modules:
  0.0 393.9 jit_solution(6451612723094159077)
XLA Ops:
  7.2 5.0 %collective-permute-start = (bf16[256,1536]{1,0:T(8,128)(2,1)}, bf16[256,1536]{1,0:T(8,128)(2,1)}, u32[]{:S(2)}, u32[]{:S(2)}) collective-permute-start(bf16[256,1536]{1,0:T(8,128)(2,1)} %bitcast.2), channel_id=1, source_target_pairs={{0,128},{128,256},{256,384},{384,0},{1,129},{129,257},{257,385},{3... | collective-permute-start | bytes 2359304 | tf_op jit(solution)/shard_map/ppermute | solution.py:23
  12.2 3.6 collective-permute-start.1
  15.8 1.0 multiply_reduce_fusion.1
  18.9 9.4 %all-to-all-start.3 = ((bf16[4,4,1536]{2,1,0:T(4,128)(2,1)}), bf16[4,4,1536]{2,1,0:T(4,128)(2,1)S(1)}, u32[]{:S(2)}, u32[]{:S(2)}) async-start(bf16[4,4,1536]{2,1,0:T(4,128)(2,1)} %fusion.80), calls=%async_computation.3 | async-start | bytes 98304 | tf_op jit(solution)/shard_map/all_to_all | solution.py:14
  28.3 0.9 reshape_squeeze.16
  29.4 0.9 reshape_squeeze.18
  30.3 0.9 reshape_squeeze.17
  32.2 4.2 %collective-permute-done = bf16[256,1536]{1,0:T(8,128)(2,1)} collective-permute-done((bf16[256,1536]{1,0:T(8,128)(2,1)}, bf16[256,1536]{1,0:T(8,128)(2,1)}, u32[]{:S(2)}, u32[]{:S(2)}) %collective-permute-start) | collective-permute-done | bytes 786464 | tf_op jit(solution)/shard_map/ppermute | solution.py:23
  36.5 16.2 %collective-permute-done.1 = bf16[1536,256]{1,0:T(8,128)(2,1)} collective-permute-done((bf16[1536,256]{1,0:T(8,128)(2,1)}, bf16[1536,256]{1,0:T(8,128)(2,1)}, u32[]{:S(2)}, u32[]{:S(2)}) %collective-permute-start.1) | collective-permute-done | bytes 786464 | tf_op jit(solution)/shard_map/ppermute | solution.py:23
  52.7 6.1 %all-to-all-start = ((bf16[16,89,128]{2,1,0:T(8,128)(2,1)}), bf16[16,89,128]{2,1,0:T(8,128)(2,1)S(1)}, u32[]{:S(2)}, u32[]{:S(2)}) async-start(bf16[16,89,128]{2,1,0:T(8,128)(2,1)} %bitcast.4), calls=%async_computation | async-start | bytes 786432 | tf_op jit(solution)/shard_map/all_to_all | solution.py:14
  58.8 5.4 %collective-permute-start.2 = (bf16[256,1536]{1,0:T(8,128)(2,1)}, bf16[256,1536]{1,0:T(8,128)(2,1)}, u32[]{:S(2)}, u32[]{:S(2)}) collective-permute-start(bf16[256,1536]{1,0:T(8,128)(2,1)} %bitcast.2), channel_id=1, source_target_pairs={{0,384},{128,0},{256,128},{384,256},{1,385},{129,1},{257,129},{385... | collective-permute-start | bytes 2359304 | tf_op jit(solution)/shard_map/ppermute | solution.py:23
  64.9 1.9 collective-permute-start.3
  66.8 6.1 %all-to-all-done = bf16[16,89,128]{2,1,0:T(8,128)(2,1)S(1)} async-done(((bf16[16,89,128]{2,1,0:T(8,128)(2,1)}), bf16[16,89,128]{2,1,0:T(8,128)(2,1)S(1)}, u32[]{:S(2)}, u32[]{:S(2)}) %all-to-all-start) | async-done | bytes 364576 | tf_op jit(solution)/shard_map/all_to_all | solution.py:14
  73.1 0.8 broadcast_in_dim.64
  73.9 12.9 %all-to-all-start.1 = ((bf16[32,4,1536]{2,1,0:T(4,128)(2,1)}), bf16[32,4,1536]{2,1,0:T(4,128)(2,1)S(1)}, u32[]{:S(2)}, u32[]{:S(2)}) async-start(bf16[32,4,1536]{2,1,0:T(4,128)(2,1)} %broadcast_in_dim.64), calls=%async_computation.1 | async-start | bytes 786432 | tf_op jit(solution)/shard_map/all_to_all | solution.py:14
  86.8 2.3 collective-permute-start.5
  89.2 5.1 %collective-permute-start.4 = (bf16[1536,256]{1,0:T(8,128)(2,1)}, bf16[1536,256]{1,0:T(8,128)(2,1)}, u32[]{:S(2)}, u32[]{:S(2)}) collective-permute-start(bf16[1536,256]{1,0:T(8,128)(2,1)} %collective-permute-done.1), channel_id=1, source_target_pairs={{0,384},{128,0},{256,128},{384,256},{1,385},{129,1},{257,129},{385... | collective-permute-start | bytes 2359304 | tf_op jit(solution)/shard_map/ppermute | solution.py:23
  95.7 5.8 %all-to-all-done.1 = bf16[32,4,1536]{2,1,0:T(4,128)(2,1)S(1)} async-done(((bf16[32,4,1536]{2,1,0:T(4,128)(2,1)}), bf16[32,4,1536]{2,1,0:T(4,128)(2,1)S(1)}, u32[]{:S(2)}, u32[]{:S(2)}) %all-to-all-start.1) | async-done | bytes 393248 | tf_op jit(solution)/shard_map/all_to_all | solution.py:14
  101.6 7.1 %collective-permute-done.2 = bf16[256,1536]{1,0:T(8,128)(2,1)} collective-permute-done((bf16[256,1536]{1,0:T(8,128)(2,1)}, bf16[256,1536]{1,0:T(8,128)(2,1)}, u32[]{:S(2)}, u32[]{:S(2)}) %collective-permute-start.2) | collective-permute-done | bytes 786464 | tf_op jit(solution)/shard_map/ppermute | solution.py:23
  108.6 1.8 convolution_convert_fusion.8
  110.4 29.5 %all-gather = bf16[512,256]{1,0:T(8,128)(2,1)S(1)} all-gather(bf16[128,256]{1,0:T(8,128)(2,1)S(1)} %convolution_convert_fusion.8), channel_id=2, replica_groups=mesh['pipe'=4,'tensor'=32,'dp'=4] {'dp'}, dimensions={0}, use_global_device_ids=true | all-gather | bytes 327680 | tf_op jit(solution)/shard_map/all_gather | solution.py:119
  140.0 1.8 convolution_convert_fusion.4
  142.7 12.9 %all-to-all-start.2 = ((bf16[32,4,1536]{2,1,0:T(4,128)(2,1)}), bf16[32,4,1536]{2,1,0:T(4,128)(2,1)S(1)}, u32[]{:S(2)}, u32[]{:S(2)}) async-start(bf16[32,4,1536]{2,1,0:T(4,128)(2,1)} %reshape.370), calls=%async_computation.2 | async-start | bytes 786432 | tf_op jit(solution)/shard_map/all_to_all | solution.py:14
  155.9 11.5 %all-to-all-done.2 = bf16[32,4,1536]{2,1,0:T(4,128)(2,1)S(1)} async-done(((bf16[32,4,1536]{2,1,0:T(4,128)(2,1)}), bf16[32,4,1536]{2,1,0:T(4,128)(2,1)S(1)}, u32[]{:S(2)}, u32[]{:S(2)}) %all-to-all-start.2) | async-done | bytes 393248 | tf_op jit(solution)/shard_map/all_to_all | solution.py:14
  167.7 8.4 %psum.21 = f32[4,1]{0,1:T(1,128)S(1)} all-reduce(f32[4,1]{0,1:T(1,128)S(1)} %bitcast.203), channel_id=1, replica_groups=mesh['pipe'=4,'tensor'=32,'dp'=4] {'dp'}, use_global_device_ids=true, to_apply=%region_4.5 | all-reduce | flops 4 | bytes 32 | tf_op jit(solution)/shard_map/psum | solution.py:138
  177.1 5.1 %all-to-all-start.4 = ((bf16[32,4,1536]{2,1,0:T(4,128)(2,1)}), bf16[32,4,1536]{2,1,0:T(4,128)(2,1)S(1)}, u32[]{:S(2)}, u32[]{:S(2)}) async-start(bf16[32,4,1536]{2,1,0:T(4,128)(2,1)} %broadcast_in_dim.66), calls=%async_computation.4 | async-start | bytes 786432 | tf_op jit(solution)/shard_map/all_to_all | solution.py:14
  182.3 10.6 %all-to-all-done.4 = bf16[32,4,1536]{2,1,0:T(4,128)(2,1)S(1)} async-done(((bf16[32,4,1536]{2,1,0:T(4,128)(2,1)}), bf16[32,4,1536]{2,1,0:T(4,128)(2,1)S(1)}, u32[]{:S(2)}, u32[]{:S(2)}) %all-to-all-start.4) | async-done | bytes 393248 | tf_op jit(solution)/shard_map/all_to_all | solution.py:14
  193.0 1.8 convolution_convert_fusion.7
  194.7 10.4 %all-gather.1 = bf16[512,256]{1,0:T(8,128)(2,1)S(1)} all-gather(bf16[128,256]{1,0:T(8,128)(2,1)S(1)} %convolution_convert_fusion.7), channel_id=3, replica_groups=mesh['pipe'=4,'tensor'=32,'dp'=4] {'dp'}, dimensions={0}, use_global_device_ids=true | all-gather | bytes 327680 | tf_op jit(solution)/shard_map/all_gather | solution.py:119
  205.2 1.8 convolution_convert_fusion.3
  207.9 4.9 %all-to-all-start.5 = ((bf16[32,4,1536]{2,1,0:T(4,128)(2,1)}), bf16[32,4,1536]{2,1,0:T(4,128)(2,1)S(1)}, u32[]{:S(2)}, u32[]{:S(2)}) async-start(bf16[32,4,1536]{2,1,0:T(4,128)(2,1)} %reshape.373), calls=%async_computation.5 | async-start | bytes 786432 | tf_op jit(solution)/shard_map/all_to_all | solution.py:14
  212.9 6.1 %all-gather.2 = bf16[512,256]{1,0:T(8,128)(2,1)S(1)} all-gather(bf16[128,256]{1,0:T(8,128)(2,1)S(1)} %fusion.73), channel_id=4, replica_groups=mesh['pipe'=4,'tensor'=32,'dp'=4] {'dp'}, dimensions={0}, use_global_device_ids=true | all-gather | bytes 327680 | tf_op jit(solution)/shard_map/all_gather | solution.py:112
  219.0 6.0 %all-to-all-done.5 = bf16[32,4,1536]{2,1,0:T(4,128)(2,1)S(1)} async-done(((bf16[32,4,1536]{2,1,0:T(4,128)(2,1)}), bf16[32,4,1536]{2,1,0:T(4,128)(2,1)S(1)}, u32[]{:S(2)}, u32[]{:S(2)}) %all-to-all-start.5) | async-done | bytes 393248 | tf_op jit(solution)/shard_map/all_to_all | solution.py:14
  225.3 7.9 %psum.22 = f32[4,1]{0,1:T(1,128)S(1)} all-reduce(f32[4,1]{0,1:T(1,128)S(1)} %bitcast.204), channel_id=1, replica_groups=mesh['pipe'=4,'tensor'=32,'dp'=4] {'dp'}, use_global_device_ids=true, to_apply=%region_8.9 | all-reduce | flops 4 | bytes 32 | tf_op jit(solution)/shard_map/psum | solution.py:138
  234.1 5.3 %all-to-all-start.6 = ((bf16[32,4,1536]{2,1,0:T(4,128)(2,1)}), bf16[32,4,1536]{2,1,0:T(4,128)(2,1)S(1)}, u32[]{:S(2)}, u32[]{:S(2)}) async-start(bf16[32,4,1536]{2,1,0:T(4,128)(2,1)} %broadcast_in_dim.68), calls=%async_computation.6 | async-start | bytes 786432 | tf_op jit(solution)/shard_map/all_to_all | solution.py:14
  241.0 9.1 %all-to-all-done.6 = bf16[32,4,1536]{2,1,0:T(4,128)(2,1)S(1)} async-done(((bf16[32,4,1536]{2,1,0:T(4,128)(2,1)}), bf16[32,4,1536]{2,1,0:T(4,128)(2,1)S(1)}, u32[]{:S(2)}, u32[]{:S(2)}) %all-to-all-start.6) | async-done | bytes 393248 | tf_op jit(solution)/shard_map/all_to_all | solution.py:14
  250.2 2.0 convolution_convert_fusion.6
  252.2 10.4 %all-gather.3 = bf16[512,256]{1,0:T(8,128)(2,1)S(1)} all-gather(bf16[128,256]{1,0:T(8,128)(2,1)S(1)} %convolution_convert_fusion.6), channel_id=5, replica_groups=mesh['pipe'=4,'tensor'=32,'dp'=4] {'dp'}, dimensions={0}, use_global_device_ids=true | all-gather | bytes 327680 | tf_op jit(solution)/shard_map/all_gather | solution.py:119
  262.7 2.1 convolution_convert_fusion.2
  265.6 8.1 %all-to-all-start.7 = ((bf16[32,4,1536]{2,1,0:T(4,128)(2,1)}), bf16[32,4,1536]{2,1,0:T(4,128)(2,1)S(1)}, u32[]{:S(2)}, u32[]{:S(2)}) async-start(bf16[32,4,1536]{2,1,0:T(4,128)(2,1)} %reshape.375), calls=%async_computation.7 | async-start | bytes 786432 | tf_op jit(solution)/shard_map/all_to_all | solution.py:14
  273.7 3.6 collective-permute-start.7
  277.4 8.6 %collective-permute-done.7 = bf16[128,1792]{1,0:T(8,128)(2,1)} collective-permute-done((bf16[128,1792]{1,0:T(8,128)(2,1)S(1)}, bf16[128,1792]{1,0:T(8,128)(2,1)}, u32[]{:S(2)}, u32[]{:S(2)}) %collective-permute-start.7) | collective-permute-done | bytes 458784 | tf_op jit(solution)/shard_map/ppermute | solution.py:28
  286.3 7.9 %psum.23 = f32[4,1]{0,1:T(1,128)S(1)} all-reduce(f32[4,1]{0,1:T(1,128)S(1)} %bitcast.205), channel_id=1, replica_groups=mesh['pipe'=4,'tensor'=32,'dp'=4] {'dp'}, use_global_device_ids=true, to_apply=%region_12.13 | all-reduce | flops 4 | bytes 32 | tf_op jit(solution)/shard_map/psum | solution.py:138
  295.2 8.9 %all-to-all-start.8 = ((bf16[32,4,1536]{2,1,0:T(4,128)(2,1)}), bf16[32,4,1536]{2,1,0:T(4,128)(2,1)S(1)}, u32[]{:S(2)}, u32[]{:S(2)}) async-start(bf16[32,4,1536]{2,1,0:T(4,128)(2,1)} %broadcast_in_dim.70), calls=%async_computation.8 | async-start | bytes 786432 | tf_op jit(solution)/shard_map/all_to_all | solution.py:14
  304.9 1.4 collective-permute-start.8
  307.1 1.4 fusion.82
  308.6 6.8 %all-to-all-done.8 = bf16[32,4,1536]{2,1,0:T(4,128)(2,1)S(1)} async-done(((bf16[32,4,1536]{2,1,0:T(4,128)(2,1)}), bf16[32,4,1536]{2,1,0:T(4,128)(2,1)S(1)}, u32[]{:S(2)}, u32[]{:S(2)}) %all-to-all-start.8) | async-done | bytes 393248 | tf_op jit(solution)/shard_map/all_to_all | solution.py:14
  315.5 1.8 convolution_convert_fusion.5
  317.3 10.0 %all-gather.4 = bf16[512,256]{1,0:T(8,128)(2,1)S(1)} all-gather(bf16[128,256]{1,0:T(8,128)(2,1)S(1)} %convolution_convert_fusion.5), channel_id=6, replica_groups=mesh['pipe'=4,'tensor'=32,'dp'=4] {'dp'}, dimensions={0}, use_global_device_ids=true | all-gather | bytes 327680 | tf_op jit(solution)/shard_map/all_gather | solution.py:119
  327.3 1.8 convolution_convert_fusion.1
  329.2 0.9 reshape.377
  330.0 4.8 %all-to-all-start.9 = ((bf16[32,4,1536]{2,1,0:T(4,128)(2,1)}), bf16[32,4,1536]{2,1,0:T(4,128)(2,1)S(1)}, u32[]{:S(2)}, u32[]{:S(2)}) async-start(bf16[32,4,1536]{2,1,0:T(4,128)(2,1)} %reshape.377), calls=%async_computation.9 | async-start | bytes 786432 | tf_op jit(solution)/shard_map/all_to_all | solution.py:14
  335.8 1.0 pad_maximum_fusion.3
  336.8 1.4 collective-permute-start.10
  338.2 1.3 select_select_fusion
  339.5 10.6 %collective-permute-start.9 = (bf16[128,1792]{1,0:T(8,128)(2,1)}, bf16[128,1792]{1,0:T(8,128)(2,1)}, u32[]{:S(2)}, u32[]{:S(2)}) collective-permute-start(bf16[128,1792]{1,0:T(8,128)(2,1)} %get-tuple-element.41), channel_id=1, source_target_pairs={{0,128},{128,256},{256,384},{384,0},{1,129},{129,257},{257,385},{3... | collective-permute-start | bytes 1376264 | tf_op jit(solution)/shard_map/ppermute | solution.py:23
  350.1 1.9 collective-permute-start.11
  353.2 8.8 %all-to-all-start.10 = ((bf16[16,24,128]{2,1,0:T(8,128)(2,1)}), bf16[16,24,128]{2,1,0:T(8,128)(2,1)S(1)}, u32[]{:S(2)}, u32[]{:S(2)}) async-start(bf16[16,24,128]{2,1,0:T(8,128)(2,1)} %reshape.378), calls=%async_computation.10 | async-start | bytes 196608 | tf_op jit(solution)/shard_map/all_to_all | solution.py:14
  362.0 1.2 select_select_fusion.1
  363.2 16.5 %all-to-all-done.10 = bf16[16,24,128]{2,1,0:T(8,128)(2,1)S(1)} async-done(((bf16[16,24,128]{2,1,0:T(8,128)(2,1)}), bf16[16,24,128]{2,1,0:T(8,128)(2,1)S(1)}, u32[]{:S(2)}, u32[]{:S(2)}) %all-to-all-start.10) | async-done | bytes 98336 | tf_op jit(solution)/shard_map/all_to_all | solution.py:14
  380.7 0.9 select_select_fusion.11
  382.0 1.8 fusion.1
  383.9 0.9 fusion.9
  385.6 1.5 fusion
  (143 shorter events, 20.1 us)
Async XLA Ops:
  7.2 29.3 %collective-permute-start = (bf16[256,1536]{1,0:T(8,128)(2,1)}, bf16[256,1536]{1,0:T(8,128)(2,1)}, u32[]{:S(2)}, u32[]{:S(2)}) collective-permute-start(bf16[256,1536]{1,0:T(8,128)(2,1)} %bitcast.2), channel_id=1, source_target_pairs={{0,128},{128,256},{256,384},{384,0},{1,129},{129,257},{257,385},{3... | collective-permute-start | bytes 2359304 | tf_op jit(solution)/shard_map/ppermute | solution.py:23
  12.2 40.5 %collective-permute-start.1 = (bf16[1536,256]{1,0:T(8,128)(2,1)}, bf16[1536,256]{1,0:T(8,128)(2,1)}, u32[]{:S(2)}, u32[]{:S(2)}) collective-permute-start(bf16[1536,256]{1,0:T(8,128)(2,1)} %bitcast.3), channel_id=1, source_target_pairs={{0,384},{128,0},{256,128},{384,256},{1,385},{129,1},{257,129},{385... | collective-permute-start | bytes 2359304 | tf_op jit(solution)/shard_map/ppermute | solution.py:23
  18.2 11.2 %copy-start.12 = (f32[4]{0:T(128)}, f32[4]{0:T(128)S(1)}, u32[]{:S(2)}) copy-start(f32[4]{0:T(128)S(1)} %get-tuple-element.35) | copy-start | bytes 52
  18.9 33.8 %all-to-all-start.3 = ((bf16[4,4,1536]{2,1,0:T(4,128)(2,1)}), bf16[4,4,1536]{2,1,0:T(4,128)(2,1)S(1)}, u32[]{:S(2)}, u32[]{:S(2)}) async-start(bf16[4,4,1536]{2,1,0:T(4,128)(2,1)} %fusion.80), calls=%async_computation.3 | async-start | bytes 98304 | tf_op jit(solution)/shard_map/all_to_all | solution.py:14
  52.7 20.2 %all-to-all-start = ((bf16[16,89,128]{2,1,0:T(8,128)(2,1)}), bf16[16,89,128]{2,1,0:T(8,128)(2,1)S(1)}, u32[]{:S(2)}, u32[]{:S(2)}) async-start(bf16[16,89,128]{2,1,0:T(8,128)(2,1)} %bitcast.4), calls=%async_computation | async-start | bytes 786432 | tf_op jit(solution)/shard_map/all_to_all | solution.py:14
  58.8 108.6 %all-gather.7.cloned.1.call-start = ((), (), s32[]{:S(2)}) async-start(), calls=%async_computation.11 | async-start | bytes 1622016 | tf_op jit(solution)/shard_map/all_gather | solution.py:103
  58.8 49.8 %collective-permute-start.2 = (bf16[256,1536]{1,0:T(8,128)(2,1)}, bf16[256,1536]{1,0:T(8,128)(2,1)}, u32[]{:S(2)}, u32[]{:S(2)}) collective-permute-start(bf16[256,1536]{1,0:T(8,128)(2,1)} %bitcast.2), channel_id=1, source_target_pairs={{0,384},{128,0},{256,128},{384,256},{1,385},{129,1},{257,129},{385... | collective-permute-start | bytes 2359304 | tf_op jit(solution)/shard_map/ppermute | solution.py:23
  64.9 43.7 %collective-permute-start.3 = (bf16[256,1536]{1,0:T(8,128)(2,1)}, bf16[256,1536]{1,0:T(8,128)(2,1)}, u32[]{:S(2)}, u32[]{:S(2)}) collective-permute-start(bf16[256,1536]{1,0:T(8,128)(2,1)} %collective-permute-done), channel_id=1, source_target_pairs={{0,128},{128,256},{256,384},{384,0},{1,129},{129,257},{257,385},{3... | collective-permute-start | bytes 2359304 | tf_op jit(solution)/shard_map/ppermute | solution.py:23
  73.9 27.5 %all-to-all-start.1 = ((bf16[32,4,1536]{2,1,0:T(4,128)(2,1)}), bf16[32,4,1536]{2,1,0:T(4,128)(2,1)S(1)}, u32[]{:S(2)}, u32[]{:S(2)}) async-start(bf16[32,4,1536]{2,1,0:T(4,128)(2,1)} %broadcast_in_dim.64), calls=%async_computation.1 | async-start | bytes 786432 | tf_op jit(solution)/shard_map/all_to_all | solution.py:14
  86.8 53.2 %collective-permute-start.5 = (bf16[1536,256]{1,0:T(8,128)(2,1)}, bf16[1536,256]{1,0:T(8,128)(2,1)}, u32[]{:S(2)}, u32[]{:S(2)}) collective-permute-start(bf16[1536,256]{1,0:T(8,128)(2,1)} %bitcast.3), channel_id=1, source_target_pairs={{0,128},{128,256},{256,384},{384,0},{1,129},{129,257},{257,385},{3... | collective-permute-start | bytes 2359304 | tf_op jit(solution)/shard_map/ppermute | solution.py:23
  89.2 50.9 %collective-permute-start.4 = (bf16[1536,256]{1,0:T(8,128)(2,1)}, bf16[1536,256]{1,0:T(8,128)(2,1)}, u32[]{:S(2)}, u32[]{:S(2)}) collective-permute-start(bf16[1536,256]{1,0:T(8,128)(2,1)} %collective-permute-done.1), channel_id=1, source_target_pairs={{0,384},{128,0},{256,128},{384,256},{1,385},{129,1},{257,129},{385... | collective-permute-start | bytes 2359304 | tf_op jit(solution)/shard_map/ppermute | solution.py:23
  142.7 24.6 %all-to-all-start.2 = ((bf16[32,4,1536]{2,1,0:T(4,128)(2,1)}), bf16[32,4,1536]{2,1,0:T(4,128)(2,1)S(1)}, u32[]{:S(2)}, u32[]{:S(2)}) async-start(bf16[32,4,1536]{2,1,0:T(4,128)(2,1)} %reshape.370), calls=%async_computation.2 | async-start | bytes 786432 | tf_op jit(solution)/shard_map/all_to_all | solution.py:14
  155.9 51.2 %copy-start.14 = (f32[4]{0:T(128)}, f32[4]{0:T(128)S(1)}, u32[]{:S(2)}) copy-start(f32[4]{0:T(128)S(1)} %multiply_multiply_fusion.3) | copy-start | bytes 52
  176.1 30.9 %copy-start.15 = (f32[4]{0:T(128)}, f32[4]{0:T(128)S(1)}, u32[]{:S(2)}) copy-start(f32[4]{0:T(128)S(1)} %multiply_bitcast_fusion.2) | copy-start | bytes 52
  177.1 15.8 %all-to-all-start.4 = ((bf16[32,4,1536]{2,1,0:T(4,128)(2,1)}), bf16[32,4,1536]{2,1,0:T(4,128)(2,1)S(1)}, u32[]{:S(2)}, u32[]{:S(2)}) async-start(bf16[32,4,1536]{2,1,0:T(4,128)(2,1)} %broadcast_in_dim.66), calls=%async_computation.4 | async-start | bytes 786432 | tf_op jit(solution)/shard_map/all_to_all | solution.py:14
  207.1 5.8 %copy-start.2 = (bf16[1,1,1,128,256]{4,3,2,1,0:T(8,128)(2,1)S(1)}, bf16[1,1,1,128,256]{4,3,2,1,0:T(8,128)(2,1)}, u32[]{:S(2)}) copy-start(bf16[1,1,1,128,256]{4,3,2,1,0:T(8,128)(2,1)} %param.6) | copy-start | bytes 196612
  207.9 17.1 %all-to-all-start.5 = ((bf16[32,4,1536]{2,1,0:T(4,128)(2,1)}), bf16[32,4,1536]{2,1,0:T(4,128)(2,1)S(1)}, u32[]{:S(2)}, u32[]{:S(2)}) async-start(bf16[32,4,1536]{2,1,0:T(4,128)(2,1)} %reshape.373), calls=%async_computation.5 | async-start | bytes 786432 | tf_op jit(solution)/shard_map/all_to_all | solution.py:14
  233.3 60.9 %copy-start.3 = (bf16[4,1536]{1,0:T(4,128)(2,1)}, bf16[4,1536]{1,0:T(4,128)(2,1)S(1)}, u32[]{:S(2)}) copy-start(bf16[4,1536]{1,0:T(4,128)(2,1)S(1)} %subtract_convert_fusion.2) | copy-start | bytes 36868
  234.1 16.0 %all-to-all-start.6 = ((bf16[32,4,1536]{2,1,0:T(4,128)(2,1)}), bf16[32,4,1536]{2,1,0:T(4,128)(2,1)S(1)}, u32[]{:S(2)}, u32[]{:S(2)}) async-start(bf16[32,4,1536]{2,1,0:T(4,128)(2,1)} %broadcast_in_dim.68), calls=%async_computation.6 | async-start | bytes 786432 | tf_op jit(solution)/shard_map/all_to_all | solution.py:14
  240.3 9.9 %collective-permute-start.6 = (bf16[128,1792]{1,0:T(8,128)(2,1)}, bf16[128,1792]{1,0:T(8,128)(2,1)S(1)}, u32[]{:S(2)}, u32[]{:S(2)}) collective-permute-start(bf16[128,1792]{1,0:T(8,128)(2,1)} %pad_maximum_fusion), channel_id=1, source_target_pairs={{128,384},{129,385},{130,386},{131,387},{132,388},{133,389},{134,3... | collective-permute-start | bytes 1376264 | tf_op jit(solution)/shard_map/ppermute | solution.py:28
  265.6 20.4 %all-to-all-start.7 = ((bf16[32,4,1536]{2,1,0:T(4,128)(2,1)}), bf16[32,4,1536]{2,1,0:T(4,128)(2,1)S(1)}, u32[]{:S(2)}, u32[]{:S(2)}) async-start(bf16[32,4,1536]{2,1,0:T(4,128)(2,1)} %reshape.375), calls=%async_computation.7 | async-start | bytes 786432 | tf_op jit(solution)/shard_map/all_to_all | solution.py:14
  273.7 32.6 %copy-start = (bf16[1,1,1,4,6144]{4,3,2,1,0:T(4,128)(2,1)S(1)}, bf16[1,1,1,4,6144]{4,3,2,1,0:T(4,128)(2,1)}, u32[]{:S(2)}) copy-start(bf16[1,1,1,4,6144]{4,3,2,1,0:T(4,128)(2,1)} %param.5) | copy-start | bytes 147460
  273.7 12.3 %collective-permute-start.7 = (bf16[128,1792]{1,0:T(8,128)(2,1)S(1)}, bf16[128,1792]{1,0:T(8,128)(2,1)}, u32[]{:S(2)}, u32[]{:S(2)}) collective-permute-start(bf16[128,1792]{1,0:T(8,128)(2,1)S(1)} %pad_maximum_fusion.1), channel_id=1, source_target_pairs={{0,256},{1,257},{2,258},{3,259},{4,260},{5,261},{6,262},{7,263},{8... | collective-permute-start | bytes 1376264 | tf_op jit(solution)/shard_map/ppermute | solution.py:28
  294.3 0.9 copy-start.5
  295.2 20.3 %all-to-all-start.8 = ((bf16[32,4,1536]{2,1,0:T(4,128)(2,1)}), bf16[32,4,1536]{2,1,0:T(4,128)(2,1)S(1)}, u32[]{:S(2)}, u32[]{:S(2)}) async-start(bf16[32,4,1536]{2,1,0:T(4,128)(2,1)} %broadcast_in_dim.70), calls=%async_computation.8 | async-start | bytes 786432 | tf_op jit(solution)/shard_map/all_to_all | solution.py:14
  304.9 10.6 %collective-permute-start.8 = (bf16[128,1792]{1,0:T(8,128)(2,1)}, bf16[128,1792]{1,0:T(8,128)(2,1)}, u32[]{:S(2)}, u32[]{:S(2)}) collective-permute-start(bf16[128,1792]{1,0:T(8,128)(2,1)} %pad_maximum_fusion.2), channel_id=1, source_target_pairs={{384,128},{385,129},{386,130},{387,131},{388,132},{389,133},{390,1... | collective-permute-start | bytes 1376264 | tf_op jit(solution)/shard_map/ppermute | solution.py:28
  330.0 22.0 %all-to-all-start.9 = ((bf16[32,4,1536]{2,1,0:T(4,128)(2,1)}), bf16[32,4,1536]{2,1,0:T(4,128)(2,1)S(1)}, u32[]{:S(2)}, u32[]{:S(2)}) async-start(bf16[32,4,1536]{2,1,0:T(4,128)(2,1)} %reshape.377), calls=%async_computation.9 | async-start | bytes 786432 | tf_op jit(solution)/shard_map/all_to_all | solution.py:14
  336.8 15.4 %copy-start.4 = (bf16[4,1536]{1,0:T(4,128)(2,1)S(1)}, bf16[4,1536]{1,0:T(4,128)(2,1)}, u32[]{:S(2)}) copy-start(bf16[4,1536]{1,0:T(4,128)(2,1)} %copy-done.3) | copy-start | bytes 36868
  336.8 15.4 %copy-start.6 = (bf16[4,1536]{1,0:T(4,128)(2,1)S(1)}, bf16[4,1536]{1,0:T(4,128)(2,1)}, u32[]{:S(2)}) copy-start(bf16[4,1536]{1,0:T(4,128)(2,1)} %copy-done.5) | copy-start | bytes 36868
  336.8 15.4 %copy-start.11 = (bf16[1,4,1536]{2,1,0:T(4,128)(2,1)S(1)}, bf16[1,4,1536]{2,1,0:T(4,128)(2,1)}, u32[]{:S(2)}) copy-start(bf16[1,4,1536]{2,1,0:T(4,128)(2,1)} %fusion.82) | copy-start | bytes 36868
  336.8 25.3 %collective-permute-start.10 = (bf16[128,1792]{1,0:T(8,128)(2,1)}, bf16[128,1792]{1,0:T(8,128)(2,1)}, u32[]{:S(2)}, u32[]{:S(2)}) collective-permute-start(bf16[128,1792]{1,0:T(8,128)(2,1)} %get-tuple-element.46), channel_id=1, source_target_pairs={{256,0},{257,1},{258,2},{259,3},{260,4},{261,5},{262,6},{263,7},{2... | collective-permute-start | bytes 1376264 | tf_op jit(solution)/shard_map/ppermute | solution.py:28
  339.5 41.2 %collective-permute-start.9 = (bf16[128,1792]{1,0:T(8,128)(2,1)}, bf16[128,1792]{1,0:T(8,128)(2,1)}, u32[]{:S(2)}, u32[]{:S(2)}) collective-permute-start(bf16[128,1792]{1,0:T(8,128)(2,1)} %get-tuple-element.41), channel_id=1, source_target_pairs={{0,128},{128,256},{256,384},{384,0},{1,129},{129,257},{257,385},{3... | collective-permute-start | bytes 1376264 | tf_op jit(solution)/shard_map/ppermute | solution.py:23
  350.1 30.6 %collective-permute-start.11 = (bf16[128,1792]{1,0:T(8,128)(2,1)}, bf16[128,1792]{1,0:T(8,128)(2,1)}, u32[]{:S(2)}, u32[]{:S(2)}) collective-permute-start(bf16[128,1792]{1,0:T(8,128)(2,1)} %get-tuple-element.40), channel_id=1, source_target_pairs={{0,384},{128,0},{256,128},{384,256},{1,385},{129,1},{257,129},{385... | collective-permute-start | bytes 1376264 | tf_op jit(solution)/shard_map/ppermute | solution.py:23
  352.5 27.6 %copy-start.1 = (f32[4,4,1,1536]{3,2,1,0:T(1,128)S(1)}, f32[4,4,1,1536]{3,2,1,0:T(1,128)}, u32[]{:S(2)}) copy-start(f32[4,4,1,1536]{3,2,1,0:T(1,128)} %reshape.386) | copy-start | bytes 294916
  353.2 26.5 %all-to-all-start.10 = ((bf16[16,24,128]{2,1,0:T(8,128)(2,1)}), bf16[16,24,128]{2,1,0:T(8,128)(2,1)S(1)}, u32[]{:S(2)}, u32[]{:S(2)}) async-start(bf16[16,24,128]{2,1,0:T(8,128)(2,1)} %reshape.378), calls=%async_computation.10 | async-start | bytes 196608 | tf_op jit(solution)/shard_map/all_to_all | solution.py:14
  363.2 18.8 %copy-start.7 = (bf16[128,256]{1,0:T(8,128)(2,1)S(1)}, bf16[128,256]{1,0:T(8,128)(2,1)}, u32[]{:S(2)}) copy-start(bf16[128,256]{1,0:T(8,128)(2,1)} %get-tuple-element.48) | copy-start | bytes 196612
  363.2 18.8 %copy-start.8 = (bf16[128,256]{1,0:T(8,128)(2,1)S(1)}, bf16[128,256]{1,0:T(8,128)(2,1)}, u32[]{:S(2)}) copy-start(bf16[128,256]{1,0:T(8,128)(2,1)} %get-tuple-element.49) | copy-start | bytes 196612
  363.2 18.8 %copy-start.9 = (bf16[128,256]{1,0:T(8,128)(2,1)S(1)}, bf16[128,256]{1,0:T(8,128)(2,1)}, u32[]{:S(2)}) copy-start(bf16[128,256]{1,0:T(8,128)(2,1)} %get-tuple-element.50) | copy-start | bytes 196612
  363.2 18.8 %copy-start.10 = (bf16[128,256]{1,0:T(8,128)(2,1)S(1)}, bf16[128,256]{1,0:T(8,128)(2,1)}, u32[]{:S(2)}) copy-start(bf16[128,256]{1,0:T(8,128)(2,1)} %get-tuple-element.51) | copy-start | bytes 196612
  383.8 1.0 copy-start.13
  383.8 1.0 copy-start.16
  383.9 1.7 copy-start.17
Sparse Core Ops, SparseCore 0:
  65.0 82.8 all-gather.6

commit v6 on v5

--- a/solution.py
+++ b/solution.py
@@ -141,6 +141,7 @@
         out_store[section] = grad
 
     outs = jnp.stack([jnp.stack(out_store), jnp.broadcast_to(grad, (pipe,) + grad.shape)], 2)
+    unsent = outs
     outs = exchange(outs, ("pipe", "dp"), pipe * groups)
     outs = outs.reshape(own_rows, groups, 2, block)
     whole = outs[:, :, 0].reshape(own_rows, width)
@@ -157,7 +158,7 @@
         moved.append(shifted(chosen, k))
     third, second, first = opposite
     moved.insert(2, choose(pipe_index, [across(stores, 0), first, second, third]))
-    moved = lax.optimization_barrier((moved, outs))[0]
+    moved = lax.optimization_barrier((moved, unsent))[0]
     hidden = jnp.transpose(hidden.reshape(groups, parts, pipe, hidden_width), (2, 1, 0, 3))
     hidden = hidden.reshape(pipe, tokens, hidden_width)
     hidden = jnp.concatenate(

time: 396 us -> 393 us (level)
  waiting for transfers between devices: 109 us -> 98.6 us
    all_to_all x11, waiting for transfers between devices: 72.4 us -> 57.3 us  [exchange(): return lax.all_to_all(flat, axis, 0, 0).reshape(blocks.shape)]
    ppermute x8, waiting for transfers between devices: 27.5 us -> 33.1 us  [shifted(): lax.ppermute(value, 'pipe', [(i, (i + steps) % count) for i in range(coun...]
  transfers between devices with their start and end apart: 24 -> 24, of which waited for: 12 -> 14; matrix products, arithmetic and copies ran while one was open for 6% -> 8% of each run, Pallas kernels for 0% -> 0%
where the time goes in v6:
time: 393 us; the launch traced here: 387 us
  starting transfers between devices  133 us (34%)
  waiting for transfers between devices  98.6 us (25%)
  blocking collectives  90.4 us (23%)
  matrix products  18.1 us (5%)
  local copies, waits for them, and re-layouts  16.3 us (4%)
  other arithmetic  15.7 us (4%)
  between operations  14.8 us (4%)
    all_to_all x11, starting transfers between devices, exchange(): return lax.all_to_all(flat, axis, 0, 0).reshape(blocks.shape)  89.7 us
    all_gather x4, blocking collectives, per_device(): lax.all_gather(dot_nt(grad_rows, choose(place, down_all)), 'dp', axis=0)  60.4 us
    all_to_all x11, waiting for transfers between devices, exchange(): return lax.all_to_all(flat, axis, 0, 0).reshape(blocks.shape)  57.3 us
    ppermute x8, starting transfers between devices, shifted(): lax.ppermute(value, 'pipe', [(i, (i + steps) % count) for i in range(coun...  36.7 us
    ppermute x8, waiting for transfers between devices, shifted(): lax.ppermute(value, 'pipe', [(i, (i + steps) % count) for i in range(coun...  33.1 us
    psum x3, blocking collectives, per_device(): lax.psum(jnp.sum(normed_grad * x_s, axis=-1, keepdims=True), 'dp') / width  23.9 us
    dot_general x8, matrix products, dot_nt(): lax.dot_general(left, right, (((1,), (1,)), ((), ())), preferred_element_...  14.9 us
    ppermute x4, waiting for transfers between devices, across(): return lax.ppermute(stores[section], 'pipe', [(source, section)])  8.24 us
  transfers between devices with their start and end apart: 24, of which 14 were waited for; matrix products, arithmetic and copies ran while one was open for 8% of the time, Pallas kernels for 0%

profile of v6, /device:TPU:1, one launch (start us, length us, event | category | flops | bytes accessed | tf_op | source)
XLA Modules:
  0.0 387.2 jit_solution(12964303688954360744)
XLA Ops:
  7.2 5.0 %collective-permute-start = (bf16[256,1536]{1,0:T(8,128)(2,1)}, bf16[256,1536]{1,0:T(8,128)(2,1)}, u32[]{:S(2)}, u32[]{:S(2)}) collective-permute-start(bf16[256,1536]{1,0:T(8,128)(2,1)} %bitcast.2), channel_id=1, source_target_pairs={{0,128},{128,256},{256,384},{384,0},{1,129},{129,257},{257,385},{3... | collective-permute-start | bytes 2359304 | tf_op jit(solution)/shard_map/ppermute | solution.py:23
  12.2 3.6 collective-permute-start.1
  15.8 1.0 multiply_reduce_fusion.1
  18.9 9.4 %all-to-all-start.3 = ((bf16[4,4,1536]{2,1,0:T(4,128)(2,1)}), bf16[4,4,1536]{2,1,0:T(4,128)(2,1)S(1)}, u32[]{:S(2)}, u32[]{:S(2)}) async-start(bf16[4,4,1536]{2,1,0:T(4,128)(2,1)} %fusion.80), calls=%async_computation.3 | async-start | bytes 98304 | tf_op jit(solution)/shard_map/all_to_all | solution.py:14
  28.3 0.9 reshape_squeeze.16
  29.4 0.9 reshape_squeeze.18
  30.4 0.9 reshape_squeeze.17
  32.3 4.2 %collective-permute-done = bf16[256,1536]{1,0:T(8,128)(2,1)} collective-permute-done((bf16[256,1536]{1,0:T(8,128)(2,1)}, bf16[256,1536]{1,0:T(8,128)(2,1)}, u32[]{:S(2)}, u32[]{:S(2)}) %collective-permute-start) | collective-permute-done | bytes 786464 | tf_op jit(solution)/shard_map/ppermute | solution.py:23
  36.5 16.2 %collective-permute-done.1 = bf16[1536,256]{1,0:T(8,128)(2,1)} collective-permute-done((bf16[1536,256]{1,0:T(8,128)(2,1)}, bf16[1536,256]{1,0:T(8,128)(2,1)}, u32[]{:S(2)}, u32[]{:S(2)}) %collective-permute-start.1) | collective-permute-done | bytes 786464 | tf_op jit(solution)/shard_map/ppermute | solution.py:23
  52.7 6.1 %all-to-all-start = ((bf16[16,89,128]{2,1,0:T(8,128)(2,1)}), bf16[16,89,128]{2,1,0:T(8,128)(2,1)S(1)}, u32[]{:S(2)}, u32[]{:S(2)}) async-start(bf16[16,89,128]{2,1,0:T(8,128)(2,1)} %bitcast.4), calls=%async_computation | async-start | bytes 786432 | tf_op jit(solution)/shard_map/all_to_all | solution.py:14
  58.8 5.4 %collective-permute-start.2 = (bf16[256,1536]{1,0:T(8,128)(2,1)}, bf16[256,1536]{1,0:T(8,128)(2,1)}, u32[]{:S(2)}, u32[]{:S(2)}) collective-permute-start(bf16[256,1536]{1,0:T(8,128)(2,1)} %bitcast.2), channel_id=1, source_target_pairs={{0,384},{128,0},{256,128},{384,256},{1,385},{129,1},{257,129},{385... | collective-permute-start | bytes 2359304 | tf_op jit(solution)/shard_map/ppermute | solution.py:23
  64.9 1.9 collective-permute-start.3
  66.8 6.1 %all-to-all-done = bf16[16,89,128]{2,1,0:T(8,128)(2,1)S(1)} async-done(((bf16[16,89,128]{2,1,0:T(8,128)(2,1)}), bf16[16,89,128]{2,1,0:T(8,128)(2,1)S(1)}, u32[]{:S(2)}, u32[]{:S(2)}) %all-to-all-start) | async-done | bytes 364576 | tf_op jit(solution)/shard_map/all_to_all | solution.py:14
  73.9 12.9 %all-to-all-start.1 = ((bf16[32,4,1536]{2,1,0:T(4,128)(2,1)}), bf16[32,4,1536]{2,1,0:T(4,128)(2,1)S(1)}, u32[]{:S(2)}, u32[]{:S(2)}) async-start(bf16[32,4,1536]{2,1,0:T(4,128)(2,1)} %broadcast_in_dim.64), calls=%async_computation.1 | async-start | bytes 786432 | tf_op jit(solution)/shard_map/all_to_all | solution.py:14
  86.8 2.3 collective-permute-start.5
  89.2 5.1 %collective-permute-start.4 = (bf16[1536,256]{1,0:T(8,128)(2,1)}, bf16[1536,256]{1,0:T(8,128)(2,1)}, u32[]{:S(2)}, u32[]{:S(2)}) collective-permute-start(bf16[1536,256]{1,0:T(8,128)(2,1)} %collective-permute-done.1), channel_id=1, source_target_pairs={{0,384},{128,0},{256,128},{384,256},{1,385},{129,1},{257,129},{385... | collective-permute-start | bytes 2359304 | tf_op jit(solution)/shard_map/ppermute | solution.py:23
  95.7 5.3 %all-to-all-done.1 = bf16[32,4,1536]{2,1,0:T(4,128)(2,1)S(1)} async-done(((bf16[32,4,1536]{2,1,0:T(4,128)(2,1)}), bf16[32,4,1536]{2,1,0:T(4,128)(2,1)S(1)}, u32[]{:S(2)}, u32[]{:S(2)}) %all-to-all-start.1) | async-done | bytes 393248 | tf_op jit(solution)/shard_map/all_to_all | solution.py:14
  101.1 7.5 %collective-permute-done.2 = bf16[256,1536]{1,0:T(8,128)(2,1)} collective-permute-done((bf16[256,1536]{1,0:T(8,128)(2,1)}, bf16[256,1536]{1,0:T(8,128)(2,1)}, u32[]{:S(2)}, u32[]{:S(2)}) %collective-permute-start.2) | collective-permute-done | bytes 786464 | tf_op jit(solution)/shard_map/ppermute | solution.py:23
  108.6 1.8 convolution_convert_fusion.8
  110.4 29.5 %all-gather = bf16[512,256]{1,0:T(8,128)(2,1)S(1)} all-gather(bf16[128,256]{1,0:T(8,128)(2,1)S(1)} %convolution_convert_fusion.8), channel_id=2, replica_groups=mesh['pipe'=4,'tensor'=32,'dp'=4] {'dp'}, dimensions={0}, use_global_device_ids=true | all-gather | bytes 327680 | tf_op jit(solution)/shard_map/all_gather | solution.py:119
  140.0 1.8 convolution_convert_fusion.4
  142.7 12.9 %all-to-all-start.2 = ((bf16[32,4,1536]{2,1,0:T(4,128)(2,1)}), bf16[32,4,1536]{2,1,0:T(4,128)(2,1)S(1)}, u32[]{:S(2)}, u32[]{:S(2)}) async-start(bf16[32,4,1536]{2,1,0:T(4,128)(2,1)} %reshape.370), calls=%async_computation.2 | async-start | bytes 786432 | tf_op jit(solution)/shard_map/all_to_all | solution.py:14
  155.9 11.5 %all-to-all-done.2 = bf16[32,4,1536]{2,1,0:T(4,128)(2,1)S(1)} async-done(((bf16[32,4,1536]{2,1,0:T(4,128)(2,1)}), bf16[32,4,1536]{2,1,0:T(4,128)(2,1)S(1)}, u32[]{:S(2)}, u32[]{:S(2)}) %all-to-all-start.2) | async-done | bytes 393248 | tf_op jit(solution)/shard_map/all_to_all | solution.py:14
  167.7 8.4 %psum.21 = f32[4,1]{0,1:T(1,128)S(1)} all-reduce(f32[4,1]{0,1:T(1,128)S(1)} %bitcast.203), channel_id=1, replica_groups=mesh['pipe'=4,'tensor'=32,'dp'=4] {'dp'}, use_global_device_ids=true, to_apply=%region_4.5 | all-reduce | flops 4 | bytes 32 | tf_op jit(solution)/shard_map/psum | solution.py:138
  177.1 5.1 %all-to-all-start.4 = ((bf16[32,4,1536]{2,1,0:T(4,128)(2,1)}), bf16[32,4,1536]{2,1,0:T(4,128)(2,1)S(1)}, u32[]{:S(2)}, u32[]{:S(2)}) async-start(bf16[32,4,1536]{2,1,0:T(4,128)(2,1)} %broadcast_in_dim.66), calls=%async_computation.4 | async-start | bytes 786432 | tf_op jit(solution)/shard_map/all_to_all | solution.py:14
  182.3 10.6 %all-to-all-done.4 = bf16[32,4,1536]{2,1,0:T(4,128)(2,1)S(1)} async-done(((bf16[32,4,1536]{2,1,0:T(4,128)(2,1)}), bf16[32,4,1536]{2,1,0:T(4,128)(2,1)S(1)}, u32[]{:S(2)}, u32[]{:S(2)}) %all-to-all-start.4) | async-done | bytes 393248 | tf_op jit(solution)/shard_map/all_to_all | solution.py:14
  193.0 1.8 convolution_convert_fusion.7
  194.7 10.4 %all-gather.1 = bf16[512,256]{1,0:T(8,128)(2,1)S(1)} all-gather(bf16[128,256]{1,0:T(8,128)(2,1)S(1)} %convolution_convert_fusion.7), channel_id=3, replica_groups=mesh['pipe'=4,'tensor'=32,'dp'=4] {'dp'}, dimensions={0}, use_global_device_ids=true | all-gather | bytes 327680 | tf_op jit(solution)/shard_map/all_gather | solution.py:119
  205.2 1.8 convolution_convert_fusion.3
  207.9 4.9 %all-to-all-start.5 = ((bf16[32,4,1536]{2,1,0:T(4,128)(2,1)}), bf16[32,4,1536]{2,1,0:T(4,128)(2,1)S(1)}, u32[]{:S(2)}, u32[]{:S(2)}) async-start(bf16[32,4,1536]{2,1,0:T(4,128)(2,1)} %reshape.373), calls=%async_computation.5 | async-start | bytes 786432 | tf_op jit(solution)/shard_map/all_to_all | solution.py:14
  212.9 6.1 %all-gather.2 = bf16[512,256]{1,0:T(8,128)(2,1)S(1)} all-gather(bf16[128,256]{1,0:T(8,128)(2,1)S(1)} %fusion.73), channel_id=4, replica_groups=mesh['pipe'=4,'tensor'=32,'dp'=4] {'dp'}, dimensions={0}, use_global_device_ids=true | all-gather | bytes 327680 | tf_op jit(solution)/shard_map/all_gather | solution.py:112
  219.0 6.0 %all-to-all-done.5 = bf16[32,4,1536]{2,1,0:T(4,128)(2,1)S(1)} async-done(((bf16[32,4,1536]{2,1,0:T(4,128)(2,1)}), bf16[32,4,1536]{2,1,0:T(4,128)(2,1)S(1)}, u32[]{:S(2)}, u32[]{:S(2)}) %all-to-all-start.5) | async-done | bytes 393248 | tf_op jit(solution)/shard_map/all_to_all | solution.py:14
  225.3 7.9 %psum.22 = f32[4,1]{0,1:T(1,128)S(1)} all-reduce(f32[4,1]{0,1:T(1,128)S(1)} %bitcast.204), channel_id=1, replica_groups=mesh['pipe'=4,'tensor'=32,'dp'=4] {'dp'}, use_global_device_ids=true, to_apply=%region_8.9 | all-reduce | flops 4 | bytes 32 | tf_op jit(solution)/shard_map/psum | solution.py:138
  234.1 5.3 %all-to-all-start.6 = ((bf16[32,4,1536]{2,1,0:T(4,128)(2,1)}), bf16[32,4,1536]{2,1,0:T(4,128)(2,1)S(1)}, u32[]{:S(2)}, u32[]{:S(2)}) async-start(bf16[32,4,1536]{2,1,0:T(4,128)(2,1)} %broadcast_in_dim.68), calls=%async_computation.6 | async-start | bytes 786432 | tf_op jit(solution)/shard_map/all_to_all | solution.py:14
  241.0 9.1 %all-to-all-done.6 = bf16[32,4,1536]{2,1,0:T(4,128)(2,1)S(1)} async-done(((bf16[32,4,1536]{2,1,0:T(4,128)(2,1)}), bf16[32,4,1536]{2,1,0:T(4,128)(2,1)S(1)}, u32[]{:S(2)}, u32[]{:S(2)}) %all-to-all-start.6) | async-done | bytes 393248 | tf_op jit(solution)/shard_map/all_to_all | solution.py:14
  250.2 2.0 convolution_convert_fusion.6
  252.2 10.4 %all-gather.3 = bf16[512,256]{1,0:T(8,128)(2,1)S(1)} all-gather(bf16[128,256]{1,0:T(8,128)(2,1)S(1)} %convolution_convert_fusion.6), channel_id=5, replica_groups=mesh['pipe'=4,'tensor'=32,'dp'=4] {'dp'}, dimensions={0}, use_global_device_ids=true | all-gather | bytes 327680 | tf_op jit(solution)/shard_map/all_gather | solution.py:119
  262.7 2.1 convolution_convert_fusion.2
  265.6 8.1 %all-to-all-start.7 = ((bf16[32,4,1536]{2,1,0:T(4,128)(2,1)}), bf16[32,4,1536]{2,1,0:T(4,128)(2,1)S(1)}, u32[]{:S(2)}, u32[]{:S(2)}) async-start(bf16[32,4,1536]{2,1,0:T(4,128)(2,1)} %reshape.375), calls=%async_computation.7 | async-start | bytes 786432 | tf_op jit(solution)/shard_map/all_to_all | solution.py:14
  274.5 3.5 collective-permute-start.7
  278.7 8.2 %collective-permute-done.7 = bf16[128,1792]{1,0:T(8,128)(2,1)} collective-permute-done((bf16[128,1792]{1,0:T(8,128)(2,1)}, bf16[128,1792]{1,0:T(8,128)(2,1)}, u32[]{:S(2)}, u32[]{:S(2)}) %collective-permute-start.7) | collective-permute-done | bytes 458784 | tf_op jit(solution)/shard_map/ppermute | solution.py:28
  287.2 7.6 %psum.23 = f32[4,1]{0,1:T(1,128)S(1)} all-reduce(f32[4,1]{0,1:T(1,128)S(1)} %bitcast.205), channel_id=1, replica_groups=mesh['pipe'=4,'tensor'=32,'dp'=4] {'dp'}, use_global_device_ids=true, to_apply=%region_12.13 | all-reduce | flops 4 | bytes 32 | tf_op jit(solution)/shard_map/psum | solution.py:138
  295.8 9.2 %all-to-all-start.8 = ((bf16[32,4,1536]{2,1,0:T(4,128)(2,1)}), bf16[32,4,1536]{2,1,0:T(4,128)(2,1)S(1)}, u32[]{:S(2)}, u32[]{:S(2)}) async-start(bf16[32,4,1536]{2,1,0:T(4,128)(2,1)} %broadcast_in_dim.70), calls=%async_computation.8 | async-start | bytes 786432 | tf_op jit(solution)/shard_map/all_to_all | solution.py:14
  305.0 1.4 fusion.82
  307.4 1.4 collective-permute-start.8
  309.1 7.3 %all-to-all-done.8 = bf16[32,4,1536]{2,1,0:T(4,128)(2,1)S(1)} async-done(((bf16[32,4,1536]{2,1,0:T(4,128)(2,1)}), bf16[32,4,1536]{2,1,0:T(4,128)(2,1)S(1)}, u32[]{:S(2)}, u32[]{:S(2)}) %all-to-all-start.8) | async-done | bytes 393248 | tf_op jit(solution)/shard_map/all_to_all | solution.py:14
  316.4 1.8 convolution_convert_fusion.5
  318.2 10.0 %all-gather.4 = bf16[512,256]{1,0:T(8,128)(2,1)S(1)} all-gather(bf16[128,256]{1,0:T(8,128)(2,1)S(1)} %convolution_convert_fusion.5), channel_id=6, replica_groups=mesh['pipe'=4,'tensor'=32,'dp'=4] {'dp'}, dimensions={0}, use_global_device_ids=true | all-gather | bytes 327680 | tf_op jit(solution)/shard_map/all_gather | solution.py:119
  328.3 1.0 pad_maximum_fusion.3
  329.3 1.3 collective-permute-start.10
  330.5 1.8 convolution_convert_fusion.1
  332.4 0.9 reshape.377
  333.2 4.8 %all-to-all-start.9 = ((bf16[32,4,1536]{2,1,0:T(4,128)(2,1)}), bf16[32,4,1536]{2,1,0:T(4,128)(2,1)S(1)}, u32[]{:S(2)}, u32[]{:S(2)}) async-start(bf16[32,4,1536]{2,1,0:T(4,128)(2,1)} %reshape.377), calls=%async_computation.9 | async-start | bytes 786432 | tf_op jit(solution)/shard_map/all_to_all | solution.py:14
  338.0 1.3 select_select_fusion
  339.3 11.4 %collective-permute-start.9 = (bf16[128,1792]{1,0:T(8,128)(2,1)}, bf16[128,1792]{1,0:T(8,128)(2,1)S(1)}, u32[]{:S(2)}, u32[]{:S(2)}) collective-permute-start(bf16[128,1792]{1,0:T(8,128)(2,1)} %get-tuple-element.41), channel_id=1, source_target_pairs={{0,128},{128,256},{256,384},{384,0},{1,129},{129,257},{257,385},{3... | collective-permute-start | bytes 1376264 | tf_op jit(solution)/shard_map/ppermute | solution.py:23
  350.7 1.9 collective-permute-start.11
  352.6 1.2 select_select_fusion.1
  355.0 11.0 %all-to-all-start.10 = ((bf16[16,24,128]{2,1,0:T(8,128)(2,1)}), bf16[16,24,128]{2,1,0:T(8,128)(2,1)S(1)}, u32[]{:S(2)}, u32[]{:S(2)}) async-start(bf16[16,24,128]{2,1,0:T(8,128)(2,1)} %reshape.378), calls=%async_computation.10 | async-start | bytes 196608 | tf_op jit(solution)/shard_map/all_to_all | solution.py:14
  366.0 4.6 %collective-permute-done.9 = bf16[128,1792]{1,0:T(8,128)(2,1)S(1)} collective-permute-done((bf16[128,1792]{1,0:T(8,128)(2,1)}, bf16[128,1792]{1,0:T(8,128)(2,1)S(1)}, u32[]{:S(2)}, u32[]{:S(2)}) %collective-permute-start.9) | collective-permute-done | bytes 458784 | tf_op jit(solution)/shard_map/ppermute | solution.py:23
  371.2 0.9 select_select_fusion.11
  372.4 1.7 fusion.1
  374.1 0.9 fusion.9
  375.8 1.5 fusion
  377.3 1.3 all-to-all-done.10
  (135 shorter events, 22.4 us)
Async XLA Ops:
  7.2 29.3 %collective-permute-start = (bf16[256,1536]{1,0:T(8,128)(2,1)}, bf16[256,1536]{1,0:T(8,128)(2,1)}, u32[]{:S(2)}, u32[]{:S(2)}) collective-permute-start(bf16[256,1536]{1,0:T(8,128)(2,1)} %bitcast.2), channel_id=1, source_target_pairs={{0,128},{128,256},{256,384},{384,0},{1,129},{129,257},{257,385},{3... | collective-permute-start | bytes 2359304 | tf_op jit(solution)/shard_map/ppermute | solution.py:23
  12.2 40.5 %collective-permute-start.1 = (bf16[1536,256]{1,0:T(8,128)(2,1)}, bf16[1536,256]{1,0:T(8,128)(2,1)}, u32[]{:S(2)}, u32[]{:S(2)}) collective-permute-start(bf16[1536,256]{1,0:T(8,128)(2,1)} %bitcast.3), channel_id=1, source_target_pairs={{0,384},{128,0},{256,128},{384,256},{1,385},{129,1},{257,129},{385... | collective-permute-start | bytes 2359304 | tf_op jit(solution)/shard_map/ppermute | solution.py:23
  18.2 11.2 %copy-start.8 = (f32[4]{0:T(128)}, f32[4]{0:T(128)S(1)}, u32[]{:S(2)}) copy-start(f32[4]{0:T(128)S(1)} %get-tuple-element.35) | copy-start | bytes 52
  18.9 33.8 %all-to-all-start.3 = ((bf16[4,4,1536]{2,1,0:T(4,128)(2,1)}), bf16[4,4,1536]{2,1,0:T(4,128)(2,1)S(1)}, u32[]{:S(2)}, u32[]{:S(2)}) async-start(bf16[4,4,1536]{2,1,0:T(4,128)(2,1)} %fusion.80), calls=%async_computation.3 | async-start | bytes 98304 | tf_op jit(solution)/shard_map/all_to_all | solution.py:14
  52.7 20.2 %all-to-all-start = ((bf16[16,89,128]{2,1,0:T(8,128)(2,1)}), bf16[16,89,128]{2,1,0:T(8,128)(2,1)S(1)}, u32[]{:S(2)}, u32[]{:S(2)}) async-start(bf16[16,89,128]{2,1,0:T(8,128)(2,1)} %bitcast.4), calls=%async_computation | async-start | bytes 786432 | tf_op jit(solution)/shard_map/all_to_all | solution.py:14
  58.8 108.6 %all-gather.7.cloned.1.call-start = ((), (), s32[]{:S(2)}) async-start(), calls=%async_computation.11 | async-start | bytes 1622016 | tf_op jit(solution)/shard_map/all_gather | solution.py:103
  58.8 49.8 %collective-permute-start.2 = (bf16[256,1536]{1,0:T(8,128)(2,1)}, bf16[256,1536]{1,0:T(8,128)(2,1)}, u32[]{:S(2)}, u32[]{:S(2)}) collective-permute-start(bf16[256,1536]{1,0:T(8,128)(2,1)} %bitcast.2), channel_id=1, source_target_pairs={{0,384},{128,0},{256,128},{384,256},{1,385},{129,1},{257,129},{385... | collective-permute-start | bytes 2359304 | tf_op jit(solution)/shard_map/ppermute | solution.py:23
  64.9 43.7 %collective-permute-start.3 = (bf16[256,1536]{1,0:T(8,128)(2,1)}, bf16[256,1536]{1,0:T(8,128)(2,1)}, u32[]{:S(2)}, u32[]{:S(2)}) collective-permute-start(bf16[256,1536]{1,0:T(8,128)(2,1)} %collective-permute-done), channel_id=1, source_target_pairs={{0,128},{128,256},{256,384},{384,0},{1,129},{129,257},{257,385},{3... | collective-permute-start | bytes 2359304 | tf_op jit(solution)/shard_map/ppermute | solution.py:23
  73.9 27.1 %all-to-all-start.1 = ((bf16[32,4,1536]{2,1,0:T(4,128)(2,1)}), bf16[32,4,1536]{2,1,0:T(4,128)(2,1)S(1)}, u32[]{:S(2)}, u32[]{:S(2)}) async-start(bf16[32,4,1536]{2,1,0:T(4,128)(2,1)} %broadcast_in_dim.64), calls=%async_computation.1 | async-start | bytes 786432 | tf_op jit(solution)/shard_map/all_to_all | solution.py:14
  86.8 53.2 %collective-permute-start.5 = (bf16[1536,256]{1,0:T(8,128)(2,1)}, bf16[1536,256]{1,0:T(8,128)(2,1)}, u32[]{:S(2)}, u32[]{:S(2)}) collective-permute-start(bf16[1536,256]{1,0:T(8,128)(2,1)} %bitcast.3), channel_id=1, source_target_pairs={{0,128},{128,256},{256,384},{384,0},{1,129},{129,257},{257,385},{3... | collective-permute-start | bytes 2359304 | tf_op jit(solution)/shard_map/ppermute | solution.py:23
  89.2 50.9 %collective-permute-start.4 = (bf16[1536,256]{1,0:T(8,128)(2,1)}, bf16[1536,256]{1,0:T(8,128)(2,1)}, u32[]{:S(2)}, u32[]{:S(2)}) collective-permute-start(bf16[1536,256]{1,0:T(8,128)(2,1)} %collective-permute-done.1), channel_id=1, source_target_pairs={{0,384},{128,0},{256,128},{384,256},{1,385},{129,1},{257,129},{385... | collective-permute-start | bytes 2359304 | tf_op jit(solution)/shard_map/ppermute | solution.py:23
  142.7 24.6 %all-to-all-start.2 = ((bf16[32,4,1536]{2,1,0:T(4,128)(2,1)}), bf16[32,4,1536]{2,1,0:T(4,128)(2,1)S(1)}, u32[]{:S(2)}, u32[]{:S(2)}) async-start(bf16[32,4,1536]{2,1,0:T(4,128)(2,1)} %reshape.370), calls=%async_computation.2 | async-start | bytes 786432 | tf_op jit(solution)/shard_map/all_to_all | solution.py:14
  155.9 51.2 %copy-start.10 = (f32[4]{0:T(128)}, f32[4]{0:T(128)S(1)}, u32[]{:S(2)}) copy-start(f32[4]{0:T(128)S(1)} %multiply_multiply_fusion.3) | copy-start | bytes 52
  176.1 30.9 %copy-start.11 = (f32[4]{0:T(128)}, f32[4]{0:T(128)S(1)}, u32[]{:S(2)}) copy-start(f32[4]{0:T(128)S(1)} %multiply_bitcast_fusion.2) | copy-start | bytes 52
  177.1 15.8 %all-to-all-start.4 = ((bf16[32,4,1536]{2,1,0:T(4,128)(2,1)}), bf16[32,4,1536]{2,1,0:T(4,128)(2,1)S(1)}, u32[]{:S(2)}, u32[]{:S(2)}) async-start(bf16[32,4,1536]{2,1,0:T(4,128)(2,1)} %broadcast_in_dim.66), calls=%async_computation.4 | async-start | bytes 786432 | tf_op jit(solution)/shard_map/all_to_all | solution.py:14
  207.1 5.8 %copy-start.2 = (bf16[1,1,1,128,256]{4,3,2,1,0:T(8,128)(2,1)S(1)}, bf16[1,1,1,128,256]{4,3,2,1,0:T(8,128)(2,1)}, u32[]{:S(2)}) copy-start(bf16[1,1,1,128,256]{4,3,2,1,0:T(8,128)(2,1)} %param.6) | copy-start | bytes 196612
  207.9 17.1 %all-to-all-start.5 = ((bf16[32,4,1536]{2,1,0:T(4,128)(2,1)}), bf16[32,4,1536]{2,1,0:T(4,128)(2,1)S(1)}, u32[]{:S(2)}, u32[]{:S(2)}) async-start(bf16[32,4,1536]{2,1,0:T(4,128)(2,1)} %reshape.373), calls=%async_computation.5 | async-start | bytes 786432 | tf_op jit(solution)/shard_map/all_to_all | solution.py:14
  233.3 61.6 %copy-start.3 = (bf16[4,1536]{1,0:T(4,128)(2,1)}, bf16[4,1536]{1,0:T(4,128)(2,1)S(1)}, u32[]{:S(2)}) copy-start(bf16[4,1536]{1,0:T(4,128)(2,1)S(1)} %subtract_convert_fusion.2) | copy-start | bytes 36868
  234.1 16.0 %all-to-all-start.6 = ((bf16[32,4,1536]{2,1,0:T(4,128)(2,1)}), bf16[32,4,1536]{2,1,0:T(4,128)(2,1)S(1)}, u32[]{:S(2)}, u32[]{:S(2)}) async-start(bf16[32,4,1536]{2,1,0:T(4,128)(2,1)} %broadcast_in_dim.68), calls=%async_computation.6 | async-start | bytes 786432 | tf_op jit(solution)/shard_map/all_to_all | solution.py:14
  240.3 9.9 %collective-permute-start.6 = (bf16[128,1792]{1,0:T(8,128)(2,1)}, bf16[128,1792]{1,0:T(8,128)(2,1)S(1)}, u32[]{:S(2)}, u32[]{:S(2)}) collective-permute-start(bf16[128,1792]{1,0:T(8,128)(2,1)} %pad_maximum_fusion), channel_id=1, source_target_pairs={{128,384},{129,385},{130,386},{131,387},{132,388},{133,389},{134,3... | collective-permute-start | bytes 1376264 | tf_op jit(solution)/shard_map/ppermute | solution.py:28
  264.8 13.2 %copy-start = (bf16[1,1,1,4,6144]{4,3,2,1,0:T(4,128)(2,1)S(1)}, bf16[1,1,1,4,6144]{4,3,2,1,0:T(4,128)(2,1)}, u32[]{:S(2)}) copy-start(bf16[1,1,1,4,6144]{4,3,2,1,0:T(4,128)(2,1)} %param.5) | copy-start | bytes 147460
  265.6 21.3 %all-to-all-start.7 = ((bf16[32,4,1536]{2,1,0:T(4,128)(2,1)}), bf16[32,4,1536]{2,1,0:T(4,128)(2,1)S(1)}, u32[]{:S(2)}, u32[]{:S(2)}) async-start(bf16[32,4,1536]{2,1,0:T(4,128)(2,1)} %reshape.375), calls=%async_computation.7 | async-start | bytes 786432 | tf_op jit(solution)/shard_map/all_to_all | solution.py:14
  274.5 12.4 %collective-permute-start.7 = (bf16[128,1792]{1,0:T(8,128)(2,1)}, bf16[128,1792]{1,0:T(8,128)(2,1)}, u32[]{:S(2)}, u32[]{:S(2)}) collective-permute-start(bf16[128,1792]{1,0:T(8,128)(2,1)} %pad_maximum_fusion.1), channel_id=1, source_target_pairs={{0,256},{1,257},{2,258},{3,259},{4,260},{5,261},{6,262},{7,263},{8... | collective-permute-start | bytes 1376264 | tf_op jit(solution)/shard_map/ppermute | solution.py:28
  294.9 0.9 copy-start.5
  295.8 20.5 %all-to-all-start.8 = ((bf16[32,4,1536]{2,1,0:T(4,128)(2,1)}), bf16[32,4,1536]{2,1,0:T(4,128)(2,1)S(1)}, u32[]{:S(2)}, u32[]{:S(2)}) async-start(bf16[32,4,1536]{2,1,0:T(4,128)(2,1)} %broadcast_in_dim.70), calls=%async_computation.8 | async-start | bytes 786432 | tf_op jit(solution)/shard_map/all_to_all | solution.py:14
  307.4 9.0 %collective-permute-start.8 = (bf16[128,1792]{1,0:T(8,128)(2,1)}, bf16[128,1792]{1,0:T(8,128)(2,1)}, u32[]{:S(2)}, u32[]{:S(2)}) collective-permute-start(bf16[128,1792]{1,0:T(8,128)(2,1)} %pad_maximum_fusion.2), channel_id=1, source_target_pairs={{384,128},{385,129},{386,130},{387,131},{388,132},{389,133},{390,1... | collective-permute-start | bytes 1376264 | tf_op jit(solution)/shard_map/ppermute | solution.py:28
  329.3 23.4 %collective-permute-start.10 = (bf16[128,1792]{1,0:T(8,128)(2,1)}, bf16[128,1792]{1,0:T(8,128)(2,1)}, u32[]{:S(2)}, u32[]{:S(2)}) collective-permute-start(bf16[128,1792]{1,0:T(8,128)(2,1)} %get-tuple-element.46), channel_id=1, source_target_pairs={{256,0},{257,1},{258,2},{259,3},{260,4},{261,5},{262,6},{263,7},{2... | collective-permute-start | bytes 1376264 | tf_op jit(solution)/shard_map/ppermute | solution.py:28
  333.2 20.5 %all-to-all-start.9 = ((bf16[32,4,1536]{2,1,0:T(4,128)(2,1)}), bf16[32,4,1536]{2,1,0:T(4,128)(2,1)S(1)}, u32[]{:S(2)}, u32[]{:S(2)}) async-start(bf16[32,4,1536]{2,1,0:T(4,128)(2,1)} %reshape.377), calls=%async_computation.9 | async-start | bytes 786432 | tf_op jit(solution)/shard_map/all_to_all | solution.py:14
  339.3 14.7 %copy-start.4 = (bf16[4,1536]{1,0:T(4,128)(2,1)S(1)}, bf16[4,1536]{1,0:T(4,128)(2,1)}, u32[]{:S(2)}) copy-start(bf16[4,1536]{1,0:T(4,128)(2,1)} %copy-done.3) | copy-start | bytes 36868
  339.3 14.7 %copy-start.6 = (bf16[4,1536]{1,0:T(4,128)(2,1)S(1)}, bf16[4,1536]{1,0:T(4,128)(2,1)}, u32[]{:S(2)}) copy-start(bf16[4,1536]{1,0:T(4,128)(2,1)} %copy-done.5) | copy-start | bytes 36868
  339.3 14.7 %copy-start.7 = (bf16[1,4,1536]{2,1,0:T(4,128)(2,1)S(1)}, bf16[1,4,1536]{2,1,0:T(4,128)(2,1)}, u32[]{:S(2)}) copy-start(bf16[1,4,1536]{2,1,0:T(4,128)(2,1)} %fusion.82) | copy-start | bytes 36868
  339.3 31.3 %collective-permute-start.9 = (bf16[128,1792]{1,0:T(8,128)(2,1)}, bf16[128,1792]{1,0:T(8,128)(2,1)S(1)}, u32[]{:S(2)}, u32[]{:S(2)}) collective-permute-start(bf16[128,1792]{1,0:T(8,128)(2,1)} %get-tuple-element.41), channel_id=1, source_target_pairs={{0,128},{128,256},{256,384},{384,0},{1,129},{129,257},{257,385},{3... | collective-permute-start | bytes 1376264 | tf_op jit(solution)/shard_map/ppermute | solution.py:23
  350.7 20.5 %collective-permute-start.11 = (bf16[128,1792]{1,0:T(8,128)(2,1)}, bf16[128,1792]{1,0:T(8,128)(2,1)}, u32[]{:S(2)}, u32[]{:S(2)}) collective-permute-start(bf16[128,1792]{1,0:T(8,128)(2,1)} %get-tuple-element.40), channel_id=1, source_target_pairs={{0,384},{128,0},{256,128},{384,256},{1,385},{129,1},{257,129},{385... | collective-permute-start | bytes 1376264 | tf_op jit(solution)/shard_map/ppermute | solution.py:23
  355.0 23.7 %all-to-all-start.10 = ((bf16[16,24,128]{2,1,0:T(8,128)(2,1)}), bf16[16,24,128]{2,1,0:T(8,128)(2,1)S(1)}, u32[]{:S(2)}, u32[]{:S(2)}) async-start(bf16[16,24,128]{2,1,0:T(8,128)(2,1)} %reshape.378), calls=%async_computation.10 | async-start | bytes 196608 | tf_op jit(solution)/shard_map/all_to_all | solution.py:14
  374.1 1.7 copy-start.13
  375.8 3.2 copy-start.1
  375.8 3.8 copy-start.9
  375.8 3.8 copy-start.12
Sparse Core Ops, SparseCore 0:
  65.0 83.1 all-gather.6
